TPU v7x, 128 devices: a whole 4x4x4 slice. The times are simulated.
128 devices in a mesh: dp: 8 (over y, z_hi), tensor: 16 (over z_lo, x, core).
Axes of the slice: x: 4, y: 4, z: 4 (z_hi: 2, z_lo: 2; z = z_hi * 2 + z_lo), core: 2. Of those that a mesh axis runs over, the one named last changes fastest.
Arguments:
- inputs: bfloat16 [12288, 8192], P('dp', 'tensor'), may hold values from -6 to 6
- grad_out: bfloat16 [2, 12288, 22016], P(None, 'dp', 'tensor'), may hold values from -0.0068359375 to 0.0068359375
- basis: bfloat16 [2, 8192, 128], replicated, may hold values from -0.5 to 0.5
- first_moment: float32 [2, 128, 16, 1376], P(None, None, 'tensor', 'dp'), may hold values from -4 to 4
- second_moment: float32 [2, 128, 16, 1376], P(None, None, 'tensor', 'dp'), may hold values from 0.002 to 0.05
Outputs:
- update: bfloat16 [2, 8192, 22016], P(None, 'dp', 'tensor')
- new_first: float32 [2, 128, 16, 1376], P(None, None, 'tensor', 'dp')
- new_second: float32 [2, 128, 16, 1376], P(None, None, 'tensor', 'dp')
All inputs are finite; a program needn't handle non-finite values.
Results may differ from a plain program's by a relative error of at most 0.005.
Values may be sent and summed in bfloat16 or wider, within the bound.
No kernel may reach another device: no remote copies, remote signals or barrier semaphores. Data moves between devices by JAX's collectives and lax.ppermute only.
A program may use at most 64 MiB of HBM per device.

v0:
```python
import jax
import jax.numpy as jnp
from jax import lax
from jax.sharding import PartitionSpec as P

STEP = 10


beta_one = 0.9
beta_two = 0.999
epsilon = 1e-08


def adam_step(rank_grad, first_moment, second_moment):
    new_first = beta_one * first_moment + (1.0 - beta_one) * rank_grad
    new_second = beta_two * second_moment + (1.0 - beta_two) * rank_grad * rank_grad
    corr_one = 1.0 - beta_one**STEP
    corr_two = 1.0 - beta_two**STEP
    normalized = (new_first / corr_one / (jnp.sqrt(new_second / corr_two) + epsilon)).astype(
        jnp.bfloat16
    )
    return (normalized, new_first, new_second)


def body(inputs, grad_out, basis, first_moment, second_moment):
    tokens = inputs.shape[0]
    feat_rows = inputs.shape[1]
    rank = basis.shape[2]
    tensor_pos = lax.axis_index("tensor")
    batch_pos = lax.axis_index("dp")
    weight_rows = basis.shape[1] // lax.axis_size("dp")
    feat_basis = lax.dynamic_slice_in_dim(basis, tensor_pos * feat_rows, feat_rows, 1)
    row_basis = lax.dynamic_slice_in_dim(basis, batch_pos * weight_rows, weight_rows, 1)
    partial_proj = jnp.einsum("td,gdk->tgk", inputs, feat_basis, preferred_element_type=jnp.float32)
    summed = lax.psum(partial_proj.reshape(tokens, 2 * rank), "tensor")
    projected = summed.astype(jnp.bfloat16).reshape(tokens, 2, rank)
    rank_part = jnp.einsum("tgk,gtc->gkc", projected, grad_out, preferred_element_type=jnp.float32)
    block_width = grad_out.shape[2]
    share_width = first_moment.shape[3]
    rank_grad = lax.psum(rank_part, "dp")
    first_block, second_block = (
        lax.all_gather(first_moment, "dp", axis=3, tiled=True),
        lax.all_gather(second_moment, "dp", axis=3, tiled=True),
    )
    normalized, new_first, new_second = adam_step(
        rank_grad.reshape(first_block.shape), first_block, second_block
    )
    new_first = lax.dynamic_slice_in_dim(new_first, batch_pos * share_width, share_width, 3)
    new_second = lax.dynamic_slice_in_dim(new_second, batch_pos * share_width, share_width, 3)
    flat = normalized.reshape(2, rank, block_width)
    update = jnp.einsum("gdk,gkc->gdc", row_basis, flat, preferred_element_type=jnp.float32).astype(
        jnp.bfloat16
    )
    return (update, new_first, new_second)


def solution(mesh):
    in_specs = (
        P("dp", "tensor"),
        P(None, "dp", "tensor"),
        P(),
        P(None, None, "tensor", "dp"),
        P(None, None, "tensor", "dp"),
    )
    out_specs = (
        P(None, "dp", "tensor"),
        P(None, None, "tensor", "dp"),
        P(None, None, "tensor", "dp"),
    )
    return jax.shard_map(body, mesh=mesh, in_specs=in_specs, out_specs=out_specs, check_vma=False)
```

profile of v0, /device:TPU:0, one launch (start us, length us, event | category | flops | bytes accessed | tf_op | source)
XLA Modules:
  0.0 300.8 jit_solution(9845460261671312267)
XLA Ops:
  7.2 0.0 copy-start
  7.2 0.0 all-reduce.3.cloned.1.call-start
  7.2 1.3 copy-done
  8.6 2.7 fusion
  11.3 68.8 %all-reduce.4 = bf16[1536,256]{0,1:T(8,128)(2,1)S(1)} all-reduce(f32[1536,256]{0,1:T(8,128)} %bitcast.19), channel_id=1, replica_groups=mesh['dp'=8,'tensor'=16] {'tensor'}, use_global_device_ids=true, to_apply=%region_0.0 | all-reduce | flops 393216 | bytes 2359296 | tf_op jit(solution)/shard_map/psum | solution.py:35
  80.1 6.8 %fusion.14 = f32[2,128,1376]{1,2,0:T(8,128)} fusion(bf16[1536,2,128]{0,2,1:T(8,128)(2,1)S(1)} %bitcast.18, bf16[2,1536,1376]{1,2,0:T(8,128)(2,1)} %param.6), kind=kOutput, calls=%fused_computation.22 | convolution fusion | flops 1082130432 | bytes 10649600 | tf_op jit(solution)/shard_map/tgk,gtc->gkc/dot_general | solution.py:37
  86.9 0.0 copy-start.1
  86.9 0.0 copy-start.2
  86.9 0.0 all-reduce.3.cloned.1.call-update
  87.0 0.0 all-gather.3.cloned.1.call-start
  87.0 0.8 copy-done.1
  87.9 0.8 copy.19
  88.6 0.0 all-gather.3.cloned.1.call-update
  88.6 0.0 all-gather.5.cloned.1.call-start
  88.7 0.0 copy-done.2
  88.7 0.8 copy.23
  89.5 0.0 all-gather.5.cloned.1.call-update
  89.5 91.3 %all-reduce.3.cloned.1.call-done = f32[2,128,1376]{1,2,0:T(8,128)} async-done(((f32[2,128,1376]{1,2,0:T(8,128)}), f32[2,128,1376]{1,2,0:T(8,128)}) %all-reduce.3.cloned.1.call-update) | async-done | bytes 1409040 | tf_op jit(solution)/shard_map/psum | solution.py:40
  180.8 52.1 %all-gather.3.cloned.1.call-done = f32[2,128,1,1376]{1,0,2,3:T(2,128)} async-done(((f32[2,128,1,172]{1,0,2,3:T(2,128)}), f32[2,128,1,1376]{1,0,2,3:T(2,128)}) %all-gather.3.cloned.1.call-update) | async-done | bytes 1409040 | tf_op jit(solution)/shard_map/all_gather | solution.py:42
  233.0 51.6 %all-gather.5.cloned.1.call-done = f32[2,128,1,1376]{1,0,2,3:T(2,128)} async-done(((f32[2,128,1,172]{1,0,2,3:T(2,128)}), f32[2,128,1,1376]{1,0,2,3:T(2,128)}) %all-gather.5.cloned.1.call-update) | async-done | bytes 1409040 | tf_op jit(solution)/shard_map/all_gather | solution.py:43
  284.6 2.7 bitcast_add_fusion
  287.3 0.9 copy.26
  288.2 0.9 copy.25
  289.0 5.2 %convolution_convert_fusion = bf16[2,1024,1376]{1,2,0:T(8,128)(2,1)} fusion(f32[2,128,1,1376]{1,3,0,2:T(8,128)S(1)} %get-tuple-element.13, f32[2,128,1,1376]{1,3,0,2:T(8,128)S(1)} %get-tuple-element.12, bf16[2,8192,128]{2,1,0:T(8,128)(2,1)} %param.7, s32[]{:T(128)S(6)} %select_n.10), kind=kOutput, calls=%fused_computation | convolution fusion | flops 725999616 | bytes 8978436 | tf_op jit(solution)/shard_map/gdk,gkc->gdc/dot_general | solution.py:51
  (1 shorter events, 0.0 us)
Async XLA Ops:
  7.2 1.4 copy-start
  7.2 173.7 %all-reduce.3.cloned.1.call-start = ((), (), s32[]{:S(2)}) async-start(), calls=%async_computation.1 | async-start | bytes 2818048 | tf_op jit(solution)/shard_map/psum | solution.py:40
  86.9 0.9 copy-start.1
  86.9 1.8 copy-start.2
  87.0 146.0 %all-gather.3.cloned.1.call-start = ((), (), s32[]{:S(2)}) async-start(), calls=%async_computation | async-start | bytes 1585152 | tf_op jit(solution)/shard_map/all_gather | solution.py:42
  88.6 196.0 %all-gather.5.cloned.1.call-start = ((), (), s32[]{:S(2)}) async-start(), calls=%async_computation.2 | async-start | bytes 1585152 | tf_op jit(solution)/shard_map/all_gather | solution.py:43
Sparse Core Ops, SparseCore 0:
  87.1 93.7 all-reduce.2
  183.8 49.1 all-gather.2
  235.9 48.6 all-gather.4
where the time goes:
time: 301 us
  waiting for transfers between devices  195 us (65%)
  blocking collectives  68.8 us (23%)
  matrix products  14.8 us (5%)
  between operations  13.8 us (5%)
  local copies, waits for them, and re-layouts  5.47 us (2%)
    psum x1, waiting for transfers between devices, body(): rank_grad = lax.psum(rank_part, 'dp')  91.3 us
    psum x1, blocking collectives, body(): summed = lax.psum(partial_proj.reshape(tokens, 2 * rank), 'tensor')  68.8 us
    all_gather x1, waiting for transfers between devices, body(): lax.all_gather(first_moment, 'dp', axis=3, tiled=True)  52.1 us
    all_gather x1, waiting for transfers between devices, body(): lax.all_gather(second_moment, 'dp', axis=3, tiled=True)  51.6 us
    dot_general x1, matrix products, body(): jnp.einsum('tgk,gtc->gkc', projected, grad_out, preferred_element_type=jn...  6.84 us
  transfers between devices with their start and end apart: 3, of which 3 were waited for; matrix products, arithmetic and copies ran while one was open for 1% of the time, Pallas kernels for 0%

commit v1 on v0

v1 whole, which is shorter than its diff:
```python
import functools

import jax
import jax.numpy as jnp
from jax import lax
from jax.experimental import pallas as pl
from jax.experimental.pallas import tpu as pltpu
from jax.sharding import PartitionSpec as P

STEP = 10

beta_one = 0.9
beta_two = 0.999
epsilon = 1e-08
corr_one = 1.0 - beta_one**STEP
corr_two = 1.0 - beta_two**STEP

NX, NY = 4, 4
CHAINS = ((0, 1),)

F32, BF16 = jnp.float32, jnp.bfloat16
NT = (((1,), (1,)), ((), ()))


def to_core(v):
    return lax.ppermute(v, "tensor", [(i, i ^ 1) for i in range(16)])


def to_x(v, k):
    pairs = [(i, (i & 9) | ((((i >> 1) + k) & 3) << 1)) for i in range(16)]
    return lax.ppermute(v, "tensor", pairs)


def to_zlo(v):
    return lax.ppermute(v, "tensor", [(i, i ^ 8) for i in range(16)])


def to_y(v, k):
    return lax.ppermute(v, "dp", [(i, (i & 1) | ((((i >> 1) + k) & 3) << 1)) for i in range(8)])


def to_zhi(v):
    return lax.ppermute(v, "dp", [(i, i ^ 1) for i in range(8)])


def params(mib=24):
    return pltpu.CompilerParams(vmem_limit_bytes=mib * 2**20)


def project_kernel(pos, inputs_ref, *refs):
    basis_refs, send_ref, own_ref = refs[:-2], refs[-2], refs[-1]
    step = pl.program_id(0)
    product = [
        jnp.dot(inputs_ref[...], ref[0], preferred_element_type=F32) for ref in basis_refs
    ]
    product = jnp.concatenate(product, axis=1) if len(product) > 1 else product[0]

    @pl.when(step < NX)
    def _():
        send_ref[...] = product.astype(BF16)

    @pl.when(step >= NX)
    def _():
        own_ref[...] = product


def project(pos, inputs, basis, chain):
    tokens, feat = inputs.shape
    rank = basis.shape[2]
    piece = tokens // (2 * NX)
    width = rank * len(chain)

    def rows(s, pos):
        core = jnp.where(s < NX, 1 - pos[0], pos[0])
        return core * NX + lax.rem(pos[1] + lax.rem(s, NX), NX)

    return pl.pallas_call(
        project_kernel,
        grid_spec=pltpu.PrefetchScalarGridSpec(
            num_scalar_prefetch=1,
            grid=(2 * NX,),
            in_specs=[pl.BlockSpec((piece, feat), lambda s, pos: (rows(s, pos), 0))]
            + [
                pl.BlockSpec((1, feat, rank), lambda s, pos, g=g: (g, 0, 0)) for g in chain
            ],
            out_specs=[
                pl.BlockSpec((piece, width), lambda s, pos: (jnp.minimum(s, NX - 1), 0)),
                pl.BlockSpec((piece, width), lambda s, pos: (jnp.maximum(s - NX, 0), 0)),
            ],
        ),
        out_shape=[
            jax.ShapeDtypeStruct((NX * piece, width), BF16),
            jax.ShapeDtypeStruct((NX * piece, width), F32),
        ],
        compiler_params=params(),
        name="project",
    )(pos, inputs, *([basis] * len(chain)))


BLOCK = 352


def rank_kernel(chain, steps, pos, mine_ref, theirs_ref, grad_ref, own_ref, *refs):
    outs, proj, total = refs[:-2], refs[-2], refs[-1]
    g, step = pl.program_id(0), pl.program_id(1)
    piece = mine_ref.shape[0] // NX

    @pl.when((g == 0) & (step == 0))
    def _():
        for k in range(NX):
            x = lax.rem(pos[1] - k + NX, NX)
            for ref, core in ((mine_ref, pos[0]), (theirs_ref, 1 - pos[0])):
                at = pl.multiple_of((core * NX + x) * piece, piece)
                for h in range(len(chain)):
                    proj[h, pl.ds(at, piece), :] = ref[
                        k * piece : (k + 1) * piece, h * 128 : (h + 1) * 128
                    ]

    total[pl.ds(pl.multiple_of(step * BLOCK, BLOCK), BLOCK), :] = jnp.dot(
        grad_ref[0], proj[g], preferred_element_type=F32
    )

    @pl.when(step == steps - 1)
    def _():
        share = own_ref.shape[1]
        for k in range(NY):
            y = lax.rem(pos[2] + k, NY)
            part = total[pl.ds(pl.multiple_of(y * share, 8), share), :]
            if k == 0:
                own_ref[g] = part
            else:
                outs[k - 1][g] = part.astype(BF16)


def rank_grad(pos, mine, theirs, grad_t, chain):
    n = len(chain)
    cols, tokens = grad_t.shape[1:]
    rank = mine.shape[1] // n
    share = cols // NY
    steps = pl.cdiv(cols, BLOCK)
    whole = lambda g, s, pos: (0, 0, 0)
    return pl.pallas_call(
        functools.partial(rank_kernel, chain, steps),
        grid_spec=pltpu.PrefetchScalarGridSpec(
            num_scalar_prefetch=1,
            grid=(n, steps),
            in_specs=[
                pl.BlockSpec(mine.shape, lambda g, s, pos: (0, 0)),
                pl.BlockSpec(theirs.shape, lambda g, s, pos: (0, 0)),
                pl.BlockSpec((1, BLOCK, tokens), lambda g, s, pos: (g + chain[0], s, 0)),
            ],
            out_specs=[pl.BlockSpec((n, share, rank), whole)] * NY,
            scratch_shapes=[
                pltpu.VMEM((n, tokens, rank), BF16),
                pltpu.VMEM((steps * BLOCK, rank), F32),
            ],
        ),
        out_shape=[jax.ShapeDtypeStruct((n, share, rank), F32)]
        + [jax.ShapeDtypeStruct((n, share, rank), BF16)] * (NY - 1),
        compiler_params=params(),
        name="rank_grad",
    )(pos, mine, theirs, grad_t)


def adam_kernel(
    chain, pos, own_ref, got_ref, first_ref, second_ref, far_first_ref, far_second_ref,
    norm_ref, new_first_ref, new_second_ref,
):
    low = pos[3] == 0
    half = own_ref.shape[1] // 2
    for h, g in enumerate(chain):
        rows = slice(g * half, (g + 1) * half)
        grad = own_ref[h] + got_ref[h].astype(F32)

        def both(near, far):
            near, far = near[rows, :], far[rows, :]
            return jnp.concatenate(
                [jnp.where(low, near, far), jnp.where(low, far, near)], axis=0
            )

        new_first = beta_one * both(first_ref, far_first_ref) + (1.0 - beta_one) * grad
        new_second = beta_two * both(second_ref, far_second_ref) + (1.0 - beta_two) * grad * grad
        norm_ref[h] = (
            new_first / corr_one / (jnp.sqrt(new_second / corr_two) + epsilon)
        ).astype(BF16)
        to = slice(h * half, (h + 1) * half)
        new_first_ref[to, :] = jnp.where(low, new_first[:half], new_first[half:])
        new_second_ref[to, :] = jnp.where(low, new_second[:half], new_second[half:])


def adam(pos, own, got, first, second, far_first, far_second, chain):
    n, share, rank = own.shape
    vmem = pl.BlockSpec(memory_space=pltpu.VMEM)
    return pl.pallas_call(
        functools.partial(adam_kernel, chain),
        in_specs=[pl.BlockSpec(memory_space=pltpu.SMEM)] + [vmem] * 6,
        out_specs=[vmem] * 3,
        out_shape=[jax.ShapeDtypeStruct((n, share, rank), BF16)]
        + [jax.ShapeDtypeStruct((n * share // 2, rank), F32)] * 2,
        compiler_params=params(),
        name="adam",
    )(pos, own, got, first, second, far_first, far_second)


def update_kernel(n, pos, *refs):
    pieces, basis_ref, out_ref, wide, norm = refs[: NY * n], *refs[NY * n :]
    g, step = pl.program_id(0), pl.program_id(1)
    share = pieces[0].shape[1]
    rows = out_ref.shape[1]

    for h in range(n):

        @pl.when((g == h) & (step == 0))
        def _():
            for k in range(NY):
                y = lax.rem(pos[2] - k + NY, NY)
                at = pl.multiple_of(y * share, 8)
                wide[pl.ds(at, share), :] = pieces[h * NY + k][0].astype(F32)
            norm[...] = wide[...].astype(BF16)

    at = pl.multiple_of(step * rows, rows)
    out_ref[0] = lax.dot_general(
        norm[pl.ds(at, rows), :], basis_ref[0], NT, preferred_element_type=F32
    ).astype(BF16)


def update(pos, pieces, basis, cols, weight_rows):
    n = len(pieces)
    flat = [p for per_g in pieces for p in per_g]
    share, rank = flat[0][0].shape[1:]
    rows = cols // 2
    return pl.pallas_call(
        functools.partial(update_kernel, n),
        grid_spec=pltpu.PrefetchScalarGridSpec(
            num_scalar_prefetch=1,
            grid=(n, cols // rows),
            in_specs=[
                pl.BlockSpec((1, share, rank), lambda g, s, pos, h=h: (h, 0, 0)) for _, h in flat
            ]
            + [pl.BlockSpec((1, weight_rows, rank), lambda g, s, pos: (g, 0, 0))],
            out_specs=pl.BlockSpec((1, rows, weight_rows), lambda g, s, pos: (g, s, 0)),
            scratch_shapes=[pltpu.VMEM((cols, rank), F32), pltpu.VMEM((cols, rank), BF16)],
        ),
        out_shape=jax.ShapeDtypeStruct((n, cols, weight_rows), BF16),
        compiler_params=params(),
        name="update",
    )(pos, *[a for a, _ in flat], basis)


def body(inputs, grad_out, basis, first_moment, second_moment):
    t, d = lax.axis_index("tensor"), lax.axis_index("dp")
    pos = jnp.stack([t & 1, (t >> 1) & 3, d >> 1, d & 1]).astype(jnp.int32)
    feat_rows, weight_rows = inputs.shape[1], basis.shape[1] // lax.axis_size("dp")
    feat_basis = lax.dynamic_slice_in_dim(basis, t * feat_rows, feat_rows, 1)
    row_basis = lax.dynamic_slice_in_dim(basis, d * weight_rows, weight_rows, 1)
    piece = inputs.shape[0] // (2 * NX)
    grad_t = jnp.transpose(grad_out, (0, 2, 1))
    cols = grad_t.shape[1]
    n_g, rank = first_moment.shape[:2]
    flat = lambda m: jnp.transpose(m, (0, 3, 2, 1)).reshape(-1, rank)
    first, second = flat(first_moment), flat(second_moment)
    far_first, far_second = to_zhi(first), to_zhi(second)

    norms, firsts, seconds = [], [], []
    for chain in CHAINS:
        send, own = project(pos, inputs, feat_basis, chain)
        got = to_core(send)
        part = lambda v, k: v[k * piece : (k + 1) * piece].astype(F32)
        sums = [part(own, k) + part(got, k) for k in range(NX)]
        total = sums[0]
        for k in range(1, NX):
            total = total + to_x(sums[k].astype(BF16), k).astype(F32)
        total = (total + to_zlo(total.astype(BF16)).astype(F32)).astype(BF16)
        mine = jnp.concatenate([total] + [to_x(total, k) for k in range(1, NX)], axis=0)
        theirs = to_core(mine)

        own, *others = rank_grad(pos, mine, theirs, grad_t, chain)
        for k in range(1, NY):
            own = own + to_y(others[k - 1], k).astype(F32)
        got = to_zhi(own.astype(BF16))
        norm, new_first, new_second = adam(
            pos, own, got, first, second, far_first, far_second, chain
        )
        gathered = [norm] + [to_y(norm, k) for k in range(1, NY)]
        norms += [[(v, h) for v in gathered] for h in range(len(chain))]
        firsts.append(new_first)
        seconds.append(new_second)

    out = jnp.transpose(update(pos, norms, row_basis, cols, weight_rows), (0, 2, 1))

    def shaped(parts):
        m = jnp.concatenate(parts, axis=0) if len(parts) > 1 else parts[0]
        return jnp.transpose(m.reshape(n_g, -1, 1, rank), (0, 3, 2, 1))

    return out, shaped(firsts), shaped(seconds)


def solution(mesh):
    in_specs = (
        P("dp", "tensor"),
        P(None, "dp", "tensor"),
        P(),
        P(None, None, "tensor", "dp"),
        P(None, None, "tensor", "dp"),
    )
    out_specs = (
        P(None, "dp", "tensor"),
        P(None, None, "tensor", "dp"),
        P(None, None, "tensor", "dp"),
    )
    return jax.shard_map(body, mesh=mesh, in_specs=in_specs, out_specs=out_specs, check_vma=False)
```

time: 301 us -> 81.1 us (0.27)
  waiting for transfers between devices: 195 us -> 29.9 us
  blocking collectives: 68.8 us -> 0 us
  starting transfers between devices: 0.12 us -> 28.1 us
  matrix products: 14.8 us -> 0 us
  between operations: 13.8 us -> 0.73 us
  Pallas kernels: 0 us -> 12.6 us
  local copies, waits for them, and re-layouts: 5.47 us -> 8.6 us
    all_gather x2 -> x0, waiting for transfers between devices: 104 us -> none  [the longest x1 52.1 us: body(): lax.all_gather(first_moment, 'dp', axis=3, tiled=True)]
    psum x1 -> x0, waiting for transfers between devices: 91.3 us -> none  [body(): rank_grad = lax.psum(rank_part, 'dp')]
    psum x1 -> x0, blocking collectives: 68.8 us -> none  [body(): summed = lax.psum(partial_proj.reshape(tokens, 2 * rank), 'tensor')]
    ppermute x0 -> x18, waiting for transfers between devices: none -> 29.9 us  [the longest x6 9.88 us: to_x(): return lax.ppermute(v, 'tensor', pairs)]
    ppermute x0 -> x18, starting transfers between devices: none -> 28.1 us  [the longest x6 9.33 us: to_y(): lax.ppermute(v, 'dp', [(i, i & 1 | ((i >> 1) + k & 3) << 1) for i in rang...]
    dot_general x3 -> x0, matrix products: 14.8 us -> none  [the longest x1 6.84 us: body(): jnp.einsum('tgk,gtc->gkc', projected, grad_out, preferred_element_type=jn...]
    pallas_call x0 -> x4, Pallas kernels: none -> 12.6 us  [the longest x1 4.56 us: update(): pl.pallas_call(functools.partial(update_kernel, n), grid_spec=pltpu.Prefe...]
  transfers between devices with their start and end apart: 3 -> 18, of which waited for: 3 -> 15; matrix products, arithmetic and copies ran while one was open for 1% -> 4% of each run, Pallas kernels for 0% -> 0%
where the time goes in v1:
time: 81.1 us; the launch traced here: 80.3 us
  waiting for transfers between devices  29.9 us (37%)
  starting transfers between devices  28.1 us (35%)
  Pallas kernels  12.6 us (16%)
  local copies, waits for them, and re-layouts  8.6 us (11%)
    ppermute x6, waiting for transfers between devices, to_x(): return lax.ppermute(v, 'tensor', pairs)  9.88 us
    ppermute x6, waiting for transfers between devices, to_y(): lax.ppermute(v, 'dp', [(i, i & 1 | ((i >> 1) + k & 3) << 1) for i in rang...  9.55 us
    ppermute x6, starting transfers between devices, to_y(): lax.ppermute(v, 'dp', [(i, i & 1 | ((i >> 1) + k & 3) << 1) for i in rang...  9.33 us
    ppermute x6, starting transfers between devices, to_x(): return lax.ppermute(v, 'tensor', pairs)  8.6 us
    ppermute x3, starting transfers between devices, to_zhi(): return lax.ppermute(v, 'dp', [(i, i ^ 1) for i in range(8)])  7.92 us
    unnamed x10, local copies, waits for them, and re-layouts  6.52 us
    pallas_call x1, Pallas kernels, update(): pl.pallas_call(functools.partial(update_kernel, n), grid_spec=pltpu.Prefe...  4.56 us
    pallas_call x1, Pallas kernels, rank_grad(): pl.pallas_call(functools.partial(rank_kernel, chain, steps), grid_spec=pl...  4.48 us
  transfers between devices with their start and end apart: 18, of which 15 were waited for; matrix products, arithmetic and copies ran while one was open for 4% of the time, Pallas kernels for 0%

profile of v1, /device:TPU:0, one launch (start us, length us, event | category | flops | bytes accessed | tf_op | source)
XLA Modules:
  0.0 80.3 jit_solution(18341935945673378672)
XLA Ops:
  0.6 1.0 %constant_dynamic-slice_fusion.1.refs_0_.refs_1_ = bf16[2,512,128]{2,1,0:T(8,128)(2,1)S(1)} fusion(bf16[2,8192,128]{2,1,0:T(8,128)(2,1)} %param.7, s32[]{:T(128)S(6)} %select_n.6), kind=kLoop, calls=%fused_computation.9 | loop fusion | bytes 524292 | tf_op jit(solution)/shard_map/dynamic_slice | solution.py:254
  1.7 1.4 %copy-done.1 = bf16[1536,512]{1,0:T(8,128)(2,1)S(1)} copy-done((bf16[1536,512]{1,0:T(8,128)(2,1)S(1)}, bf16[1536,512]{1,0:T(8,128)(2,1)}, u32[]{:S(2)}) %copy-start.1) | copy-done | bytes 1572888
  3.1 2.7 %project.1 = (bf16[768,256]{1,0:T(8,128)(2,1)S(1)}, f32[768,256]{1,0:T(8,128)S(1)}) custom-call(s32[4]{0:T(128)S(1)} %pad_add_fusion.pos, bf16[1536,512]{1,0:T(8,128)(2,1)S(1)} %copy-done.1, bf16[2,512,128]{2,1,0:T(8,128)(2,1)S(1)} %constant_dynamic-slice_fusion.1.refs_0_.refs_1_, bf16[2,512,128]{2,1,0:T(8,128)(2,1)S(1)} %constant_dynamic-slice_fusion.1.refs_0_.refs_1_), custom_call_target="tpu_custom_call" | custom-call | tf_op jit(solution)/shard_map/project/pallas_call | solution.py:77
  5.9 1.7 %collective-permute-done = bf16[768,256]{1,0:T(8,128)(2,1)S(1)} collective-permute-done((bf16[768,256]{1,0:T(8,128)(2,1)S(1)}, bf16[768,256]{1,0:T(8,128)(2,1)S(1)}, u32[]{:S(2)}, u32[]{:S(2)}) %collective-permute-start) | collective-permute-done | bytes 393248 | tf_op jit(solution)/shard_map/ppermute | solution.py:26
  7.7 1.6 %collective-permute-start.1 = (bf16[192,256]{1,0:T(8,128)(2,1)S(1)}, bf16[192,256]{1,0:T(8,128)(2,1)S(1)}, u32[]{:S(2)}, u32[]{:S(2)}) collective-permute-start(bf16[192,256]{1,0:T(8,128)(2,1)S(1)} %get-tuple-element.26), channel_id=1, source_target_pairs={{0,2},{1,3},{2,4},{3,5},{4,6},{5,7},{6,0},{7,1},{8,10},{9,11},{10,... | collective-permute-start | bytes 294920 | tf_op jit(solution)/shard_map/ppermute | solution.py:31
  9.3 1.7 %collective-permute-start.3 = (bf16[192,256]{1,0:T(8,128)(2,1)S(1)}, bf16[192,256]{1,0:T(8,128)(2,1)S(1)}, u32[]{:S(2)}, u32[]{:S(2)}) collective-permute-start(bf16[192,256]{1,0:T(8,128)(2,1)S(1)} %get-tuple-element.27), channel_id=1, source_target_pairs={{0,6},{1,7},{2,0},{3,1},{4,2},{5,3},{6,4},{7,5},{8,14},{9,15},{10,... | collective-permute-start | bytes 294920 | tf_op jit(solution)/shard_map/ppermute | solution.py:31
  11.0 1.9 %collective-permute-start.2 = (bf16[192,256]{1,0:T(8,128)(2,1)S(1)}, bf16[192,256]{1,0:T(8,128)(2,1)S(1)}, u32[]{:S(2)}, u32[]{:S(2)}) collective-permute-start(bf16[192,256]{1,0:T(8,128)(2,1)S(1)} %get-tuple-element.28), channel_id=1, source_target_pairs={{0,4},{1,5},{2,6},{3,7},{4,0},{5,1},{6,2},{7,3},{8,12},{9,13},{10,... | collective-permute-start | bytes 294920 | tf_op jit(solution)/shard_map/ppermute | solution.py:31
  14.3 2.8 %collective-permute-done.2 = bf16[192,256]{1,0:T(8,128)(2,1)S(1)} collective-permute-done((bf16[192,256]{1,0:T(8,128)(2,1)S(1)}, bf16[192,256]{1,0:T(8,128)(2,1)S(1)}, u32[]{:S(2)}, u32[]{:S(2)}) %collective-permute-start.2) | collective-permute-done | bytes 98336 | tf_op jit(solution)/shard_map/ppermute | solution.py:31
  17.2 2.1 %collective-permute-start.4 = (bf16[192,256]{1,0:T(8,128)(2,1)S(1)}, bf16[192,256]{1,0:T(8,128)(2,1)S(1)}, u32[]{:S(2)}, u32[]{:S(2)}) collective-permute-start(bf16[192,256]{1,0:T(8,128)(2,1)S(1)} %fusion), channel_id=1, source_target_pairs={{0,8},{1,9},{2,10},{3,11},{4,12},{5,13},{6,14},{7,15},{8,0},{9,1},... | collective-permute-start | bytes 294920 | tf_op jit(solution)/shard_map/ppermute | solution.py:35
  19.3 2.6 %collective-permute-done.4 = bf16[192,256]{1,0:T(8,128)(2,1)S(1)} collective-permute-done((bf16[192,256]{1,0:T(8,128)(2,1)S(1)}, bf16[192,256]{1,0:T(8,128)(2,1)S(1)}, u32[]{:S(2)}, u32[]{:S(2)}) %collective-permute-start.4) | collective-permute-done | bytes 98336 | tf_op jit(solution)/shard_map/ppermute | solution.py:35
  22.0 1.9 %collective-permute-start.7 = (bf16[192,256]{1,0:T(8,128)(2,1)S(1)}, bf16[192,256]{1,0:T(8,128)(2,1)S(1)}, u32[]{:S(2)}, u32[]{:S(2)}) collective-permute-start(bf16[192,256]{1,0:T(8,128)(2,1)S(1)} %add_convert_fusion), channel_id=1, source_target_pairs={{0,6},{1,7},{2,0},{3,1},{4,2},{5,3},{6,4},{7,5},{8,14},{9,15},{10,... | collective-permute-start | bytes 294920 | tf_op jit(solution)/shard_map/ppermute | solution.py:31
  23.8 1.3 %collective-permute-start.6 = (bf16[192,256]{1,0:T(8,128)(2,1)S(1)}, bf16[192,256]{1,0:T(8,128)(2,1)S(1)}, u32[]{:S(2)}, u32[]{:S(2)}) collective-permute-start(bf16[192,256]{1,0:T(8,128)(2,1)S(1)} %add_convert_fusion), channel_id=1, source_target_pairs={{0,4},{1,5},{2,6},{3,7},{4,0},{5,1},{6,2},{7,3},{8,12},{9,13},{10,... | collective-permute-start | bytes 294920 | tf_op jit(solution)/shard_map/ppermute | solution.py:31
  25.3 1.3 %collective-permute-done.7 = bf16[192,256]{1,0:T(8,128)(2,1)S(1)} collective-permute-done((bf16[192,256]{1,0:T(8,128)(2,1)S(1)}, bf16[192,256]{1,0:T(8,128)(2,1)S(1)}, u32[]{:S(2)}, u32[]{:S(2)}) %collective-permute-start.7) | collective-permute-done | bytes 98336 | tf_op jit(solution)/shard_map/ppermute | solution.py:31
  26.6 3.3 %collective-permute-done.6 = bf16[192,256]{1,0:T(8,128)(2,1)S(1)} collective-permute-done((bf16[192,256]{1,0:T(8,128)(2,1)S(1)}, bf16[192,256]{1,0:T(8,128)(2,1)S(1)}, u32[]{:S(2)}, u32[]{:S(2)}) %collective-permute-start.6) | collective-permute-done | bytes 98336 | tf_op jit(solution)/shard_map/ppermute | solution.py:31
  30.0 1.1 %collective-permute-done.5 = bf16[192,256]{1,0:T(8,128)(2,1)S(1)} collective-permute-done((bf16[192,256]{1,0:T(8,128)(2,1)S(1)}, bf16[192,256]{1,0:T(8,128)(2,1)S(1)}, u32[]{:S(2)}, u32[]{:S(2)}) %collective-permute-start.5) | collective-permute-done | bytes 98336 | tf_op jit(solution)/shard_map/ppermute | solution.py:31
  31.1 1.7 %collective-permute-done.8.theirs_ref = bf16[768,256]{1,0:T(8,128)(2,1)S(1)} collective-permute-done((bf16[768,256]{1,0:T(8,128)(2,1)S(1)}, bf16[768,256]{1,0:T(8,128)(2,1)S(1)}, u32[]{:S(2)}, u32[]{:S(2)}) %collective-permute-start.8) | collective-permute-done | bytes 393248 | tf_op jit(solution)/shard_map/ppermute | solution.py:26
  32.8 3.4 %copy-done = bf16[2,1536,1376]{1,2,0:T(8,128)(2,1)S(1)} copy-done((bf16[2,1536,1376]{1,2,0:T(8,128)(2,1)S(1)}, bf16[2,1536,1376]{1,2,0:T(8,128)(2,1)}, u32[]{:S(2)}) %copy-start) | copy-done | bytes 8454168
  36.3 4.5 %rank_grad.1 = (f32[2,344,128]{2,1,0:T(8,128)S(1)}, bf16[2,344,128]{2,1,0:T(8,128)(2,1)S(1)}, bf16[2,344,128]{2,1,0:T(8,128)(2,1)S(1)}, bf16[2,344,128]{2,1,0:T(8,128)(2,1)S(1)}) custom-call(s32[4]{0:T(128)S(1)} %pad_add_fusion.pos, bf16[768,256]{1,0:T(8,128)(2,1)S(1)} %pad_maximum_fusion.mine_ref, bf16[768,256]{1,0:T(8,128)(2,1)S(1)} %collective-permute-done.8.theirs_ref, ...), custom_call_target="tpu_custom_call" | custom-call | tf_op jit(solution)/shard_map/rank_grad/pallas_call | solution.py:142
  40.7 1.7 %collective-permute-start.9 = (bf16[2,344,128]{2,1,0:T(8,128)(2,1)S(1)}, bf16[2,344,128]{2,1,0:T(8,128)(2,1)S(1)}, u32[]{:S(2)}, u32[]{:S(2)}) collective-permute-start(bf16[2,344,128]{2,1,0:T(8,128)(2,1)S(1)} %get-tuple-element.15), channel_id=1, source_target_pairs={{0,32},{16,48},{32,64},{48,80},{64,96},{80,112},{96,0},{112,16},{1... | collective-permute-start | bytes 528392 | tf_op jit(solution)/shard_map/ppermute | solution.py:39
  42.5 2.9 %collective-permute-start.10 = (bf16[2,344,128]{2,1,0:T(8,128)(2,1)S(1)}, bf16[2,344,128]{2,1,0:T(8,128)(2,1)S(1)}, u32[]{:S(2)}, u32[]{:S(2)}) collective-permute-start(bf16[2,344,128]{2,1,0:T(8,128)(2,1)S(1)} %get-tuple-element.16), channel_id=1, source_target_pairs={{0,64},{16,80},{32,96},{48,112},{64,0},{80,16},{96,32},{112,48},{1... | collective-permute-start | bytes 528392 | tf_op jit(solution)/shard_map/ppermute | solution.py:39
  45.4 1.3 %collective-permute-start.11 = (bf16[2,344,128]{2,1,0:T(8,128)(2,1)S(1)}, bf16[2,344,128]{2,1,0:T(8,128)(2,1)S(1)}, u32[]{:S(2)}, u32[]{:S(2)}) collective-permute-start(bf16[2,344,128]{2,1,0:T(8,128)(2,1)S(1)} %get-tuple-element.17), channel_id=1, source_target_pairs={{0,96},{16,112},{32,0},{48,16},{64,32},{80,48},{96,64},{112,80},{1... | collective-permute-start | bytes 528392 | tf_op jit(solution)/shard_map/ppermute | solution.py:39
  46.7 3.9 %collective-permute-start.13 = (f32[344,128]{1,0:T(8,128)S(1)}, f32[344,128]{1,0:T(8,128)S(1)}, u32[]{:S(2)}, u32[]{:S(2)}) collective-permute-start(f32[344,128]{1,0:T(8,128)S(1)} %bitcast.15), channel_id=1, source_target_pairs={{0,16},{16,0},{32,48},{48,32},{64,80},{80,64},{96,112},{112,96},{1... | collective-permute-start | bytes 528392 | tf_op jit(solution)/shard_map/ppermute | solution.py:43
  50.7 2.9 %collective-permute-done.10 = bf16[2,344,128]{2,1,0:T(8,128)(2,1)S(1)} collective-permute-done((bf16[2,344,128]{2,1,0:T(8,128)(2,1)S(1)}, bf16[2,344,128]{2,1,0:T(8,128)(2,1)S(1)}, u32[]{:S(2)}, u32[]{:S(2)}) %collective-permute-start.10) | collective-permute-done | bytes 176160 | tf_op jit(solution)/shard_map/ppermute | solution.py:39
  53.7 4.0 %collective-permute-start.12 = (bf16[2,344,128]{2,1,0:T(8,128)(2,1)S(1)}, bf16[2,344,128]{2,1,0:T(8,128)(2,1)S(1)}, u32[]{:S(2)}, u32[]{:S(2)}) collective-permute-start(bf16[2,344,128]{2,1,0:T(8,128)(2,1)S(1)} %get-tuple-element.24), channel_id=1, source_target_pairs={{0,16},{16,0},{32,48},{48,32},{64,80},{80,64},{96,112},{112,96},{1... | collective-permute-start | bytes 528392 | tf_op jit(solution)/shard_map/ppermute | solution.py:43
  57.7 1.0 %collective-permute-done.14.far_second_ref = f32[344,128]{1,0:T(8,128)S(1)} collective-permute-done((f32[344,128]{1,0:T(8,128)S(1)}, f32[344,128]{1,0:T(8,128)S(1)}, u32[]{:S(2)}, u32[]{:S(2)}) %collective-permute-start.14) | collective-permute-done | bytes 176160 | tf_op jit(solution)/shard_map/ppermute | solution.py:43
  58.7 3.4 %collective-permute-done.12.got_ref = bf16[2,344,128]{2,1,0:T(8,128)(2,1)S(1)} collective-permute-done((bf16[2,344,128]{2,1,0:T(8,128)(2,1)S(1)}, bf16[2,344,128]{2,1,0:T(8,128)(2,1)S(1)}, u32[]{:S(2)}, u32[]{:S(2)}) %collective-permute-start.12) | collective-permute-done | bytes 176160 | tf_op jit(solution)/shard_map/ppermute | solution.py:43
  63.0 2.4 %collective-permute-start.17 = (bf16[2,344,128]{2,1,0:T(8,128)(2,1)S(1)}, bf16[2,344,128]{2,1,0:T(8,128)(2,1)S(1)}, u32[]{:S(2)}, u32[]{:S(2)}) collective-permute-start(bf16[2,344,128]{2,1,0:T(8,128)(2,1)S(1)} %get-tuple-element.18.refs_0_.refs_4_), channel_id=1, source_target_pairs={{0,96},{16,112},{32,0},{48,16},{64,32},{80,48},{96,64},{112,80},{1... | collective-permute-start | bytes 528392 | tf_op jit(solution)/shard_map/ppermute | solution.py:39
  66.3 1.1 %constant_dynamic-slice_fusion.refs_8_ = bf16[2,1024,128]{2,1,0:T(8,128)(2,1)S(1)} fusion(bf16[2,8192,128]{2,1,0:T(8,128)(2,1)} %param.7, s32[]{:T(128)S(6)} %select_n.7), kind=kLoop, calls=%fused_computation.8 | loop fusion | bytes 1048580 | tf_op jit(solution)/shard_map/dynamic_slice | solution.py:255
  69.2 3.2 %collective-permute-done.17.refs_3_.refs_7_ = bf16[2,344,128]{2,1,0:T(8,128)(2,1)S(1)} collective-permute-done((bf16[2,344,128]{2,1,0:T(8,128)(2,1)S(1)}, bf16[2,344,128]{2,1,0:T(8,128)(2,1)S(1)}, u32[]{:S(2)}, u32[]{:S(2)}) %collective-permute-start.17) | collective-permute-done | bytes 176160 | tf_op jit(solution)/shard_map/ppermute | solution.py:39
  72.4 1.8 %collective-permute-done.16.refs_2_.refs_6_ = bf16[2,344,128]{2,1,0:T(8,128)(2,1)S(1)} collective-permute-done((bf16[2,344,128]{2,1,0:T(8,128)(2,1)S(1)}, bf16[2,344,128]{2,1,0:T(8,128)(2,1)S(1)}, u32[]{:S(2)}, u32[]{:S(2)}) %collective-permute-start.16) | collective-permute-done | bytes 176160 | tf_op jit(solution)/shard_map/ppermute | solution.py:39
  74.2 1.6 %collective-permute-done.15.refs_1_.refs_5_ = bf16[2,344,128]{2,1,0:T(8,128)(2,1)S(1)} collective-permute-done((bf16[2,344,128]{2,1,0:T(8,128)(2,1)S(1)}, bf16[2,344,128]{2,1,0:T(8,128)(2,1)S(1)}, u32[]{:S(2)}, u32[]{:S(2)}) %collective-permute-start.15) | collective-permute-done | bytes 176160 | tf_op jit(solution)/shard_map/ppermute | solution.py:39
  75.8 4.6 %update.1 = bf16[2,1376,1024]{2,1,0:T(8,128)(2,1)} custom-call(s32[4]{0:T(128)S(1)} %pad_add_fusion.pos, bf16[2,344,128]{2,1,0:T(8,128)(2,1)S(1)} %get-tuple-element.18.refs_0_.refs_4_, bf16[2,344,128]{2,1,0:T(8,128)(2,1)S(1)} %collective-permute-done.15.refs_1_.refs_5_, bf16[2,344,128]{2,1,0:T(8,128)(2,1)S(1)} %collective-permute-done.16.refs_2_.refs_6_, ...), custom_call_target="tpu_custom_call" | custom-call | tf_op jit(solution)/shard_map/update/pallas_call | solution.py:232
  (28 shorter events, 5.9 us)
Async XLA Ops:
  1.7 1.4 %copy-start.1 = (bf16[1536,512]{1,0:T(8,128)(2,1)S(1)}, bf16[1536,512]{1,0:T(8,128)(2,1)}, u32[]{:S(2)}) copy-start(bf16[1536,512]{1,0:T(8,128)(2,1)} %inputs_ref.1) | copy-start | bytes 4718596
  5.8 1.8 %collective-permute-start = (bf16[768,256]{1,0:T(8,128)(2,1)S(1)}, bf16[768,256]{1,0:T(8,128)(2,1)S(1)}, u32[]{:S(2)}, u32[]{:S(2)}) collective-permute-start(bf16[768,256]{1,0:T(8,128)(2,1)S(1)} %get-tuple-element.13), channel_id=1, source_target_pairs={{0,1},{1,0},{2,3},{3,2},{4,5},{5,4},{6,7},{7,6},{8,9},{9,8},{10,11... | collective-permute-start | bytes 1179656 | tf_op jit(solution)/shard_map/ppermute | solution.py:26
  7.7 6.1 %collective-permute-start.1 = (bf16[192,256]{1,0:T(8,128)(2,1)S(1)}, bf16[192,256]{1,0:T(8,128)(2,1)S(1)}, u32[]{:S(2)}, u32[]{:S(2)}) collective-permute-start(bf16[192,256]{1,0:T(8,128)(2,1)S(1)} %get-tuple-element.26), channel_id=1, source_target_pairs={{0,2},{1,3},{2,4},{3,5},{4,6},{5,7},{6,0},{7,1},{8,10},{9,11},{10,... | collective-permute-start | bytes 294920 | tf_op jit(solution)/shard_map/ppermute | solution.py:31
  9.3 5.0 %collective-permute-start.3 = (bf16[192,256]{1,0:T(8,128)(2,1)S(1)}, bf16[192,256]{1,0:T(8,128)(2,1)S(1)}, u32[]{:S(2)}, u32[]{:S(2)}) collective-permute-start(bf16[192,256]{1,0:T(8,128)(2,1)S(1)} %get-tuple-element.27), channel_id=1, source_target_pairs={{0,6},{1,7},{2,0},{3,1},{4,2},{5,3},{6,4},{7,5},{8,14},{9,15},{10,... | collective-permute-start | bytes 294920 | tf_op jit(solution)/shard_map/ppermute | solution.py:31
  11.0 6.1 %collective-permute-start.2 = (bf16[192,256]{1,0:T(8,128)(2,1)S(1)}, bf16[192,256]{1,0:T(8,128)(2,1)S(1)}, u32[]{:S(2)}, u32[]{:S(2)}) collective-permute-start(bf16[192,256]{1,0:T(8,128)(2,1)S(1)} %get-tuple-element.28), channel_id=1, source_target_pairs={{0,4},{1,5},{2,6},{3,7},{4,0},{5,1},{6,2},{7,3},{8,12},{9,13},{10,... | collective-permute-start | bytes 294920 | tf_op jit(solution)/shard_map/ppermute | solution.py:31
  17.2 4.7 %collective-permute-start.4 = (bf16[192,256]{1,0:T(8,128)(2,1)S(1)}, bf16[192,256]{1,0:T(8,128)(2,1)S(1)}, u32[]{:S(2)}, u32[]{:S(2)}) collective-permute-start(bf16[192,256]{1,0:T(8,128)(2,1)S(1)} %fusion), channel_id=1, source_target_pairs={{0,8},{1,9},{2,10},{3,11},{4,12},{5,13},{6,14},{7,15},{8,0},{9,1},... | collective-permute-start | bytes 294920 | tf_op jit(solution)/shard_map/ppermute | solution.py:35
  22.0 4.7 %collective-permute-start.7 = (bf16[192,256]{1,0:T(8,128)(2,1)S(1)}, bf16[192,256]{1,0:T(8,128)(2,1)S(1)}, u32[]{:S(2)}, u32[]{:S(2)}) collective-permute-start(bf16[192,256]{1,0:T(8,128)(2,1)S(1)} %add_convert_fusion), channel_id=1, source_target_pairs={{0,6},{1,7},{2,0},{3,1},{4,2},{5,3},{6,4},{7,5},{8,14},{9,15},{10,... | collective-permute-start | bytes 294920 | tf_op jit(solution)/shard_map/ppermute | solution.py:31
  23.8 6.1 %collective-permute-start.6 = (bf16[192,256]{1,0:T(8,128)(2,1)S(1)}, bf16[192,256]{1,0:T(8,128)(2,1)S(1)}, u32[]{:S(2)}, u32[]{:S(2)}) collective-permute-start(bf16[192,256]{1,0:T(8,128)(2,1)S(1)} %add_convert_fusion), channel_id=1, source_target_pairs={{0,4},{1,5},{2,6},{3,7},{4,0},{5,1},{6,2},{7,3},{8,12},{9,13},{10,... | collective-permute-start | bytes 294920 | tf_op jit(solution)/shard_map/ppermute | solution.py:31
  25.2 5.9 %collective-permute-start.5 = (bf16[192,256]{1,0:T(8,128)(2,1)S(1)}, bf16[192,256]{1,0:T(8,128)(2,1)S(1)}, u32[]{:S(2)}, u32[]{:S(2)}) collective-permute-start(bf16[192,256]{1,0:T(8,128)(2,1)S(1)} %add_convert_fusion), channel_id=1, source_target_pairs={{0,2},{1,3},{2,4},{3,5},{4,6},{5,7},{6,0},{7,1},{8,10},{9,11},{10,... | collective-permute-start | bytes 294920 | tf_op jit(solution)/shard_map/ppermute | solution.py:31
  31.0 1.8 %collective-permute-start.8 = (bf16[768,256]{1,0:T(8,128)(2,1)S(1)}, bf16[768,256]{1,0:T(8,128)(2,1)S(1)}, u32[]{:S(2)}, u32[]{:S(2)}) collective-permute-start(bf16[768,256]{1,0:T(8,128)(2,1)S(1)} %pad_maximum_fusion.mine_ref), channel_id=1, source_target_pairs={{0,1},{1,0},{2,3},{3,2},{4,5},{5,4},{6,7},{7,6},{8,9},{9,8},{10,11... | collective-permute-start | bytes 1179656 | tf_op jit(solution)/shard_map/ppermute | solution.py:26
  32.8 3.4 %copy-start = (bf16[2,1536,1376]{1,2,0:T(8,128)(2,1)S(1)}, bf16[2,1536,1376]{1,2,0:T(8,128)(2,1)}, u32[]{:S(2)}) copy-start(bf16[2,1536,1376]{1,2,0:T(8,128)(2,1)} %param.6) | copy-start | bytes 25362436
  36.2 10.5 %copy-start.2 = (f32[2,128,1,172]{1,2,3,0:T(1,128)S(1)}, f32[2,128,1,172]{1,2,3,0:T(1,128)}, u32[]{:S(2)}) copy-start(f32[2,128,1,172]{1,2,3,0:T(1,128)} %param.8) | copy-start | bytes 528388
  36.2 14.4 %copy-start.3 = (f32[2,128,1,172]{1,2,3,0:T(1,128)S(1)}, f32[2,128,1,172]{1,2,3,0:T(1,128)}, u32[]{:S(2)}) copy-start(f32[2,128,1,172]{1,2,3,0:T(1,128)} %param.9) | copy-start | bytes 528388
  40.7 10.0 %collective-permute-start.9 = (bf16[2,344,128]{2,1,0:T(8,128)(2,1)S(1)}, bf16[2,344,128]{2,1,0:T(8,128)(2,1)S(1)}, u32[]{:S(2)}, u32[]{:S(2)}) collective-permute-start(bf16[2,344,128]{2,1,0:T(8,128)(2,1)S(1)} %get-tuple-element.15), channel_id=1, source_target_pairs={{0,32},{16,48},{32,64},{48,80},{64,96},{80,112},{96,0},{112,16},{1... | collective-permute-start | bytes 528392 | tf_op jit(solution)/shard_map/ppermute | solution.py:39
  42.5 11.2 %collective-permute-start.10 = (bf16[2,344,128]{2,1,0:T(8,128)(2,1)S(1)}, bf16[2,344,128]{2,1,0:T(8,128)(2,1)S(1)}, u32[]{:S(2)}, u32[]{:S(2)}) collective-permute-start(bf16[2,344,128]{2,1,0:T(8,128)(2,1)S(1)} %get-tuple-element.16), channel_id=1, source_target_pairs={{0,64},{16,80},{32,96},{48,112},{64,0},{80,16},{96,32},{112,48},{1... | collective-permute-start | bytes 528392 | tf_op jit(solution)/shard_map/ppermute | solution.py:39
  45.4 8.3 %collective-permute-start.11 = (bf16[2,344,128]{2,1,0:T(8,128)(2,1)S(1)}, bf16[2,344,128]{2,1,0:T(8,128)(2,1)S(1)}, u32[]{:S(2)}, u32[]{:S(2)}) collective-permute-start(bf16[2,344,128]{2,1,0:T(8,128)(2,1)S(1)} %get-tuple-element.17), channel_id=1, source_target_pairs={{0,96},{16,112},{32,0},{48,16},{64,32},{80,48},{96,64},{112,80},{1... | collective-permute-start | bytes 528392 | tf_op jit(solution)/shard_map/ppermute | solution.py:39
  46.7 11.0 %collective-permute-start.13 = (f32[344,128]{1,0:T(8,128)S(1)}, f32[344,128]{1,0:T(8,128)S(1)}, u32[]{:S(2)}, u32[]{:S(2)}) collective-permute-start(f32[344,128]{1,0:T(8,128)S(1)} %bitcast.15), channel_id=1, source_target_pairs={{0,16},{16,0},{32,48},{48,32},{64,80},{80,64},{96,112},{112,96},{1... | collective-permute-start | bytes 528392 | tf_op jit(solution)/shard_map/ppermute | solution.py:43
  50.6 8.1 %collective-permute-start.14 = (f32[344,128]{1,0:T(8,128)S(1)}, f32[344,128]{1,0:T(8,128)S(1)}, u32[]{:S(2)}, u32[]{:S(2)}) collective-permute-start(f32[344,128]{1,0:T(8,128)S(1)} %bitcast.17), channel_id=1, source_target_pairs={{0,16},{16,0},{32,48},{48,32},{64,80},{80,64},{96,112},{112,96},{1... | collective-permute-start | bytes 528392 | tf_op jit(solution)/shard_map/ppermute | solution.py:43
  53.7 8.3 %collective-permute-start.12 = (bf16[2,344,128]{2,1,0:T(8,128)(2,1)S(1)}, bf16[2,344,128]{2,1,0:T(8,128)(2,1)S(1)}, u32[]{:S(2)}, u32[]{:S(2)}) collective-permute-start(bf16[2,344,128]{2,1,0:T(8,128)(2,1)S(1)} %get-tuple-element.24), channel_id=1, source_target_pairs={{0,16},{16,0},{32,48},{48,32},{64,80},{80,64},{96,112},{112,96},{1... | collective-permute-start | bytes 528392 | tf_op jit(solution)/shard_map/ppermute | solution.py:43
  63.0 9.4 %collective-permute-start.17 = (bf16[2,344,128]{2,1,0:T(8,128)(2,1)S(1)}, bf16[2,344,128]{2,1,0:T(8,128)(2,1)S(1)}, u32[]{:S(2)}, u32[]{:S(2)}) collective-permute-start(bf16[2,344,128]{2,1,0:T(8,128)(2,1)S(1)} %get-tuple-element.18.refs_0_.refs_4_), channel_id=1, source_target_pairs={{0,96},{16,112},{32,0},{48,16},{64,32},{80,48},{96,64},{112,80},{1... | collective-permute-start | bytes 528392 | tf_op jit(solution)/shard_map/ppermute | solution.py:39
  65.4 8.9 %collective-permute-start.16 = (bf16[2,344,128]{2,1,0:T(8,128)(2,1)S(1)}, bf16[2,344,128]{2,1,0:T(8,128)(2,1)S(1)}, u32[]{:S(2)}, u32[]{:S(2)}) collective-permute-start(bf16[2,344,128]{2,1,0:T(8,128)(2,1)S(1)} %get-tuple-element.18.refs_0_.refs_4_), channel_id=1, source_target_pairs={{0,64},{16,80},{32,96},{48,112},{64,0},{80,16},{96,32},{112,48},{1... | collective-permute-start | bytes 528392 | tf_op jit(solution)/shard_map/ppermute | solution.py:39
  65.9 9.9 %collective-permute-start.15 = (bf16[2,344,128]{2,1,0:T(8,128)(2,1)S(1)}, bf16[2,344,128]{2,1,0:T(8,128)(2,1)S(1)}, u32[]{:S(2)}, u32[]{:S(2)}) collective-permute-start(bf16[2,344,128]{2,1,0:T(8,128)(2,1)S(1)} %get-tuple-element.18.refs_0_.refs_4_), channel_id=1, source_target_pairs={{0,32},{16,48},{32,64},{48,80},{64,96},{80,112},{96,0},{112,16},{1... | collective-permute-start | bytes 528392 | tf_op jit(solution)/shard_map/ppermute | solution.py:39

commit v2 on v0

v2 whole, which is shorter than its diff:
```python
import jax
import jax.numpy as jnp
from jax import lax
from jax.experimental import pallas as pl
from jax.experimental.pallas import tpu as pltpu
from jax.sharding import PartitionSpec as P

STEP = 10

beta_one = 0.9
beta_two = 0.999
epsilon = 1e-08
corr_one = 1.0 - beta_one**STEP
corr_two = 1.0 - beta_two**STEP

NX, NY = 4, 4

F32, BF16 = jnp.float32, jnp.bfloat16
HBM = pl.BlockSpec(memory_space=pltpu.HBM)
VMEM = pl.BlockSpec(memory_space=pltpu.VMEM)


def swap(v, axis, size, bits):
    return lax.ppermute(v, axis, [(i, i ^ bits) for i in range(size)])


def to_core(v):
    return swap(v, "tensor", 16, 1)


def to_x(v, k):
    return swap(v, "tensor", 16, k * 2)


def to_zlo(v):
    return swap(v, "tensor", 16, 8)


def to_y(v, k):
    return swap(v, "dp", 8, k * 2)


def to_zhi(v):
    return swap(v, "dp", 8, 1)


def place():
    t, d = lax.axis_index("tensor"), lax.axis_index("dp")
    return {"t": t, "core": t & 1, "x": (t >> 1) & 3, "y": d >> 1, "z": d & 1}


def params(mib):
    return pltpu.CompilerParams(vmem_limit_bytes=mib * 2**20)


def cost(flops, moved):
    return pl.CostEstimate(flops=flops, bytes_accessed=moved, transcendentals=0)


def project_kernel(
    inputs_ref, basis_ref, send_ref, own_ref, rows, basis, row_sem, basis_sem
):
    at = place()
    n_g, feat, rank = basis.shape
    half = rows.shape[1]
    piece = half // NX
    copies = []
    for g in range(n_g):
        src = basis_ref.at[g, pl.ds(pl.multiple_of(at["t"] * feat, feat), feat), :]
        copies.append(pltpu.make_async_copy(src, basis.at[g], basis_sem.at[g]))
    for h, core in enumerate((1 - at["core"], at["core"])):
        src = inputs_ref.at[pl.ds(pl.multiple_of(core * half, half), half), :]
        copies.append(pltpu.make_async_copy(src, rows.at[h], row_sem.at[h]))
    for copy in copies:
        copy.start()
    for copy in copies[:n_g]:
        copy.wait()
    both = jnp.concatenate([basis[g] for g in range(n_g)], axis=1)
    for h in range(2):
        copies[n_g + h].wait()
        for k in range(NX):
            src = pl.multiple_of((at["x"] ^ k) * piece, piece)
            product = jnp.dot(rows[h, pl.ds(src, piece), :], both, preferred_element_type=F32)
            to = slice(k * piece, (k + 1) * piece)
            if h == 0:
                send_ref[to, :] = product.astype(BF16)
            else:
                own_ref[to, :] = product


def project(inputs, basis):
    tokens, feat = inputs.shape
    n_g, _, rank = basis.shape
    half = tokens // 2
    return pl.pallas_call(
        project_kernel,
        in_specs=[HBM] * 2,
        out_specs=[VMEM] * 2,
        out_shape=[
            jax.ShapeDtypeStruct((half, n_g * rank), BF16),
            jax.ShapeDtypeStruct((half, n_g * rank), F32),
        ],
        scratch_shapes=[
            pltpu.VMEM((2, half, feat), BF16),
            pltpu.VMEM((n_g, feat, rank), BF16),
            pltpu.SemaphoreType.DMA((2,)),
            pltpu.SemaphoreType.DMA((n_g,)),
        ],
        compiler_params=params(52),
        cost_estimate=cost(2 * tokens * feat * n_g * rank, 2 * tokens * feat),
        name="project",
    )(inputs, basis)


def half_product(at, core, part_ref, grad_ref, proj, g):
    half = part_ref.shape[0]
    piece = half // NX
    rank = proj.shape[1]
    for k in range(NX):
        to = pl.multiple_of((at["x"] ^ k) * piece, piece)
        proj[pl.ds(to, piece), :] = part_ref[
            k * piece : (k + 1) * piece, g * rank : (g + 1) * rank
        ]
    tokens = pl.ds(pl.multiple_of(core * half, half), half)
    return jnp.dot(grad_ref[:, tokens], proj[...], preferred_element_type=F32)


def near_kernel(part_ref, *refs):
    grads, total_ref, proj = refs[:-2], refs[-2], refs[-1]
    at = place()
    for g, grad_ref in enumerate(grads):
        total_ref[g] = half_product(at, at["core"], part_ref, grad_ref, proj.at[g], g)


def rank_near(part, grads, rank):
    cols, tokens = grads[0].shape
    n_g = len(grads)
    return pl.pallas_call(
        near_kernel,
        in_specs=[VMEM] * (1 + n_g),
        out_specs=VMEM,
        out_shape=jax.ShapeDtypeStruct((n_g, cols, rank), F32),
        scratch_shapes=[pltpu.VMEM((n_g, tokens // 2, rank), BF16)],
        compiler_params=params(8),
        cost_estimate=cost(n_g * tokens * cols * rank, 4 * 2**20),
        name="rank_near",
    )(part, *grads)


def far_kernel(g, part_ref, near_ref, grad_ref, own_ref, *refs):
    outs, proj, total = refs[:-2], refs[-2], refs[-1]
    at = place()
    share = own_ref.shape[0]
    total[...] = near_ref[g] + half_product(at, 1 - at["core"], part_ref, grad_ref, proj, g)
    for k in range(NY):
        mine = total[pl.ds(pl.multiple_of((at["y"] ^ k) * share, 8), share), :]
        if k == 0:
            own_ref[...] = mine
        else:
            outs[k - 1][...] = mine.astype(BF16)


def rank_far(part, near, grad, g):
    cols, tokens = grad.shape
    rank = near.shape[2]
    share = cols // NY
    return pl.pallas_call(
        lambda *refs: far_kernel(g, *refs),
        in_specs=[VMEM] * 3,
        out_specs=[VMEM] * NY,
        out_shape=[jax.ShapeDtypeStruct((share, rank), F32)]
        + [jax.ShapeDtypeStruct((share, rank), BF16)] * (NY - 1),
        scratch_shapes=[pltpu.VMEM((tokens // 2, rank), BF16), pltpu.VMEM((cols, rank), F32)],
        compiler_params=params(8),
        cost_estimate=cost(tokens * cols * rank, 2 * 2**20),
        name="rank_far",
    )(part, near, grad)


def adam_kernel(n_g, *refs):
    owns, gots = refs[:n_g], refs[n_g : 2 * n_g]
    near_ref, far_ref, norm_ref, new_first_ref, new_second_ref = refs[2 * n_g :]
    low = place()["z"] == 0
    half = owns[0].shape[0] // 2
    for g in range(n_g):
        grad = owns[g][...] + gots[g][...].astype(F32)

        def moment(i):
            rows = slice((i * n_g + g) * half, (i * n_g + g + 1) * half)
            near, far = near_ref[rows, :], far_ref[rows, :]
            return jnp.concatenate(
                [jnp.where(low, near, far), jnp.where(low, far, near)], axis=0
            )

        new_first = beta_one * moment(0) + (1.0 - beta_one) * grad
        new_second = beta_two * moment(1) + (1.0 - beta_two) * grad * grad
        norm_ref[g] = (
            new_first / corr_one / (jnp.sqrt(new_second / corr_two) + epsilon)
        ).astype(BF16)
        rows = slice(g * half, (g + 1) * half)
        new_first_ref[rows, 0, :] = jnp.where(low, new_first[:half], new_first[half:])
        new_second_ref[rows, 0, :] = jnp.where(low, new_second[:half], new_second[half:])


def adam(owns, gots, moments, far_moments):
    n_g = len(owns)
    share, rank = owns[0].shape
    return pl.pallas_call(
        lambda *refs: adam_kernel(n_g, *refs),
        in_specs=[VMEM] * (2 * n_g + 2),
        out_specs=[VMEM] * 3,
        out_shape=[jax.ShapeDtypeStruct((n_g, share, rank), BF16)]
        + [jax.ShapeDtypeStruct((n_g * share // 2, 1, rank), F32)] * 2,
        compiler_params=params(8),
        name="adam",
    )(*owns, *gots, moments, far_moments)


BLOCK = 352


def update_kernel(first_half, even_ref, odd_ref, basis_ref, *refs):
    out_ref, wide, norm, block, sem = refs[-5:]
    y = place()["y"]
    pair = y >> 1 if first_half else 1 - (y >> 1)
    n_g, share, _ = even_ref.shape
    rows = 2 * share
    copies = []
    for g in range(n_g):
        for ref, parity in ((even_ref, y & 1), (odd_ref, 1 - (y & 1))):
            wide[g, pl.ds(pl.multiple_of(parity * share, 8), share), :] = ref[g].astype(F32)
        norm[g] = wide[g].astype(BF16)
        for i, start in enumerate(range(0, rows, BLOCK)):
            size = min(BLOCK, rows - start)
            block[g, start : start + size, :] = jnp.dot(
                norm[g, start : start + size, :], basis_ref[g], preferred_element_type=F32
            ).astype(BF16)
            copies.append(
                pltpu.make_async_copy(
                    block.at[g, start : start + size, :],
                    out_ref.at[g, pl.ds(pl.multiple_of(pair * rows + start, 16), size), :],
                    sem.at[g, i],
                )
            )
            copies[-1].start()
    for copy in copies:
        copy.wait()


def update(even, odd, basis_t, out):
    n_g, share, rank = even.shape
    weight_rows = basis_t.shape[2]
    return pl.pallas_call(
        lambda *refs: update_kernel(out is None, *refs),
        in_specs=[VMEM] * 3 + ([HBM] if out is not None else []),
        out_specs=HBM,
        out_shape=jax.ShapeDtypeStruct((n_g, share * NY, weight_rows), BF16),
        scratch_shapes=[
            pltpu.VMEM((n_g, 2 * share, rank), F32),
            pltpu.VMEM((n_g, 2 * share, rank), BF16),
            pltpu.VMEM((n_g, 2 * share, weight_rows), BF16),
            pltpu.SemaphoreType.DMA((n_g, pl.cdiv(2 * share, BLOCK))),
        ],
        input_output_aliases={} if out is None else {3: 0},
        compiler_params=params(12),
        cost_estimate=cost(4 * n_g * share * rank * weight_rows, 4 * n_g * share * weight_rows),
        name="update",
    )(even, odd, basis_t, *([] if out is None else [out]))


def body(inputs, grad_out, basis, first_moment, second_moment):
    weight_rows = basis.shape[1] // lax.axis_size("dp")
    row_basis = lax.dynamic_slice_in_dim(
        basis, lax.axis_index("dp") * weight_rows, weight_rows, 1
    )
    row_basis_t = jnp.transpose(row_basis, (0, 2, 1))
    piece = inputs.shape[0] // (2 * NX)
    grad_t = jnp.transpose(grad_out, (0, 2, 1))
    n_g, rank = first_moment.shape[:2]
    flat = lambda m: jnp.transpose(m, (0, 3, 2, 1)).reshape(-1, rank)
    send, own = project(inputs, basis)
    send, first, second = lax.optimization_barrier(
        (send, flat(first_moment), flat(second_moment))
    )
    moments = jnp.concatenate([first, second], axis=0)
    got = to_core(send)
    far_moments = to_zhi(moments)
    part = lambda v, k: v[k * piece : (k + 1) * piece].astype(F32)
    sums = [part(own, k) + part(got, k) for k in range(NX)]
    total = sums[0]
    for k in range(1, NX):
        total = total + to_x(sums[k].astype(BF16), k).astype(F32)
    total, far_moments, row_basis_t = lax.optimization_barrier(
        (total, far_moments, row_basis_t)
    )
    total = (total + to_zlo(total.astype(BF16)).astype(F32)).astype(BF16)
    near_part = jnp.concatenate([total] + [to_x(total, k) for k in range(1, NX)], axis=0)
    near_part, *grads = lax.optimization_barrier((near_part, *(grad_t[g] for g in range(n_g))))
    far_part = to_core(near_part)
    near = rank_near(near_part, grads, rank)
    far_part, near = lax.optimization_barrier((far_part, near))

    owns, gots = [], []
    for g in range(n_g):
        own, *others = rank_far(far_part, near, grads[g], g)
        for k in range(1, NY):
            own = own + to_y(others[k - 1], k).astype(F32)
        owns.append(own)
        gots.append(to_zhi(own.astype(BF16)))
    norm, new_first, new_second = adam(owns, gots, moments, far_moments)
    pieces = [norm] + [to_y(norm, k) for k in range(1, NY)]
    out = update(pieces[0], pieces[1], row_basis_t, None)
    out = update(pieces[2], pieces[3], row_basis_t, out)

    def shaped(m):
        return jnp.transpose(m.reshape(n_g, -1, 1, rank), (0, 3, 2, 1))

    return jnp.transpose(out, (0, 2, 1)), shaped(new_first), shaped(new_second)


def solution(mesh):
    in_specs = (
        P("dp", "tensor"),
        P(None, "dp", "tensor"),
        P(),
        P(None, None, "tensor", "dp"),
        P(None, None, "tensor", "dp"),
    )
    out_specs = (
        P(None, "dp", "tensor"),
        P(None, None, "tensor", "dp"),
        P(None, None, "tensor", "dp"),
    )
    return jax.shard_map(body, mesh=mesh, in_specs=in_specs, out_specs=out_specs, check_vma=False)
```

time: 301 us -> 66.5 us (0.22)
  waiting for transfers between devices: 195 us -> 16.2 us
  blocking collectives: 68.8 us -> 0 us
  starting transfers between devices: 0.12 us -> 33.9 us
  matrix products: 14.8 us -> 0 us
  between operations: 13.8 us -> 0.82 us
  Pallas kernels: 0 us -> 10.1 us
    all_gather x2 -> x0, waiting for transfers between devices: 104 us -> none  [the longest x1 52.1 us: body(): lax.all_gather(first_moment, 'dp', axis=3, tiled=True)]
    psum x1 -> x0, waiting for transfers between devices: 91.3 us -> none  [body(): rank_grad = lax.psum(rank_part, 'dp')]
    psum x1 -> x0, blocking collectives: 68.8 us -> none  [body(): summed = lax.psum(partial_proj.reshape(tokens, 2 * rank), 'tensor')]
    ppermute x0 -> x21, starting transfers between devices: none -> 33.9 us  [swap(): return lax.ppermute(v, axis, [(i, i ^ bits) for i in range(size)])]
    ppermute x0 -> x21, waiting for transfers between devices: none -> 16.2 us  [swap(): return lax.ppermute(v, axis, [(i, i ^ bits) for i in range(size)])]
    dot_general x3 -> x0, matrix products: 14.8 us -> none  [the longest x1 6.84 us: body(): jnp.einsum('tgk,gtc->gkc', projected, grad_out, preferred_element_type=jn...]
    pallas_call x0 -> x7, Pallas kernels: none -> 10.1 us  [the longest x2 3.9 us: update(): pl.pallas_call(lambda *refs: update_kernel(out is None, *refs), in_specs=...]
    unnamed x10 -> x6, local copies, waits for them, and re-layouts: 5.43 us -> 0.24 us
  transfers between devices with their start and end apart: 3 -> 21, of which waited for: 3 -> 10; matrix products, arithmetic and copies ran while one was open for 1% -> 8% of each run, Pallas kernels for 0% -> 6%
where the time goes in v2:
time: 66.5 us; the launch traced here: 66.4 us
  starting transfers between devices  33.9 us (51%)
  waiting for transfers between devices  16.2 us (24%)
  Pallas kernels  10.1 us (15%)
  local copies, waits for them, and re-layouts  5.1 us (8%)
  between operations  0.82 us (1%)
    ppermute x21, starting transfers between devices, swap(): return lax.ppermute(v, axis, [(i, i ^ bits) for i in range(size)])  33.9 us
    ppermute x21, waiting for transfers between devices, swap(): return lax.ppermute(v, axis, [(i, i ^ bits) for i in range(size)])  16.2 us
    pallas_call x2, Pallas kernels, update(): pl.pallas_call(lambda *refs: update_kernel(out is None, *refs), in_specs=...  3.9 us
    squeeze x1, local copies, waits for them, and re-layouts, body(): grad_t[g]  3.78 us
    pallas_call x1, Pallas kernels, project(): pl.pallas_call(project_kernel, in_specs=[HBM] * 2, out_specs=[VMEM] * 2,...  2.12 us
    pallas_call x2, Pallas kernels, rank_far(): pl.pallas_call(lambda *refs: far_kernel(g, *refs), in_specs=[VMEM] * 3, o...  1.67 us
    pallas_call x1, Pallas kernels, rank_near(): pl.pallas_call(near_kernel, in_specs=[VMEM] * (1 + n_g), out_specs=VMEM,...  1.35 us
  transfers between devices with their start and end apart: 21, of which 10 were waited for; matrix products, arithmetic and copies ran while one was open for 8% of the time, Pallas kernels for 6%

profile of v2, /device:TPU:0, one launch (start us, length us, event | category | flops | bytes accessed | tf_op | source)
XLA Modules:
  0.0 66.4 jit_solution(8253531864589125260)
XLA Ops:
  0.7 2.1 %project.1 = (bf16[768,256]{1,0:T(8,128)(2,1)S(1)}, f32[768,256]{1,0:T(8,128)S(1)}) custom-call(bf16[1536,512]{1,0:T(8,128)(2,1)} %inputs_ref.1, bf16[2,8192,128]{2,1,0:T(8,128)(2,1)} %basis_ref.1), custom_call_target="tpu_custom_call" | custom-call | flops 402653184 | bytes 1572864 | tf_op jit(solution)/shard_map/project/pallas_call | solution.py:95
  2.9 4.0 %collective-permute-start.4 = (f32[688,128]{1,0:T(8,128)S(1)}, f32[688,128]{1,0:T(8,128)S(1)}, u32[]{:S(2)}, u32[]{:S(2)}) collective-permute-start(f32[688,128]{1,0:T(8,128)S(1)} %constant_dynamic-update-slice_fusion.refs_4_), channel_id=1, source_target_pairs={{0,16},{16,0},{32,48},{48,32},{64,80},{80,64},{96,112},{112,96},{1... | collective-permute-start | bytes 1056776 | tf_op jit(solution)/shard_map/ppermute | solution.py:24
  7.0 1.6 %collective-permute-start.1 = (bf16[192,256]{1,0:T(8,128)(2,1)S(1)}, bf16[192,256]{1,0:T(8,128)(2,1)S(1)}, u32[]{:S(2)}, u32[]{:S(2)}) collective-permute-start(bf16[192,256]{1,0:T(8,128)(2,1)S(1)} %get-tuple-element.57), channel_id=1, source_target_pairs={{0,2},{1,3},{2,0},{3,1},{4,6},{5,7},{6,4},{7,5},{8,10},{9,11},{10,... | collective-permute-start | bytes 294920 | tf_op jit(solution)/shard_map/ppermute | solution.py:24
  8.6 2.1 %collective-permute-start.3 = (bf16[192,256]{1,0:T(8,128)(2,1)S(1)}, bf16[192,256]{1,0:T(8,128)(2,1)S(1)}, u32[]{:S(2)}, u32[]{:S(2)}) collective-permute-start(bf16[192,256]{1,0:T(8,128)(2,1)S(1)} %get-tuple-element.58), channel_id=1, source_target_pairs={{0,6},{1,7},{2,4},{3,5},{4,2},{5,3},{6,0},{7,1},{8,14},{9,15},{10,... | collective-permute-start | bytes 294920 | tf_op jit(solution)/shard_map/ppermute | solution.py:24
  10.7 0.6 collective-permute-start.2
  11.4 1.1 %constant_dynamic-slice_fusion = bf16[2,1024,128]{2,1,0:T(8,128)(2,1)S(1)} fusion(bf16[2,8192,128]{2,1,0:T(8,128)(2,1)} %basis_ref.1, s32[]{:T(128)S(6)} %select_n.3), kind=kLoop, calls=%fused_computation.12 | loop fusion | bytes 1048580 | tf_op jit(solution)/shard_map/dynamic_slice | solution.py:273
  12.7 2.3 %collective-permute-done.3 = bf16[192,256]{1,0:T(8,128)(2,1)S(1)} collective-permute-done((bf16[192,256]{1,0:T(8,128)(2,1)S(1)}, bf16[192,256]{1,0:T(8,128)(2,1)S(1)}, u32[]{:S(2)}, u32[]{:S(2)}) %collective-permute-start.3) | collective-permute-done | bytes 98336 | tf_op jit(solution)/shard_map/ppermute | solution.py:24
  15.0 1.8 %collective-permute-done.2 = bf16[192,256]{1,0:T(8,128)(2,1)S(1)} collective-permute-done((bf16[192,256]{1,0:T(8,128)(2,1)S(1)}, bf16[192,256]{1,0:T(8,128)(2,1)S(1)}, u32[]{:S(2)}, u32[]{:S(2)}) %collective-permute-start.2) | collective-permute-done | bytes 98336 | tf_op jit(solution)/shard_map/ppermute | solution.py:24
  16.9 1.1 %collective-permute-start.5 = (bf16[192,256]{1,0:T(8,128)(2,1)S(1)}, bf16[192,256]{1,0:T(8,128)(2,1)S(1)}, u32[]{:S(2)}, u32[]{:S(2)}) collective-permute-start(bf16[192,256]{1,0:T(8,128)(2,1)S(1)} %convert_element_type.73), channel_id=1, source_target_pairs={{0,8},{1,9},{2,10},{3,11},{4,12},{5,13},{6,14},{7,15},{8,0},{9,1},... | collective-permute-start | bytes 294920 | tf_op jit(solution)/shard_map/ppermute | solution.py:24
  18.0 3.6 %collective-permute-done.5 = bf16[192,256]{1,0:T(8,128)(2,1)S(1)} collective-permute-done((bf16[192,256]{1,0:T(8,128)(2,1)S(1)}, bf16[192,256]{1,0:T(8,128)(2,1)S(1)}, u32[]{:S(2)}, u32[]{:S(2)}) %collective-permute-start.5) | collective-permute-done | bytes 98336 | tf_op jit(solution)/shard_map/ppermute | solution.py:24
  21.6 1.9 %collective-permute-start.8 = (bf16[192,256]{1,0:T(8,128)(2,1)S(1)}, bf16[192,256]{1,0:T(8,128)(2,1)S(1)}, u32[]{:S(2)}, u32[]{:S(2)}) collective-permute-start(bf16[192,256]{1,0:T(8,128)(2,1)S(1)} %add_convert_fusion), channel_id=1, source_target_pairs={{0,6},{1,7},{2,4},{3,5},{4,2},{5,3},{6,0},{7,1},{8,14},{9,15},{10,... | collective-permute-start | bytes 294920 | tf_op jit(solution)/shard_map/ppermute | solution.py:24
  23.5 0.8 %collective-permute-start.7 = (bf16[192,256]{1,0:T(8,128)(2,1)S(1)}, bf16[192,256]{1,0:T(8,128)(2,1)S(1)}, u32[]{:S(2)}, u32[]{:S(2)}) collective-permute-start(bf16[192,256]{1,0:T(8,128)(2,1)S(1)} %add_convert_fusion), channel_id=1, source_target_pairs={{0,4},{1,5},{2,6},{3,7},{4,0},{5,1},{6,2},{7,3},{8,12},{9,13},{10,... | collective-permute-start | bytes 294920 | tf_op jit(solution)/shard_map/ppermute | solution.py:24
  24.4 1.4 %collective-permute-start.6 = (bf16[192,256]{1,0:T(8,128)(2,1)S(1)}, bf16[192,256]{1,0:T(8,128)(2,1)S(1)}, u32[]{:S(2)}, u32[]{:S(2)}) collective-permute-start(bf16[192,256]{1,0:T(8,128)(2,1)S(1)} %add_convert_fusion), channel_id=1, source_target_pairs={{0,2},{1,3},{2,0},{3,1},{4,6},{5,7},{6,4},{7,5},{8,10},{9,11},{10,... | collective-permute-start | bytes 294920 | tf_op jit(solution)/shard_map/ppermute | solution.py:24
  25.8 3.8 %slice_bitcast_fusion = (bf16[1376,1536]{1,0:T(8,128)(2,1)S(1)}, bf16[1376,1536]{1,0:T(8,128)(2,1)S(1)}) fusion(bf16[2,1376,1536]{2,1,0:T(8,128)(2,1)} %bitcast.22), kind=kLoop, calls=%fused_computation | loop fusion | bytes 16908288 | tf_op jit(solution)/shard_map/squeeze | solution.py:298
  29.8 1.3 %rank_near.1.refs_1_ = f32[2,1376,128]{2,1,0:T(8,128)S(1)} custom-call(bf16[768,256]{1,0:T(8,128)(2,1)S(1)} %pad_maximum_fusion.part_ref, bf16[1376,1536]{1,0:T(8,128)(2,1)S(1)} %get-tuple-element.34.refs_0_.refs_2_, bf16[1376,1536]{1,0:T(8,128)(2,1)S(1)} %get-tuple-element.35.refs_1_.refs_2_), custom_call_target="tpu_custom_call" | custom-call | flops 541065216 | bytes 4194304 | tf_op jit(solution)/shard_map/rank_near/pallas_call | solution.py:138
  31.5 0.8 %rank_far.3 = (f32[344,128]{1,0:T(8,128)S(1)}, bf16[344,128]{1,0:T(8,128)(2,1)S(1)}, bf16[344,128]{1,0:T(8,128)(2,1)S(1)}, bf16[344,128]{1,0:T(8,128)(2,1)S(1)}) custom-call(bf16[768,256]{1,0:T(8,128)(2,1)S(1)} %collective-permute-done.9.refs_0_, f32[2,1376,128]{2,1,0:T(8,128)S(1)} %rank_near.1.refs_1_, bf16[1376,1536]{1,0:T(8,128)(2,1)S(1)} %get-tuple-element.35.refs_1_.refs_2_), custom_call_target="tpu_custom_call" | custom-call | flops 270532608 | bytes 2097152 | tf_op jit(solution)/shard_map/rank_far/pallas_call | solution.py:167
  32.3 1.7 %collective-permute-start.13 = (bf16[344,128]{1,0:T(8,128)(2,1)S(1)}, bf16[344,128]{1,0:T(8,128)(2,1)S(1)}, u32[]{:S(2)}, u32[]{:S(2)}) collective-permute-start(bf16[344,128]{1,0:T(8,128)(2,1)S(1)} %get-tuple-element.43), channel_id=1, source_target_pairs={{0,32},{16,48},{32,0},{48,16},{64,96},{80,112},{96,64},{112,80},{1... | collective-permute-start | bytes 264200 | tf_op jit(solution)/shard_map/ppermute | solution.py:24
  34.0 2.9 %collective-permute-start.14 = (bf16[344,128]{1,0:T(8,128)(2,1)S(1)}, bf16[344,128]{1,0:T(8,128)(2,1)S(1)}, u32[]{:S(2)}, u32[]{:S(2)}) collective-permute-start(bf16[344,128]{1,0:T(8,128)(2,1)S(1)} %get-tuple-element.44), channel_id=1, source_target_pairs={{0,64},{16,80},{32,96},{48,112},{64,0},{80,16},{96,32},{112,48},{1... | collective-permute-start | bytes 264200 | tf_op jit(solution)/shard_map/ppermute | solution.py:24
  37.1 0.8 %rank_far.2 = (f32[344,128]{1,0:T(8,128)S(1)}, bf16[344,128]{1,0:T(8,128)(2,1)S(1)}, bf16[344,128]{1,0:T(8,128)(2,1)S(1)}, bf16[344,128]{1,0:T(8,128)(2,1)S(1)}) custom-call(bf16[768,256]{1,0:T(8,128)(2,1)S(1)} %collective-permute-done.9.refs_0_, f32[2,1376,128]{2,1,0:T(8,128)S(1)} %rank_near.1.refs_1_, bf16[1376,1536]{1,0:T(8,128)(2,1)S(1)} %get-tuple-element.34.refs_0_.refs_2_), custom_call_target="tpu_custom_call" | custom-call | flops 270532608 | bytes 2097152 | tf_op jit(solution)/shard_map/rank_far/pallas_call | solution.py:167
  38.4 4.1 %collective-permute-start.11 = (bf16[344,128]{1,0:T(8,128)(2,1)S(1)}, bf16[344,128]{1,0:T(8,128)(2,1)S(1)}, u32[]{:S(2)}, u32[]{:S(2)}) collective-permute-start(bf16[344,128]{1,0:T(8,128)(2,1)S(1)} %get-tuple-element.40), channel_id=1, source_target_pairs={{0,64},{16,80},{32,96},{48,112},{64,0},{80,16},{96,32},{112,48},{1... | collective-permute-start | bytes 264200 | tf_op jit(solution)/shard_map/ppermute | solution.py:24
  42.8 0.6 collective-permute-done.15
  43.4 3.2 %collective-permute-start.17 = (bf16[344,128]{1,0:T(8,128)(2,1)S(1)}, bf16[344,128]{1,0:T(8,128)(2,1)S(1)}, u32[]{:S(2)}, u32[]{:S(2)}) collective-permute-start(bf16[344,128]{1,0:T(8,128)(2,1)S(1)} %get-tuple-element.51), channel_id=1, source_target_pairs={{0,16},{16,0},{32,48},{48,32},{64,80},{80,64},{96,112},{112,96},{1... | collective-permute-start | bytes 264200 | tf_op jit(solution)/shard_map/ppermute | solution.py:24
  46.6 1.7 %collective-permute-done.12 = bf16[344,128]{1,0:T(8,128)(2,1)S(1)} collective-permute-done((bf16[344,128]{1,0:T(8,128)(2,1)S(1)}, bf16[344,128]{1,0:T(8,128)(2,1)S(1)}, u32[]{:S(2)}, u32[]{:S(2)}) %collective-permute-start.12) | collective-permute-done | bytes 88096 | tf_op jit(solution)/shard_map/ppermute | solution.py:24
  48.3 3.2 %collective-permute-start.16 = (bf16[344,128]{1,0:T(8,128)(2,1)S(1)}, bf16[344,128]{1,0:T(8,128)(2,1)S(1)}, u32[]{:S(2)}, u32[]{:S(2)}) collective-permute-start(bf16[344,128]{1,0:T(8,128)(2,1)S(1)} %get-tuple-element.53), channel_id=1, source_target_pairs={{0,16},{16,0},{32,48},{48,32},{64,80},{80,64},{96,112},{112,96},{1... | collective-permute-start | bytes 264200 | tf_op jit(solution)/shard_map/ppermute | solution.py:24
  51.6 2.9 %collective-permute-done.16.refs_2_ = bf16[344,128]{1,0:T(8,128)(2,1)S(1)} collective-permute-done((bf16[344,128]{1,0:T(8,128)(2,1)S(1)}, bf16[344,128]{1,0:T(8,128)(2,1)S(1)}, u32[]{:S(2)}, u32[]{:S(2)}) %collective-permute-start.16) | collective-permute-done | bytes 88096 | tf_op jit(solution)/shard_map/ppermute | solution.py:24
  54.4 1.1 %adam.1 = (bf16[2,344,128]{2,1,0:T(8,128)(2,1)S(1)}, f32[344,1,128]{2,1,0:T(1,128)}, f32[344,1,128]{2,1,0:T(1,128)}) custom-call(f32[344,128]{1,0:T(8,128)S(1)} %get-tuple-element.54.refs_0_, f32[344,128]{1,0:T(8,128)S(1)} %get-tuple-element.52.refs_1_, bf16[344,128]{1,0:T(8,128)(2,1)S(1)} %collective-permute-done.16.refs_2_, ...), custom_call_target="tpu_custom_call" | custom-call | tf_op jit(solution)/shard_map/adam/pallas_call | solution.py:208
  55.5 0.9 %collective-permute-start.19 = (bf16[2,344,128]{2,1,0:T(8,128)(2,1)S(1)}, bf16[2,344,128]{2,1,0:T(8,128)(2,1)S(1)}, u32[]{:S(2)}, u32[]{:S(2)}) collective-permute-start(bf16[2,344,128]{2,1,0:T(8,128)(2,1)S(1)} %get-tuple-element.47.refs_0_), channel_id=1, source_target_pairs={{0,96},{16,112},{32,64},{48,80},{64,32},{80,48},{96,0},{112,16},{1... | collective-permute-start | bytes 528392 | tf_op jit(solution)/shard_map/ppermute | solution.py:24
  56.4 3.2 %collective-permute-start.18 = (bf16[2,344,128]{2,1,0:T(8,128)(2,1)S(1)}, bf16[2,344,128]{2,1,0:T(8,128)(2,1)S(1)}, u32[]{:S(2)}, u32[]{:S(2)}) collective-permute-start(bf16[2,344,128]{2,1,0:T(8,128)(2,1)S(1)} %get-tuple-element.47.refs_0_), channel_id=1, source_target_pairs={{0,64},{16,80},{32,96},{48,112},{64,0},{80,16},{96,32},{112,48},{1... | collective-permute-start | bytes 528392 | tf_op jit(solution)/shard_map/ppermute | solution.py:24
  59.6 1.6 %collective-permute-done.20.refs_1_ = bf16[2,344,128]{2,1,0:T(8,128)(2,1)S(1)} collective-permute-done((bf16[2,344,128]{2,1,0:T(8,128)(2,1)S(1)}, bf16[2,344,128]{2,1,0:T(8,128)(2,1)S(1)}, u32[]{:S(2)}, u32[]{:S(2)}) %collective-permute-start.20) | collective-permute-done | bytes 176160 | tf_op jit(solution)/shard_map/ppermute | solution.py:24
  61.2 1.9 %update.2.refs_3_ = bf16[2,1376,1024]{2,1,0:T(8,128)(2,1)} custom-call(bf16[2,344,128]{2,1,0:T(8,128)(2,1)S(1)} %get-tuple-element.47.refs_0_, bf16[2,344,128]{2,1,0:T(8,128)(2,1)S(1)} %collective-permute-done.20.refs_1_, bf16[2,128,1024]{2,1,0:T(8,128)(2,1)S(1)} %bitcast.19), custom_call_target="tpu_custom_call" | custom-call | flops 360710144 | bytes 2818048 | tf_op jit(solution)/shard_map/update/pallas_call | solution.py:253
  63.1 1.3 %collective-permute-done.19.refs_1_ = bf16[2,344,128]{2,1,0:T(8,128)(2,1)S(1)} collective-permute-done((bf16[2,344,128]{2,1,0:T(8,128)(2,1)S(1)}, bf16[2,344,128]{2,1,0:T(8,128)(2,1)S(1)}, u32[]{:S(2)}, u32[]{:S(2)}) %collective-permute-start.19) | collective-permute-done | bytes 176160 | tf_op jit(solution)/shard_map/ppermute | solution.py:24
  64.4 2.0 %update.3 = bf16[2,1376,1024]{2,1,0:T(8,128)(2,1)} custom-call(bf16[2,344,128]{2,1,0:T(8,128)(2,1)S(1)} %collective-permute-done.18.refs_0_, bf16[2,344,128]{2,1,0:T(8,128)(2,1)S(1)} %collective-permute-done.19.refs_1_, bf16[2,128,1024]{2,1,0:T(8,128)(2,1)S(1)} %bitcast.20, bf16[2,1376,1024]{2,1,0:T(8,128)(2,1)} %update.2.refs_3_), custom_call_target="tpu_custom_call", output_to_operand_aliasing={{}: (3, {})} | custom-call | flops 360710144 | bytes 2818048 | tf_op jit(solution)/shard_map/update/pallas_call | solution.py:253
  (33 shorter events, 2.0 us)
Async XLA Ops:
  0.6 2.3 %copy-start.1 = (f32[2,128,1,172]{1,2,3,0:T(1,128)S(1)}, f32[2,128,1,172]{1,2,3,0:T(1,128)}, u32[]{:S(2)}) copy-start(f32[2,128,1,172]{1,2,3,0:T(1,128)} %param.9) | copy-start | bytes 528388
  0.6 2.2 %copy-start = (f32[2,128,1,172]{1,2,3,0:T(1,128)S(1)}, f32[2,128,1,172]{1,2,3,0:T(1,128)}, u32[]{:S(2)}) copy-start(f32[2,128,1,172]{1,2,3,0:T(1,128)} %param.8) | copy-start | bytes 528388
  2.8 4.2 %collective-permute-start = (bf16[768,256]{1,0:T(8,128)(2,1)S(1)}, bf16[768,256]{1,0:T(8,128)(2,1)S(1)}, u32[]{:S(2)}, u32[]{:S(2)}) collective-permute-start(bf16[768,256]{1,0:T(8,128)(2,1)S(1)} %get-tuple-element.29), channel_id=1, source_target_pairs={{0,1},{1,0},{2,3},{3,2},{4,5},{5,4},{6,7},{7,6},{8,9},{9,8},{10,11... | collective-permute-start | bytes 1179656 | tf_op jit(solution)/shard_map/ppermute | solution.py:24
  2.9 14.0 %collective-permute-start.4 = (f32[688,128]{1,0:T(8,128)S(1)}, f32[688,128]{1,0:T(8,128)S(1)}, u32[]{:S(2)}, u32[]{:S(2)}) collective-permute-start(f32[688,128]{1,0:T(8,128)S(1)} %constant_dynamic-update-slice_fusion.refs_4_), channel_id=1, source_target_pairs={{0,16},{16,0},{32,48},{48,32},{64,80},{80,64},{96,112},{112,96},{1... | collective-permute-start | bytes 1056776 | tf_op jit(solution)/shard_map/ppermute | solution.py:24
  7.0 5.6 %collective-permute-start.1 = (bf16[192,256]{1,0:T(8,128)(2,1)S(1)}, bf16[192,256]{1,0:T(8,128)(2,1)S(1)}, u32[]{:S(2)}, u32[]{:S(2)}) collective-permute-start(bf16[192,256]{1,0:T(8,128)(2,1)S(1)} %get-tuple-element.57), channel_id=1, source_target_pairs={{0,2},{1,3},{2,0},{3,1},{4,6},{5,7},{6,4},{7,5},{8,10},{9,11},{10,... | collective-permute-start | bytes 294920 | tf_op jit(solution)/shard_map/ppermute | solution.py:24
  8.6 6.4 %collective-permute-start.3 = (bf16[192,256]{1,0:T(8,128)(2,1)S(1)}, bf16[192,256]{1,0:T(8,128)(2,1)S(1)}, u32[]{:S(2)}, u32[]{:S(2)}) collective-permute-start(bf16[192,256]{1,0:T(8,128)(2,1)S(1)} %get-tuple-element.58), channel_id=1, source_target_pairs={{0,6},{1,7},{2,4},{3,5},{4,2},{5,3},{6,0},{7,1},{8,14},{9,15},{10,... | collective-permute-start | bytes 294920 | tf_op jit(solution)/shard_map/ppermute | solution.py:24
  10.7 6.1 %collective-permute-start.2 = (bf16[192,256]{1,0:T(8,128)(2,1)S(1)}, bf16[192,256]{1,0:T(8,128)(2,1)S(1)}, u32[]{:S(2)}, u32[]{:S(2)}) collective-permute-start(bf16[192,256]{1,0:T(8,128)(2,1)S(1)} %get-tuple-element.59), channel_id=1, source_target_pairs={{0,4},{1,5},{2,6},{3,7},{4,0},{5,1},{6,2},{7,3},{8,12},{9,13},{10,... | collective-permute-start | bytes 294920 | tf_op jit(solution)/shard_map/ppermute | solution.py:24
  16.9 4.7 %collective-permute-start.5 = (bf16[192,256]{1,0:T(8,128)(2,1)S(1)}, bf16[192,256]{1,0:T(8,128)(2,1)S(1)}, u32[]{:S(2)}, u32[]{:S(2)}) collective-permute-start(bf16[192,256]{1,0:T(8,128)(2,1)S(1)} %convert_element_type.73), channel_id=1, source_target_pairs={{0,8},{1,9},{2,10},{3,11},{4,12},{5,13},{6,14},{7,15},{8,0},{9,1},... | collective-permute-start | bytes 294920 | tf_op jit(solution)/shard_map/ppermute | solution.py:24
  21.6 8.0 %collective-permute-start.8 = (bf16[192,256]{1,0:T(8,128)(2,1)S(1)}, bf16[192,256]{1,0:T(8,128)(2,1)S(1)}, u32[]{:S(2)}, u32[]{:S(2)}) collective-permute-start(bf16[192,256]{1,0:T(8,128)(2,1)S(1)} %add_convert_fusion), channel_id=1, source_target_pairs={{0,6},{1,7},{2,4},{3,5},{4,2},{5,3},{6,0},{7,1},{8,14},{9,15},{10,... | collective-permute-start | bytes 294920 | tf_op jit(solution)/shard_map/ppermute | solution.py:24
  23.5 6.1 %collective-permute-start.7 = (bf16[192,256]{1,0:T(8,128)(2,1)S(1)}, bf16[192,256]{1,0:T(8,128)(2,1)S(1)}, u32[]{:S(2)}, u32[]{:S(2)}) collective-permute-start(bf16[192,256]{1,0:T(8,128)(2,1)S(1)} %add_convert_fusion), channel_id=1, source_target_pairs={{0,4},{1,5},{2,6},{3,7},{4,0},{5,1},{6,2},{7,3},{8,12},{9,13},{10,... | collective-permute-start | bytes 294920 | tf_op jit(solution)/shard_map/ppermute | solution.py:24
  24.4 5.3 %collective-permute-start.6 = (bf16[192,256]{1,0:T(8,128)(2,1)S(1)}, bf16[192,256]{1,0:T(8,128)(2,1)S(1)}, u32[]{:S(2)}, u32[]{:S(2)}) collective-permute-start(bf16[192,256]{1,0:T(8,128)(2,1)S(1)} %add_convert_fusion), channel_id=1, source_target_pairs={{0,2},{1,3},{2,0},{3,1},{4,6},{5,7},{6,4},{7,5},{8,10},{9,11},{10,... | collective-permute-start | bytes 294920 | tf_op jit(solution)/shard_map/ppermute | solution.py:24
  29.7 1.8 %collective-permute-start.9 = (bf16[768,256]{1,0:T(8,128)(2,1)S(1)}, bf16[768,256]{1,0:T(8,128)(2,1)S(1)}, u32[]{:S(2)}, u32[]{:S(2)}) collective-permute-start(bf16[768,256]{1,0:T(8,128)(2,1)S(1)} %pad_maximum_fusion.part_ref), channel_id=1, source_target_pairs={{0,1},{1,0},{2,3},{3,2},{4,5},{5,4},{6,7},{7,6},{8,9},{9,8},{10,11... | collective-permute-start | bytes 1179656 | tf_op jit(solution)/shard_map/ppermute | solution.py:24
  32.3 10.2 %collective-permute-start.13 = (bf16[344,128]{1,0:T(8,128)(2,1)S(1)}, bf16[344,128]{1,0:T(8,128)(2,1)S(1)}, u32[]{:S(2)}, u32[]{:S(2)}) collective-permute-start(bf16[344,128]{1,0:T(8,128)(2,1)S(1)} %get-tuple-element.43), channel_id=1, source_target_pairs={{0,32},{16,48},{32,0},{48,16},{64,96},{80,112},{96,64},{112,80},{1... | collective-permute-start | bytes 264200 | tf_op jit(solution)/shard_map/ppermute | solution.py:24
  34.0 8.7 %collective-permute-start.14 = (bf16[344,128]{1,0:T(8,128)(2,1)S(1)}, bf16[344,128]{1,0:T(8,128)(2,1)S(1)}, u32[]{:S(2)}, u32[]{:S(2)}) collective-permute-start(bf16[344,128]{1,0:T(8,128)(2,1)S(1)} %get-tuple-element.44), channel_id=1, source_target_pairs={{0,64},{16,80},{32,96},{48,112},{64,0},{80,16},{96,32},{112,48},{1... | collective-permute-start | bytes 264200 | tf_op jit(solution)/shard_map/ppermute | solution.py:24
  36.9 6.4 %collective-permute-start.15 = (bf16[344,128]{1,0:T(8,128)(2,1)S(1)}, bf16[344,128]{1,0:T(8,128)(2,1)S(1)}, u32[]{:S(2)}, u32[]{:S(2)}) collective-permute-start(bf16[344,128]{1,0:T(8,128)(2,1)S(1)} %get-tuple-element.45), channel_id=1, source_target_pairs={{0,96},{16,112},{32,64},{48,80},{64,32},{80,48},{96,0},{112,16},{1... | collective-permute-start | bytes 264200 | tf_op jit(solution)/shard_map/ppermute | solution.py:24
  38.0 8.6 %collective-permute-start.10 = (bf16[344,128]{1,0:T(8,128)(2,1)S(1)}, bf16[344,128]{1,0:T(8,128)(2,1)S(1)}, u32[]{:S(2)}, u32[]{:S(2)}) collective-permute-start(bf16[344,128]{1,0:T(8,128)(2,1)S(1)} %get-tuple-element.39), channel_id=1, source_target_pairs={{0,32},{16,48},{32,0},{48,16},{64,96},{80,112},{96,64},{112,80},{1... | collective-permute-start | bytes 264200 | tf_op jit(solution)/shard_map/ppermute | solution.py:24
  38.4 8.2 %collective-permute-start.11 = (bf16[344,128]{1,0:T(8,128)(2,1)S(1)}, bf16[344,128]{1,0:T(8,128)(2,1)S(1)}, u32[]{:S(2)}, u32[]{:S(2)}) collective-permute-start(bf16[344,128]{1,0:T(8,128)(2,1)S(1)} %get-tuple-element.40), channel_id=1, source_target_pairs={{0,64},{16,80},{32,96},{48,112},{64,0},{80,16},{96,32},{112,48},{1... | collective-permute-start | bytes 264200 | tf_op jit(solution)/shard_map/ppermute | solution.py:24
  42.6 5.7 %collective-permute-start.12 = (bf16[344,128]{1,0:T(8,128)(2,1)S(1)}, bf16[344,128]{1,0:T(8,128)(2,1)S(1)}, u32[]{:S(2)}, u32[]{:S(2)}) collective-permute-start(bf16[344,128]{1,0:T(8,128)(2,1)S(1)} %get-tuple-element.41), channel_id=1, source_target_pairs={{0,96},{16,112},{32,64},{48,80},{64,32},{80,48},{96,0},{112,16},{1... | collective-permute-start | bytes 264200 | tf_op jit(solution)/shard_map/ppermute | solution.py:24
  43.4 8.2 %collective-permute-start.17 = (bf16[344,128]{1,0:T(8,128)(2,1)S(1)}, bf16[344,128]{1,0:T(8,128)(2,1)S(1)}, u32[]{:S(2)}, u32[]{:S(2)}) collective-permute-start(bf16[344,128]{1,0:T(8,128)(2,1)S(1)} %get-tuple-element.51), channel_id=1, source_target_pairs={{0,16},{16,0},{32,48},{48,32},{64,80},{80,64},{96,112},{112,96},{1... | collective-permute-start | bytes 264200 | tf_op jit(solution)/shard_map/ppermute | solution.py:24
  48.3 6.1 %collective-permute-start.16 = (bf16[344,128]{1,0:T(8,128)(2,1)S(1)}, bf16[344,128]{1,0:T(8,128)(2,1)S(1)}, u32[]{:S(2)}, u32[]{:S(2)}) collective-permute-start(bf16[344,128]{1,0:T(8,128)(2,1)S(1)} %get-tuple-element.53), channel_id=1, source_target_pairs={{0,16},{16,0},{32,48},{48,32},{64,80},{80,64},{96,112},{112,96},{1... | collective-permute-start | bytes 264200 | tf_op jit(solution)/shard_map/ppermute | solution.py:24
  55.5 5.7 %collective-permute-start.20 = (bf16[2,344,128]{2,1,0:T(8,128)(2,1)S(1)}, bf16[2,344,128]{2,1,0:T(8,128)(2,1)S(1)}, u32[]{:S(2)}, u32[]{:S(2)}) collective-permute-start(bf16[2,344,128]{2,1,0:T(8,128)(2,1)S(1)} %get-tuple-element.47.refs_0_), channel_id=1, source_target_pairs={{0,32},{16,48},{32,0},{48,16},{64,96},{80,112},{96,64},{112,80},{1... | collective-permute-start | bytes 528392 | tf_op jit(solution)/shard_map/ppermute | solution.py:24
  55.5 8.9 %collective-permute-start.19 = (bf16[2,344,128]{2,1,0:T(8,128)(2,1)S(1)}, bf16[2,344,128]{2,1,0:T(8,128)(2,1)S(1)}, u32[]{:S(2)}, u32[]{:S(2)}) collective-permute-start(bf16[2,344,128]{2,1,0:T(8,128)(2,1)S(1)} %get-tuple-element.47.refs_0_), channel_id=1, source_target_pairs={{0,96},{16,112},{32,64},{48,80},{64,32},{80,48},{96,0},{112,16},{1... | collective-permute-start | bytes 528392 | tf_op jit(solution)/shard_map/ppermute | solution.py:24
  56.4 8.0 %collective-permute-start.18 = (bf16[2,344,128]{2,1,0:T(8,128)(2,1)S(1)}, bf16[2,344,128]{2,1,0:T(8,128)(2,1)S(1)}, u32[]{:S(2)}, u32[]{:S(2)}) collective-permute-start(bf16[2,344,128]{2,1,0:T(8,128)(2,1)S(1)} %get-tuple-element.47.refs_0_), channel_id=1, source_target_pairs={{0,64},{16,80},{32,96},{48,112},{64,0},{80,16},{96,32},{112,48},{1... | collective-permute-start | bytes 528392 | tf_op jit(solution)/shard_map/ppermute | solution.py:24

commit v3 on v2

--- a/solution.py
+++ b/solution.py
@@ -14,6 +14,10 @@
 corr_two = 1.0 - beta_two**STEP
 
 NX, NY = 4, 4
+ORDER = (2, 1, 3)
+STAGE_MIB = 48
+AG_X, AG_Y = (2, 1, 3), (2, 1, 3)
+PIECES = (0, 1, 3, 2)
 
 F32, BF16 = jnp.float32, jnp.bfloat16
 HBM = pl.BlockSpec(memory_space=pltpu.HBM)
@@ -112,14 +116,33 @@
     )(inputs, basis)
 
 
+def stage_kernel(g, src_ref, dst_ref, sem):
+    copy = pltpu.make_async_copy(src_ref.at[g], dst_ref, sem)
+    copy.start()
+    copy.wait()
+
+
+def stage(stack, g):
+    return pl.pallas_call(
+        lambda *refs: stage_kernel(g, *refs),
+        in_specs=[HBM],
+        out_specs=VMEM,
+        out_shape=jax.ShapeDtypeStruct(stack.shape[1:], stack.dtype),
+        scratch_shapes=[pltpu.SemaphoreType.DMA],
+        compiler_params=params(STAGE_MIB),
+        cost_estimate=cost(0, 2 * 2 * stack.shape[1] * stack.shape[2]),
+        name="stage",
+    )(stack)
+
+
 def half_product(at, core, part_ref, grad_ref, proj, g):
     half = part_ref.shape[0]
     piece = half // NX
     rank = proj.shape[1]
-    for k in range(NX):
+    for i, k in enumerate(PIECES):
         to = pl.multiple_of((at["x"] ^ k) * piece, piece)
         proj[pl.ds(to, piece), :] = part_ref[
-            k * piece : (k + 1) * piece, g * rank : (g + 1) * rank
+            i * piece : (i + 1) * piece, g * rank : (g + 1) * rank
         ]
     tokens = pl.ds(pl.multiple_of(core * half, half), half)
     return jnp.dot(grad_ref[:, tokens], proj[...], preferred_element_type=F32)
@@ -179,7 +202,7 @@
 
 def adam_kernel(n_g, *refs):
     owns, gots = refs[:n_g], refs[n_g : 2 * n_g]
-    near_ref, far_ref, norm_ref, new_first_ref, new_second_ref = refs[2 * n_g :]
+    near_ref, far_ref, norm_ref = refs[2 * n_g :]
     low = place()["z"] == 0
     half = owns[0].shape[0] // 2
     for g in range(n_g):
@@ -197,9 +220,6 @@
         norm_ref[g] = (
             new_first / corr_one / (jnp.sqrt(new_second / corr_two) + epsilon)
         ).astype(BF16)
-        rows = slice(g * half, (g + 1) * half)
-        new_first_ref[rows, 0, :] = jnp.where(low, new_first[:half], new_first[half:])
-        new_second_ref[rows, 0, :] = jnp.where(low, new_second[:half], new_second[half:])
 
 
 def adam(owns, gots, moments, far_moments):
@@ -208,38 +228,69 @@
     return pl.pallas_call(
         lambda *refs: adam_kernel(n_g, *refs),
         in_specs=[VMEM] * (2 * n_g + 2),
-        out_specs=[VMEM] * 3,
-        out_shape=[jax.ShapeDtypeStruct((n_g, share, rank), BF16)]
-        + [jax.ShapeDtypeStruct((n_g * share // 2, 1, rank), F32)] * 2,
+        out_specs=VMEM,
+        out_shape=jax.ShapeDtypeStruct((n_g, share, rank), BF16),
         compiler_params=params(8),
         name="adam",
     )(*owns, *gots, moments, far_moments)
 
 
-BLOCK = 352
-
-
-def update_kernel(first_half, even_ref, odd_ref, basis_ref, *refs):
+def moments_kernel(n_g, *refs):
+    owns, gots = refs[:n_g], refs[n_g : 2 * n_g]
+    near_ref, new_first_ref, new_second_ref = refs[2 * n_g :]
+    low = place()["z"] == 0
+    half = owns[0].shape[0] // 2
+    for g in range(n_g):
+        grad = owns[g][...] + gots[g][...].astype(F32)
+        grad = jnp.where(low, grad[:half], grad[half:])
+        rows = slice(g * half, (g + 1) * half)
+        first = near_ref[rows, :]
+        second = near_ref[slice((n_g + g) * half, (n_g + g + 1) * half), :]
+        new_first_ref[rows, 0, :] = beta_one * first + (1.0 - beta_one) * grad
+        new_second_ref[rows, 0, :] = beta_two * second + (1.0 - beta_two) * grad * grad
+
+
+def new_moments(owns, gots, moments):
+    n_g = len(owns)
+    share, rank = owns[0].shape
+    return pl.pallas_call(
+        lambda *refs: moments_kernel(n_g, *refs),
+        in_specs=[VMEM] * (2 * n_g + 1),
+        out_specs=[VMEM] * 2,
+        out_shape=[jax.ShapeDtypeStruct((n_g * share // 2, 1, rank), F32)] * 2,
+        compiler_params=params(8),
+        name="new_moments",
+    )(*owns, *gots, moments)
+
+
+FIRST, REST = 336, 352
+
+
+def update_kernel(windows, n, *refs):
+    pieces, basis_ref = refs[:n], refs[n]
     out_ref, wide, norm, block, sem = refs[-5:]
     y = place()["y"]
-    pair = y >> 1 if first_half else 1 - (y >> 1)
-    n_g, share, _ = even_ref.shape
-    rows = 2 * share
+    n_g, share, _ = pieces[0].shape
     copies = []
-    for g in range(n_g):
-        for ref, parity in ((even_ref, y & 1), (odd_ref, 1 - (y & 1))):
-            wide[g, pl.ds(pl.multiple_of(parity * share, 8), share), :] = ref[g].astype(F32)
-        norm[g] = wide[g].astype(BF16)
-        for i, start in enumerate(range(0, rows, BLOCK)):
-            size = min(BLOCK, rows - start)
-            block[g, start : start + size, :] = jnp.dot(
-                norm[g, start : start + size, :], basis_ref[g], preferred_element_type=F32
+    for w, (own_pair, which) in enumerate(windows):
+        pair = y >> 1 if own_pair else 1 - (y >> 1)
+        parity = y & 1
+        size = FIRST if len(which) == 1 else REST
+        start = parity * REST if len(which) == 1 else (1 - parity) * FIRST
+        for g in range(n_g):
+            for i, at in zip(which, (parity, 1 - parity)):
+                to = pl.ds(pl.multiple_of(at * share, 8), share)
+                wide[w, g, to, :] = pieces[i][g].astype(F32)
+            norm[w, g, :size, :] = wide[
+                w, g, pl.ds(pl.multiple_of(start, 16), size), :
+            ].astype(BF16)
+            block[w, g, :size, :] = jnp.dot(
+                norm[w, g, :size, :], basis_ref[g], preferred_element_type=F32
             ).astype(BF16)
+            to = pl.ds(pl.multiple_of(pair * (2 * share) + start, 16), size)
             copies.append(
                 pltpu.make_async_copy(
-                    block.at[g, start : start + size, :],
-                    out_ref.at[g, pl.ds(pl.multiple_of(pair * rows + start, 16), size), :],
-                    sem.at[g, i],
+                    block.at[w, g, :size, :], out_ref.at[g, to, :], sem.at[w, g]
                 )
             )
             copies[-1].start()
@@ -247,25 +298,28 @@
         copy.wait()
 
 
-def update(even, odd, basis_t, out):
-    n_g, share, rank = even.shape
+def update(windows, pieces, basis_t, out):
+    n, n_w = len(pieces), len(windows)
+    n_g, share, rank = pieces[0].shape
     weight_rows = basis_t.shape[2]
     return pl.pallas_call(
-        lambda *refs: update_kernel(out is None, *refs),
-        in_specs=[VMEM] * 3 + ([HBM] if out is not None else []),
+        lambda *refs: update_kernel(windows, n, *refs),
+        in_specs=[VMEM] * (n + 1) + ([HBM] if out is not None else []),
         out_specs=HBM,
         out_shape=jax.ShapeDtypeStruct((n_g, share * NY, weight_rows), BF16),
         scratch_shapes=[
-            pltpu.VMEM((n_g, 2 * share, rank), F32),
-            pltpu.VMEM((n_g, 2 * share, rank), BF16),
-            pltpu.VMEM((n_g, 2 * share, weight_rows), BF16),
-            pltpu.SemaphoreType.DMA((n_g, pl.cdiv(2 * share, BLOCK))),
+            pltpu.VMEM((n_w, n_g, 2 * share, rank), F32),
+            pltpu.VMEM((n_w, n_g, REST, rank), BF16),
+            pltpu.VMEM((n_w, n_g, REST, weight_rows), BF16),
+            pltpu.SemaphoreType.DMA((n_w, n_g)),
         ],
-        input_output_aliases={} if out is None else {3: 0},
+        input_output_aliases={} if out is None else {n + 1: 0},
         compiler_params=params(12),
-        cost_estimate=cost(4 * n_g * share * rank * weight_rows, 4 * n_g * share * weight_rows),
+        cost_estimate=cost(
+            2 * n_w * n_g * REST * rank * weight_rows, 2 * n_w * n_g * REST * weight_rows
+        ),
         name="update",
-    )(even, odd, basis_t, *([] if out is None else [out]))
+    )(*pieces, basis_t, *([] if out is None else [out]))
 
 
 def body(inputs, grad_out, basis, first_moment, second_moment):
@@ -284,18 +338,28 @@
     )
     moments = jnp.concatenate([first, second], axis=0)
     got = to_core(send)
-    far_moments = to_zhi(moments)
     part = lambda v, k: v[k * piece : (k + 1) * piece].astype(F32)
     sums = [part(own, k) + part(got, k) for k in range(NX)]
+    sums[0], grad_a = lax.optimization_barrier((sums[0], grad_t))
     total = sums[0]
-    for k in range(1, NX):
+    for k in ORDER:
         total = total + to_x(sums[k].astype(BF16), k).astype(F32)
-    total, far_moments, row_basis_t = lax.optimization_barrier(
-        (total, far_moments, row_basis_t)
-    )
-    total = (total + to_zlo(total.astype(BF16)).astype(F32)).astype(BF16)
-    near_part = jnp.concatenate([total] + [to_x(total, k) for k in range(1, NX)], axis=0)
-    near_part, *grads = lax.optimization_barrier((near_part, *(grad_t[g] for g in range(n_g))))
+    grads = [stage(grad_a, 0)]
+    total, moments, row_basis_t, grads[0] = lax.optimization_barrier(
+        (total, moments, row_basis_t, grads[0])
+    )
+    got = to_zlo(total.astype(BF16))
+    far_moments = to_zhi(moments)
+    total = (total + got.astype(F32)).astype(BF16)
+    total, grad_b = lax.optimization_barrier((total, grad_t))
+    parts = {0: total}
+    for k in AG_X:
+        parts[k] = to_x(total, k)
+    near_part = jnp.concatenate([parts[k] for k in PIECES], axis=0)
+    near_part, grad, far_moments = lax.optimization_barrier(
+        (near_part, stage(grad_b, 1), far_moments)
+    )
+    grads.append(grad)
     far_part = to_core(near_part)
     near = rank_near(near_part, grads, rank)
     far_part, near = lax.optimization_barrier((far_part, near))
@@ -303,14 +367,21 @@
     owns, gots = [], []
     for g in range(n_g):
         own, *others = rank_far(far_part, near, grads[g], g)
-        for k in range(1, NY):
+        for k in ORDER:
             own = own + to_y(others[k - 1], k).astype(F32)
         owns.append(own)
         gots.append(to_zhi(own.astype(BF16)))
-    norm, new_first, new_second = adam(owns, gots, moments, far_moments)
-    pieces = [norm] + [to_y(norm, k) for k in range(1, NY)]
-    out = update(pieces[0], pieces[1], row_basis_t, None)
-    out = update(pieces[2], pieces[3], row_basis_t, out)
+    norm = adam(owns, gots, moments, far_moments)
+    pieces = {k: to_y(norm, k) for k in AG_Y}
+    out = update([(True, (0,))], [norm], row_basis_t, None)
+    new_first, new_second = new_moments(owns, gots, moments)
+    out = update([(False, (0,))], [pieces[2]], row_basis_t, out)
+    out = update(
+        [(True, (0, 1)), (False, (2, 3))],
+        [norm, pieces[1], pieces[2], pieces[3]],
+        row_basis_t,
+        out,
+    )
 
     def shaped(m):
         return jnp.transpose(m.reshape(n_g, -1, 1, rank), (0, 3, 2, 1))

time: 66.5 us -> 64.1 us (0.964); the launches traced: 66.4 us -> 63.3 us
  Pallas kernels: 10.1 us -> 15.7 us
  waiting for transfers between devices: 16.2 us -> 10.8 us
  local copies, waits for them, and re-layouts: 5.1 us -> 1.32 us
    pallas_call x2 -> x6, Pallas kernels: 3.9 us -> 10.3 us  [the longest x3 4.93 us: update(): pl.pallas_call(lambda *refs: update_kernel(windows, n, *refs), in_specs=[...]
    ppermute x21, waiting for transfers between devices: 16.2 us -> 10.8 us  [swap(): return lax.ppermute(v, axis, [(i, i ^ bits) for i in range(size)])]
    squeeze x1 -> x0, local copies, waits for them, and re-layouts: 3.78 us -> none  [body(): grad_t[g]]
    pallas_call x1, Pallas kernels: 1.07 us -> 0.32 us  [adam(): pl.pallas_call(lambda *refs: adam_kernel(n_g, *refs), in_specs=[VMEM] * (...]
  transfers between devices with their start and end apart: 21 -> 21, of which waited for: 10 -> 11; matrix products, arithmetic and copies ran while one was open for 8% -> 2% of each run, Pallas kernels for 6% -> 17%
where the time goes in v3:
time: 64.1 us; the launch traced here: 63.3 us
  starting transfers between devices  34.2 us (53%)
  Pallas kernels  15.7 us (24%)
  waiting for transfers between devices  10.8 us (17%)
  local copies, waits for them, and re-layouts  1.32 us (2%)
  between operations  0.8 us (1%)
    ppermute x21, starting transfers between devices, swap(): return lax.ppermute(v, axis, [(i, i ^ bits) for i in range(size)])  34.2 us
    ppermute x21, waiting for transfers between devices, swap(): return lax.ppermute(v, axis, [(i, i ^ bits) for i in range(size)])  10.8 us
    pallas_call x3, Pallas kernels, update(): pl.pallas_call(lambda *refs: update_kernel(windows, n, *refs), in_specs=[...  4.93 us
    pallas_call x2, Pallas kernels, stage(): pl.pallas_call(lambda *refs: stage_kernel(g, *refs), in_specs=[HBM], out_...  4.41 us
    pallas_call x1, Pallas kernels, project(): pl.pallas_call(project_kernel, in_specs=[HBM] * 2, out_specs=[VMEM] * 2,...  2.1 us
    pallas_call x2, Pallas kernels, rank_far(): pl.pallas_call(lambda *refs: far_kernel(g, *refs), in_specs=[VMEM] * 3, o...  1.71 us
    pallas_call x1, Pallas kernels, rank_near(): pl.pallas_call(near_kernel, in_specs=[VMEM] * (1 + n_g), out_specs=VMEM,...  1.33 us
  transfers between devices with their start and end apart: 21, of which 11 were waited for; matrix products, arithmetic and copies ran while one was open for 2% of the time, Pallas kernels for 17%

profile of v3, /device:TPU:0, one launch (start us, length us, event | category | flops | bytes accessed | tf_op | source)
XLA Modules:
  0.0 63.3 jit_solution(5118986731207234125)
XLA Ops:
  0.7 2.1 %project.1 = (bf16[768,256]{1,0:T(8,128)(2,1)S(1)}, f32[768,256]{1,0:T(8,128)S(1)}) custom-call(bf16[1536,512]{1,0:T(8,128)(2,1)} %inputs_ref.1, bf16[2,8192,128]{2,1,0:T(8,128)(2,1)} %basis_ref.1), custom_call_target="tpu_custom_call" | custom-call | flops 402653184 | bytes 1572864 | tf_op jit(solution)/shard_map/project/pallas_call | solution.py:99
  2.9 1.1 %constant_dynamic-slice_fusion = bf16[2,1024,128]{2,1,0:T(8,128)(2,1)S(1)} fusion(bf16[2,8192,128]{2,1,0:T(8,128)(2,1)} %basis_ref.1, s32[]{:T(128)S(6)} %select_n.3), kind=kLoop, calls=%fused_computation.10 | loop fusion | bytes 1048580 | tf_op jit(solution)/shard_map/dynamic_slice | solution.py:327
  4.7 3.2 %collective-permute-start.1 = (bf16[192,256]{1,0:T(8,128)(2,1)S(1)}, bf16[192,256]{1,0:T(8,128)(2,1)S(1)}, u32[]{:S(2)}, u32[]{:S(2)}) collective-permute-start(bf16[192,256]{1,0:T(8,128)(2,1)S(1)} %get-tuple-element.63), channel_id=1, source_target_pairs={{0,4},{1,5},{2,6},{3,7},{4,0},{5,1},{6,2},{7,3},{8,12},{9,13},{10,... | collective-permute-start | bytes 294920 | tf_op jit(solution)/shard_map/ppermute | solution.py:28
  7.8 1.1 %collective-permute-start.3 = (bf16[192,256]{1,0:T(8,128)(2,1)S(1)}, bf16[192,256]{1,0:T(8,128)(2,1)S(1)}, u32[]{:S(2)}, u32[]{:S(2)}) collective-permute-start(bf16[192,256]{1,0:T(8,128)(2,1)S(1)} %get-tuple-element.64), channel_id=1, source_target_pairs={{0,6},{1,7},{2,4},{3,5},{4,2},{5,3},{6,0},{7,1},{8,14},{9,15},{10,... | collective-permute-start | bytes 294920 | tf_op jit(solution)/shard_map/ppermute | solution.py:28
  9.0 2.2 %stage.2.refs_0_.refs_2_ = bf16[1376,1536]{1,0:T(8,128)(2,1)S(1)} custom-call(bf16[2,1376,1536]{2,1,0:T(8,128)(2,1)} %bitcast.19), custom_call_target="tpu_custom_call" | custom-call | bytes 8454144 | tf_op jit(solution)/shard_map/stage/pallas_call | solution.py:126
  11.2 2.4 %collective-permute-done.3 = bf16[192,256]{1,0:T(8,128)(2,1)S(1)} collective-permute-done((bf16[192,256]{1,0:T(8,128)(2,1)S(1)}, bf16[192,256]{1,0:T(8,128)(2,1)S(1)}, u32[]{:S(2)}, u32[]{:S(2)}) %collective-permute-start.3) | collective-permute-done | bytes 98336 | tf_op jit(solution)/shard_map/ppermute | solution.py:28
  13.7 2.0 %collective-permute-start.4 = (bf16[192,256]{1,0:T(8,128)(2,1)S(1)}, bf16[192,256]{1,0:T(8,128)(2,1)S(1)}, u32[]{:S(2)}, u32[]{:S(2)}) collective-permute-start(bf16[192,256]{1,0:T(8,128)(2,1)S(1)} %convert_element_type.73), channel_id=1, source_target_pairs={{0,8},{1,9},{2,10},{3,11},{4,12},{5,13},{6,14},{7,15},{8,0},{9,1},... | collective-permute-start | bytes 294920 | tf_op jit(solution)/shard_map/ppermute | solution.py:28
  15.7 3.6 %collective-permute-start.8 = (f32[688,128]{1,0:T(8,128)S(1)}, f32[688,128]{1,0:T(8,128)S(1)}, u32[]{:S(2)}, u32[]{:S(2)}) collective-permute-start(f32[688,128]{1,0:T(8,128)S(1)} %pad_maximum_fusion.1.refs_4_), channel_id=1, source_target_pairs={{0,16},{16,0},{32,48},{48,32},{64,80},{80,64},{96,112},{112,96},{1... | collective-permute-start | bytes 1056776 | tf_op jit(solution)/shard_map/ppermute | solution.py:28
  19.4 1.8 %collective-permute-start.7 = (bf16[192,256]{1,0:T(8,128)(2,1)S(1)}, bf16[192,256]{1,0:T(8,128)(2,1)S(1)}, u32[]{:S(2)}, u32[]{:S(2)}) collective-permute-start(bf16[192,256]{1,0:T(8,128)(2,1)S(1)} %add_convert_fusion), channel_id=1, source_target_pairs={{0,4},{1,5},{2,6},{3,7},{4,0},{5,1},{6,2},{7,3},{8,12},{9,13},{10,... | collective-permute-start | bytes 294920 | tf_op jit(solution)/shard_map/ppermute | solution.py:28
  21.2 2.1 %collective-permute-start.6 = (bf16[192,256]{1,0:T(8,128)(2,1)S(1)}, bf16[192,256]{1,0:T(8,128)(2,1)S(1)}, u32[]{:S(2)}, u32[]{:S(2)}) collective-permute-start(bf16[192,256]{1,0:T(8,128)(2,1)S(1)} %add_convert_fusion), channel_id=1, source_target_pairs={{0,6},{1,7},{2,4},{3,5},{4,2},{5,3},{6,0},{7,1},{8,14},{9,15},{10,... | collective-permute-start | bytes 294920 | tf_op jit(solution)/shard_map/ppermute | solution.py:28
  23.3 2.2 %stage.3.refs_1_.refs_2_ = bf16[1376,1536]{1,0:T(8,128)(2,1)S(1)} custom-call(bf16[2,1376,1536]{2,1,0:T(8,128)(2,1)} %bitcast.20), custom_call_target="tpu_custom_call" | custom-call | bytes 8454144 | tf_op jit(solution)/shard_map/stage/pallas_call | solution.py:126
  25.5 1.1 %collective-permute-done.7 = bf16[192,256]{1,0:T(8,128)(2,1)S(1)} collective-permute-done((bf16[192,256]{1,0:T(8,128)(2,1)S(1)}, bf16[192,256]{1,0:T(8,128)(2,1)S(1)}, u32[]{:S(2)}, u32[]{:S(2)}) %collective-permute-start.7) | collective-permute-done | bytes 98336 | tf_op jit(solution)/shard_map/ppermute | solution.py:28
  26.5 0.8 %collective-permute-done.6 = bf16[192,256]{1,0:T(8,128)(2,1)S(1)} collective-permute-done((bf16[192,256]{1,0:T(8,128)(2,1)S(1)}, bf16[192,256]{1,0:T(8,128)(2,1)S(1)}, u32[]{:S(2)}, u32[]{:S(2)}) %collective-permute-start.6) | collective-permute-done | bytes 98336 | tf_op jit(solution)/shard_map/ppermute | solution.py:28
  28.3 1.3 %rank_near.1.refs_1_ = f32[2,1376,128]{2,1,0:T(8,128)S(1)} custom-call(bf16[768,256]{1,0:T(8,128)(2,1)S(1)} %pad_maximum_fusion.part_ref, bf16[1376,1536]{1,0:T(8,128)(2,1)S(1)} %stage.2.refs_0_.refs_2_, bf16[1376,1536]{1,0:T(8,128)(2,1)S(1)} %stage.3.refs_1_.refs_2_), custom_call_target="tpu_custom_call" | custom-call | flops 541065216 | bytes 4194304 | tf_op jit(solution)/shard_map/rank_near/pallas_call | solution.py:161
  30.0 0.9 %rank_far.3 = (f32[344,128]{1,0:T(8,128)S(1)}, bf16[344,128]{1,0:T(8,128)(2,1)S(1)}, bf16[344,128]{1,0:T(8,128)(2,1)S(1)}, bf16[344,128]{1,0:T(8,128)(2,1)S(1)}) custom-call(bf16[768,256]{1,0:T(8,128)(2,1)S(1)} %collective-permute-done.9.refs_0_, f32[2,1376,128]{2,1,0:T(8,128)S(1)} %rank_near.1.refs_1_, bf16[1376,1536]{1,0:T(8,128)(2,1)S(1)} %stage.3.refs_1_.refs_2_), custom_call_target="tpu_custom_call" | custom-call | flops 270532608 | bytes 2097152 | tf_op jit(solution)/shard_map/rank_far/pallas_call | solution.py:190
  30.8 3.3 %collective-permute-start.13 = (bf16[344,128]{1,0:T(8,128)(2,1)S(1)}, bf16[344,128]{1,0:T(8,128)(2,1)S(1)}, u32[]{:S(2)}, u32[]{:S(2)}) collective-permute-start(bf16[344,128]{1,0:T(8,128)(2,1)S(1)} %get-tuple-element.52), channel_id=1, source_target_pairs={{0,64},{16,80},{32,96},{48,112},{64,0},{80,16},{96,32},{112,48},{1... | collective-permute-start | bytes 264200 | tf_op jit(solution)/shard_map/ppermute | solution.py:28
  35.2 0.9 %rank_far.2 = (f32[344,128]{1,0:T(8,128)S(1)}, bf16[344,128]{1,0:T(8,128)(2,1)S(1)}, bf16[344,128]{1,0:T(8,128)(2,1)S(1)}, bf16[344,128]{1,0:T(8,128)(2,1)S(1)}) custom-call(bf16[768,256]{1,0:T(8,128)(2,1)S(1)} %collective-permute-done.9.refs_0_, f32[2,1376,128]{2,1,0:T(8,128)S(1)} %rank_near.1.refs_1_, bf16[1376,1536]{1,0:T(8,128)(2,1)S(1)} %stage.2.refs_0_.refs_2_), custom_call_target="tpu_custom_call" | custom-call | flops 270532608 | bytes 2097152 | tf_op jit(solution)/shard_map/rank_far/pallas_call | solution.py:190
  36.0 3.1 %collective-permute-start.10 = (bf16[344,128]{1,0:T(8,128)(2,1)S(1)}, bf16[344,128]{1,0:T(8,128)(2,1)S(1)}, u32[]{:S(2)}, u32[]{:S(2)}) collective-permute-start(bf16[344,128]{1,0:T(8,128)(2,1)S(1)} %get-tuple-element.48), channel_id=1, source_target_pairs={{0,64},{16,80},{32,96},{48,112},{64,0},{80,16},{96,32},{112,48},{1... | collective-permute-start | bytes 264200 | tf_op jit(solution)/shard_map/ppermute | solution.py:28
  39.2 0.7 %collective-permute-start.11 = (bf16[344,128]{1,0:T(8,128)(2,1)S(1)}, bf16[344,128]{1,0:T(8,128)(2,1)S(1)}, u32[]{:S(2)}, u32[]{:S(2)}) collective-permute-start(bf16[344,128]{1,0:T(8,128)(2,1)S(1)} %get-tuple-element.49), channel_id=1, source_target_pairs={{0,32},{16,48},{32,0},{48,16},{64,96},{80,112},{96,64},{112,80},{1... | collective-permute-start | bytes 264200 | tf_op jit(solution)/shard_map/ppermute | solution.py:28
  39.9 1.0 %collective-permute-start.12 = (bf16[344,128]{1,0:T(8,128)(2,1)S(1)}, bf16[344,128]{1,0:T(8,128)(2,1)S(1)}, u32[]{:S(2)}, u32[]{:S(2)}) collective-permute-start(bf16[344,128]{1,0:T(8,128)(2,1)S(1)} %get-tuple-element.50), channel_id=1, source_target_pairs={{0,96},{16,112},{32,64},{48,80},{64,32},{80,48},{96,0},{112,16},{1... | collective-permute-start | bytes 264200 | tf_op jit(solution)/shard_map/ppermute | solution.py:28
  40.9 0.9 %collective-permute-done.15 = bf16[344,128]{1,0:T(8,128)(2,1)S(1)} collective-permute-done((bf16[344,128]{1,0:T(8,128)(2,1)S(1)}, bf16[344,128]{1,0:T(8,128)(2,1)S(1)}, u32[]{:S(2)}, u32[]{:S(2)}) %collective-permute-start.15) | collective-permute-done | bytes 88096 | tf_op jit(solution)/shard_map/ppermute | solution.py:28
  41.9 3.9 %collective-permute-start.17 = (bf16[344,128]{1,0:T(8,128)(2,1)S(1)}, bf16[344,128]{1,0:T(8,128)(2,1)S(1)}, u32[]{:S(2)}, u32[]{:S(2)}) collective-permute-start(bf16[344,128]{1,0:T(8,128)(2,1)S(1)} %get-tuple-element.59), channel_id=1, source_target_pairs={{0,16},{16,0},{32,48},{48,32},{64,80},{80,64},{96,112},{112,96},{1... | collective-permute-start | bytes 264200 | tf_op jit(solution)/shard_map/ppermute | solution.py:28
  45.8 3.7 %collective-permute-start.16 = (bf16[344,128]{1,0:T(8,128)(2,1)S(1)}, bf16[344,128]{1,0:T(8,128)(2,1)S(1)}, u32[]{:S(2)}, u32[]{:S(2)}) collective-permute-start(bf16[344,128]{1,0:T(8,128)(2,1)S(1)} %get-tuple-element.61), channel_id=1, source_target_pairs={{0,16},{16,0},{32,48},{48,32},{64,80},{80,64},{96,112},{112,96},{1... | collective-permute-start | bytes 264200 | tf_op jit(solution)/shard_map/ppermute | solution.py:28
  49.5 2.5 %collective-permute-done.16.refs_2_ = bf16[344,128]{1,0:T(8,128)(2,1)S(1)} collective-permute-done((bf16[344,128]{1,0:T(8,128)(2,1)S(1)}, bf16[344,128]{1,0:T(8,128)(2,1)S(1)}, u32[]{:S(2)}, u32[]{:S(2)}) %collective-permute-start.16) | collective-permute-done | bytes 88096 | tf_op jit(solution)/shard_map/ppermute | solution.py:28
  52.3 1.4 %collective-permute-start.19 = (bf16[2,344,128]{2,1,0:T(8,128)(2,1)S(1)}, bf16[2,344,128]{2,1,0:T(8,128)(2,1)S(1)}, u32[]{:S(2)}, u32[]{:S(2)}) collective-permute-start(bf16[2,344,128]{2,1,0:T(8,128)(2,1)S(1)} %adam.1.refs_0_), channel_id=1, source_target_pairs={{0,64},{16,80},{32,96},{48,112},{64,0},{80,16},{96,32},{112,48},{1... | collective-permute-start | bytes 528392 | tf_op jit(solution)/shard_map/ppermute | solution.py:28
  53.7 1.4 %collective-permute-start.20 = (bf16[2,344,128]{2,1,0:T(8,128)(2,1)S(1)}, bf16[2,344,128]{2,1,0:T(8,128)(2,1)S(1)}, u32[]{:S(2)}, u32[]{:S(2)}) collective-permute-start(bf16[2,344,128]{2,1,0:T(8,128)(2,1)S(1)} %adam.1.refs_0_), channel_id=1, source_target_pairs={{0,96},{16,112},{32,64},{48,80},{64,32},{80,48},{96,0},{112,16},{1... | collective-permute-start | bytes 528392 | tf_op jit(solution)/shard_map/ppermute | solution.py:28
  55.2 0.7 %collective-permute-start.18 = (bf16[2,344,128]{2,1,0:T(8,128)(2,1)S(1)}, bf16[2,344,128]{2,1,0:T(8,128)(2,1)S(1)}, u32[]{:S(2)}, u32[]{:S(2)}) collective-permute-start(bf16[2,344,128]{2,1,0:T(8,128)(2,1)S(1)} %adam.1.refs_0_), channel_id=1, source_target_pairs={{0,32},{16,48},{32,0},{48,16},{64,96},{80,112},{96,64},{112,80},{1... | collective-permute-start | bytes 528392 | tf_op jit(solution)/shard_map/ppermute | solution.py:28
  55.9 0.9 %new_moments.1 = (f32[344,1,128]{2,1,0:T(1,128)}, f32[344,1,128]{2,1,0:T(1,128)}) custom-call(f32[344,128]{1,0:T(8,128)S(1)} %get-tuple-element.62.refs_0_, f32[344,128]{1,0:T(8,128)S(1)} %get-tuple-element.60.refs_1_, bf16[344,128]{1,0:T(8,128)(2,1)S(1)} %collective-permute-done.16.refs_2_, bf16[344,128]{1,0:T(8,128)(2,1)S(1)} %collective-permute-done.17.refs_3_, ...), custom_call_target="tpu_custom_call" | custom-call | tf_op jit(solution)/shard_map/new_moments/pallas_call | solution.py:256
  56.8 1.5 %update.3.refs_2_ = bf16[2,1376,1024]{2,1,0:T(8,128)(2,1)} custom-call(bf16[2,344,128]{2,1,0:T(8,128)(2,1)S(1)} %adam.1.refs_0_, bf16[2,128,1024]{2,1,0:T(8,128)(2,1)S(1)} %bitcast.15), custom_call_target="tpu_custom_call" | custom-call | flops 184549376 | bytes 1441792 | tf_op jit(solution)/shard_map/update/pallas_call | solution.py:305
  58.3 1.1 %collective-permute-done.19.refs_0_.refs_2_ = bf16[2,344,128]{2,1,0:T(8,128)(2,1)S(1)} collective-permute-done((bf16[2,344,128]{2,1,0:T(8,128)(2,1)S(1)}, bf16[2,344,128]{2,1,0:T(8,128)(2,1)S(1)}, u32[]{:S(2)}, u32[]{:S(2)}) %collective-permute-start.19) | collective-permute-done | bytes 176160 | tf_op jit(solution)/shard_map/ppermute | solution.py:28
  59.4 1.5 %update.4.refs_5_ = bf16[2,1376,1024]{2,1,0:T(8,128)(2,1)} custom-call(bf16[2,344,128]{2,1,0:T(8,128)(2,1)S(1)} %collective-permute-done.19.refs_0_.refs_2_, bf16[2,128,1024]{2,1,0:T(8,128)(2,1)S(1)} %bitcast.16, bf16[2,1376,1024]{2,1,0:T(8,128)(2,1)} %update.3.refs_2_), custom_call_target="tpu_custom_call", output_to_operand_aliasing={{}: (2, {})} | custom-call | flops 184549376 | bytes 1441792 | tf_op jit(solution)/shard_map/update/pallas_call | solution.py:305
  61.2 2.0 %update.5 = bf16[2,1376,1024]{2,1,0:T(8,128)(2,1)} custom-call(bf16[2,344,128]{2,1,0:T(8,128)(2,1)S(1)} %adam.1.refs_0_, bf16[2,344,128]{2,1,0:T(8,128)(2,1)S(1)} %collective-permute-done.18.refs_1_, bf16[2,344,128]{2,1,0:T(8,128)(2,1)S(1)} %collective-permute-done.19.refs_0_.refs_2_, ...), custom_call_target="tpu_custom_call", output_to_operand_aliasing={{}: (5, {})} | custom-call | flops 369098752 | bytes 2883584 | tf_op jit(solution)/shard_map/update/pallas_call | solution.py:305
  (35 shorter events, 4.1 us)
Async XLA Ops:
  0.6 8.4 %copy-start = (f32[2,128,1,172]{1,2,3,0:T(1,128)S(1)}, f32[2,128,1,172]{1,2,3,0:T(1,128)}, u32[]{:S(2)}) copy-start(f32[2,128,1,172]{1,2,3,0:T(1,128)} %param.9) | copy-start | bytes 528388
  0.6 8.3 %copy-start.1 = (f32[2,128,1,172]{1,2,3,0:T(1,128)S(1)}, f32[2,128,1,172]{1,2,3,0:T(1,128)}, u32[]{:S(2)}) copy-start(f32[2,128,1,172]{1,2,3,0:T(1,128)} %param.8) | copy-start | bytes 528388
  2.8 1.8 %collective-permute-start = (bf16[768,256]{1,0:T(8,128)(2,1)S(1)}, bf16[768,256]{1,0:T(8,128)(2,1)S(1)}, u32[]{:S(2)}, u32[]{:S(2)}) collective-permute-start(bf16[768,256]{1,0:T(8,128)(2,1)S(1)} %get-tuple-element.33), channel_id=1, source_target_pairs={{0,1},{1,0},{2,3},{3,2},{4,5},{5,4},{6,7},{7,6},{8,9},{9,8},{10,11... | collective-permute-start | bytes 1179656 | tf_op jit(solution)/shard_map/ppermute | solution.py:28
  4.7 6.6 %collective-permute-start.1 = (bf16[192,256]{1,0:T(8,128)(2,1)S(1)}, bf16[192,256]{1,0:T(8,128)(2,1)S(1)}, u32[]{:S(2)}, u32[]{:S(2)}) collective-permute-start(bf16[192,256]{1,0:T(8,128)(2,1)S(1)} %get-tuple-element.63), channel_id=1, source_target_pairs={{0,4},{1,5},{2,6},{3,7},{4,0},{5,1},{6,2},{7,3},{8,12},{9,13},{10,... | collective-permute-start | bytes 294920 | tf_op jit(solution)/shard_map/ppermute | solution.py:28
  7.8 5.8 %collective-permute-start.3 = (bf16[192,256]{1,0:T(8,128)(2,1)S(1)}, bf16[192,256]{1,0:T(8,128)(2,1)S(1)}, u32[]{:S(2)}, u32[]{:S(2)}) collective-permute-start(bf16[192,256]{1,0:T(8,128)(2,1)S(1)} %get-tuple-element.64), channel_id=1, source_target_pairs={{0,6},{1,7},{2,4},{3,5},{4,2},{5,3},{6,0},{7,1},{8,14},{9,15},{10,... | collective-permute-start | bytes 294920 | tf_op jit(solution)/shard_map/ppermute | solution.py:28
  9.0 4.7 %collective-permute-start.2 = (bf16[192,256]{1,0:T(8,128)(2,1)S(1)}, bf16[192,256]{1,0:T(8,128)(2,1)S(1)}, u32[]{:S(2)}, u32[]{:S(2)}) collective-permute-start(bf16[192,256]{1,0:T(8,128)(2,1)S(1)} %get-tuple-element.65), channel_id=1, source_target_pairs={{0,2},{1,3},{2,0},{3,1},{4,6},{5,7},{6,4},{7,5},{8,10},{9,11},{10,... | collective-permute-start | bytes 294920 | tf_op jit(solution)/shard_map/ppermute | solution.py:28
  13.7 5.6 %collective-permute-start.4 = (bf16[192,256]{1,0:T(8,128)(2,1)S(1)}, bf16[192,256]{1,0:T(8,128)(2,1)S(1)}, u32[]{:S(2)}, u32[]{:S(2)}) collective-permute-start(bf16[192,256]{1,0:T(8,128)(2,1)S(1)} %convert_element_type.73), channel_id=1, source_target_pairs={{0,8},{1,9},{2,10},{3,11},{4,12},{5,13},{6,14},{7,15},{8,0},{9,1},... | collective-permute-start | bytes 294920 | tf_op jit(solution)/shard_map/ppermute | solution.py:28
  15.7 12.5 %collective-permute-start.8 = (f32[688,128]{1,0:T(8,128)S(1)}, f32[688,128]{1,0:T(8,128)S(1)}, u32[]{:S(2)}, u32[]{:S(2)}) collective-permute-start(f32[688,128]{1,0:T(8,128)S(1)} %pad_maximum_fusion.1.refs_4_), channel_id=1, source_target_pairs={{0,16},{16,0},{32,48},{48,32},{64,80},{80,64},{96,112},{112,96},{1... | collective-permute-start | bytes 1056776 | tf_op jit(solution)/shard_map/ppermute | solution.py:28
  19.4 7.2 %collective-permute-start.7 = (bf16[192,256]{1,0:T(8,128)(2,1)S(1)}, bf16[192,256]{1,0:T(8,128)(2,1)S(1)}, u32[]{:S(2)}, u32[]{:S(2)}) collective-permute-start(bf16[192,256]{1,0:T(8,128)(2,1)S(1)} %add_convert_fusion), channel_id=1, source_target_pairs={{0,4},{1,5},{2,6},{3,7},{4,0},{5,1},{6,2},{7,3},{8,12},{9,13},{10,... | collective-permute-start | bytes 294920 | tf_op jit(solution)/shard_map/ppermute | solution.py:28
  21.2 6.1 %collective-permute-start.6 = (bf16[192,256]{1,0:T(8,128)(2,1)S(1)}, bf16[192,256]{1,0:T(8,128)(2,1)S(1)}, u32[]{:S(2)}, u32[]{:S(2)}) collective-permute-start(bf16[192,256]{1,0:T(8,128)(2,1)S(1)} %add_convert_fusion), channel_id=1, source_target_pairs={{0,6},{1,7},{2,4},{3,5},{4,2},{5,3},{6,0},{7,1},{8,14},{9,15},{10,... | collective-permute-start | bytes 294920 | tf_op jit(solution)/shard_map/ppermute | solution.py:28
  23.3 4.6 %collective-permute-start.5 = (bf16[192,256]{1,0:T(8,128)(2,1)S(1)}, bf16[192,256]{1,0:T(8,128)(2,1)S(1)}, u32[]{:S(2)}, u32[]{:S(2)}) collective-permute-start(bf16[192,256]{1,0:T(8,128)(2,1)S(1)} %add_convert_fusion), channel_id=1, source_target_pairs={{0,2},{1,3},{2,0},{3,1},{4,6},{5,7},{6,4},{7,5},{8,10},{9,11},{10,... | collective-permute-start | bytes 294920 | tf_op jit(solution)/shard_map/ppermute | solution.py:28
  28.2 1.7 %collective-permute-start.9 = (bf16[768,256]{1,0:T(8,128)(2,1)S(1)}, bf16[768,256]{1,0:T(8,128)(2,1)S(1)}, u32[]{:S(2)}, u32[]{:S(2)}) collective-permute-start(bf16[768,256]{1,0:T(8,128)(2,1)S(1)} %pad_maximum_fusion.part_ref), channel_id=1, source_target_pairs={{0,1},{1,0},{2,3},{3,2},{4,5},{5,4},{6,7},{7,6},{8,9},{9,8},{10,11... | collective-permute-start | bytes 1179656 | tf_op jit(solution)/shard_map/ppermute | solution.py:28
  30.8 9.0 %collective-permute-start.13 = (bf16[344,128]{1,0:T(8,128)(2,1)S(1)}, bf16[344,128]{1,0:T(8,128)(2,1)S(1)}, u32[]{:S(2)}, u32[]{:S(2)}) collective-permute-start(bf16[344,128]{1,0:T(8,128)(2,1)S(1)} %get-tuple-element.52), channel_id=1, source_target_pairs={{0,64},{16,80},{32,96},{48,112},{64,0},{80,16},{96,32},{112,48},{1... | collective-permute-start | bytes 264200 | tf_op jit(solution)/shard_map/ppermute | solution.py:28
  34.1 6.8 %collective-permute-start.14 = (bf16[344,128]{1,0:T(8,128)(2,1)S(1)}, bf16[344,128]{1,0:T(8,128)(2,1)S(1)}, u32[]{:S(2)}, u32[]{:S(2)}) collective-permute-start(bf16[344,128]{1,0:T(8,128)(2,1)S(1)} %get-tuple-element.53), channel_id=1, source_target_pairs={{0,32},{16,48},{32,0},{48,16},{64,96},{80,112},{96,64},{112,80},{1... | collective-permute-start | bytes 264200 | tf_op jit(solution)/shard_map/ppermute | solution.py:28
  34.8 7.0 %collective-permute-start.15 = (bf16[344,128]{1,0:T(8,128)(2,1)S(1)}, bf16[344,128]{1,0:T(8,128)(2,1)S(1)}, u32[]{:S(2)}, u32[]{:S(2)}) collective-permute-start(bf16[344,128]{1,0:T(8,128)(2,1)S(1)} %get-tuple-element.54), channel_id=1, source_target_pairs={{0,96},{16,112},{32,64},{48,80},{64,32},{80,48},{96,0},{112,16},{1... | collective-permute-start | bytes 264200 | tf_op jit(solution)/shard_map/ppermute | solution.py:28
  36.0 9.7 %collective-permute-start.10 = (bf16[344,128]{1,0:T(8,128)(2,1)S(1)}, bf16[344,128]{1,0:T(8,128)(2,1)S(1)}, u32[]{:S(2)}, u32[]{:S(2)}) collective-permute-start(bf16[344,128]{1,0:T(8,128)(2,1)S(1)} %get-tuple-element.48), channel_id=1, source_target_pairs={{0,64},{16,80},{32,96},{48,112},{64,0},{80,16},{96,32},{112,48},{1... | collective-permute-start | bytes 264200 | tf_op jit(solution)/shard_map/ppermute | solution.py:28
  39.2 6.6 %collective-permute-start.11 = (bf16[344,128]{1,0:T(8,128)(2,1)S(1)}, bf16[344,128]{1,0:T(8,128)(2,1)S(1)}, u32[]{:S(2)}, u32[]{:S(2)}) collective-permute-start(bf16[344,128]{1,0:T(8,128)(2,1)S(1)} %get-tuple-element.49), channel_id=1, source_target_pairs={{0,32},{16,48},{32,0},{48,16},{64,96},{80,112},{96,64},{112,80},{1... | collective-permute-start | bytes 264200 | tf_op jit(solution)/shard_map/ppermute | solution.py:28
  39.9 5.9 %collective-permute-start.12 = (bf16[344,128]{1,0:T(8,128)(2,1)S(1)}, bf16[344,128]{1,0:T(8,128)(2,1)S(1)}, u32[]{:S(2)}, u32[]{:S(2)}) collective-permute-start(bf16[344,128]{1,0:T(8,128)(2,1)S(1)} %get-tuple-element.50), channel_id=1, source_target_pairs={{0,96},{16,112},{32,64},{48,80},{64,32},{80,48},{96,0},{112,16},{1... | collective-permute-start | bytes 264200 | tf_op jit(solution)/shard_map/ppermute | solution.py:28
  41.9 7.6 %collective-permute-start.17 = (bf16[344,128]{1,0:T(8,128)(2,1)S(1)}, bf16[344,128]{1,0:T(8,128)(2,1)S(1)}, u32[]{:S(2)}, u32[]{:S(2)}) collective-permute-start(bf16[344,128]{1,0:T(8,128)(2,1)S(1)} %get-tuple-element.59), channel_id=1, source_target_pairs={{0,16},{16,0},{32,48},{48,32},{64,80},{80,64},{96,112},{112,96},{1... | collective-permute-start | bytes 264200 | tf_op jit(solution)/shard_map/ppermute | solution.py:28
  45.8 6.2 %collective-permute-start.16 = (bf16[344,128]{1,0:T(8,128)(2,1)S(1)}, bf16[344,128]{1,0:T(8,128)(2,1)S(1)}, u32[]{:S(2)}, u32[]{:S(2)}) collective-permute-start(bf16[344,128]{1,0:T(8,128)(2,1)S(1)} %get-tuple-element.61), channel_id=1, source_target_pairs={{0,16},{16,0},{32,48},{48,32},{64,80},{80,64},{96,112},{112,96},{1... | collective-permute-start | bytes 264200 | tf_op jit(solution)/shard_map/ppermute | solution.py:28
  52.3 7.1 %collective-permute-start.19 = (bf16[2,344,128]{2,1,0:T(8,128)(2,1)S(1)}, bf16[2,344,128]{2,1,0:T(8,128)(2,1)S(1)}, u32[]{:S(2)}, u32[]{:S(2)}) collective-permute-start(bf16[2,344,128]{2,1,0:T(8,128)(2,1)S(1)} %adam.1.refs_0_), channel_id=1, source_target_pairs={{0,64},{16,80},{32,96},{48,112},{64,0},{80,16},{96,32},{112,48},{1... | collective-permute-start | bytes 528392 | tf_op jit(solution)/shard_map/ppermute | solution.py:28
  53.7 7.5 %collective-permute-start.20 = (bf16[2,344,128]{2,1,0:T(8,128)(2,1)S(1)}, bf16[2,344,128]{2,1,0:T(8,128)(2,1)S(1)}, u32[]{:S(2)}, u32[]{:S(2)}) collective-permute-start(bf16[2,344,128]{2,1,0:T(8,128)(2,1)S(1)} %adam.1.refs_0_), channel_id=1, source_target_pairs={{0,96},{16,112},{32,64},{48,80},{64,32},{80,48},{96,0},{112,16},{1... | collective-permute-start | bytes 528392 | tf_op jit(solution)/shard_map/ppermute | solution.py:28
  55.2 6.1 %collective-permute-start.18 = (bf16[2,344,128]{2,1,0:T(8,128)(2,1)S(1)}, bf16[2,344,128]{2,1,0:T(8,128)(2,1)S(1)}, u32[]{:S(2)}, u32[]{:S(2)}) collective-permute-start(bf16[2,344,128]{2,1,0:T(8,128)(2,1)S(1)} %adam.1.refs_0_), channel_id=1, source_target_pairs={{0,32},{16,48},{32,0},{48,16},{64,96},{80,112},{96,64},{112,80},{1... | collective-permute-start | bytes 528392 | tf_op jit(solution)/shard_map/ppermute | solution.py:28

commit v4 on v3

--- a/solution.py
+++ b/solution.py
@@ -68,20 +68,17 @@
     n_g, feat, rank = basis.shape
     half = rows.shape[1]
     piece = half // NX
-    copies = []
-    for g in range(n_g):
-        src = basis_ref.at[g, pl.ds(pl.multiple_of(at["t"] * feat, feat), feat), :]
-        copies.append(pltpu.make_async_copy(src, basis.at[g], basis_sem.at[g]))
+    src = basis_ref.at[:, pl.ds(pl.multiple_of(at["t"] * feat, feat), feat), :]
+    copies = [pltpu.make_async_copy(src, basis, basis_sem)]
     for h, core in enumerate((1 - at["core"], at["core"])):
         src = inputs_ref.at[pl.ds(pl.multiple_of(core * half, half), half), :]
         copies.append(pltpu.make_async_copy(src, rows.at[h], row_sem.at[h]))
     for copy in copies:
         copy.start()
-    for copy in copies[:n_g]:
-        copy.wait()
+    copies[0].wait()
     both = jnp.concatenate([basis[g] for g in range(n_g)], axis=1)
     for h in range(2):
-        copies[n_g + h].wait()
+        copies[1 + h].wait()
         for k in range(NX):
             src = pl.multiple_of((at["x"] ^ k) * piece, piece)
             product = jnp.dot(rows[h, pl.ds(src, piece), :], both, preferred_element_type=F32)
@@ -108,7 +105,7 @@
             pltpu.VMEM((2, half, feat), BF16),
             pltpu.VMEM((n_g, feat, rank), BF16),
             pltpu.SemaphoreType.DMA((2,)),
-            pltpu.SemaphoreType.DMA((n_g,)),
+            pltpu.SemaphoreType.DMA,
         ],
         compiler_params=params(52),
         cost_estimate=cost(2 * tokens * feat * n_g * rank, 2 * tokens * feat),
@@ -284,16 +281,19 @@
             norm[w, g, :size, :] = wide[
                 w, g, pl.ds(pl.multiple_of(start, 16), size), :
             ].astype(BF16)
-            block[w, g, :size, :] = jnp.dot(
-                norm[w, g, :size, :], basis_ref[g], preferred_element_type=F32
-            ).astype(BF16)
-            to = pl.ds(pl.multiple_of(pair * (2 * share) + start, 16), size)
-            copies.append(
-                pltpu.make_async_copy(
-                    block.at[w, g, :size, :], out_ref.at[g, to, :], sem.at[w, g]
+            for c, (low, high) in enumerate(((0, 176), (176, size))):
+                block[w, g, low:high, :] = jnp.dot(
+                    norm[w, g, low:high, :], basis_ref[g], preferred_element_type=F32
+                ).astype(BF16)
+                at_row = pl.multiple_of(pair * (2 * share) + start + low, 16)
+                copies.append(
+                    pltpu.make_async_copy(
+                        block.at[w, g, low:high, :],
+                        out_ref.at[g, pl.ds(at_row, high - low), :],
+                        sem.at[w, g, c],
+                    )
                 )
-            )
-            copies[-1].start()
+                copies[-1].start()
     for copy in copies:
         copy.wait()
 
@@ -311,7 +311,7 @@
             pltpu.VMEM((n_w, n_g, 2 * share, rank), F32),
             pltpu.VMEM((n_w, n_g, REST, rank), BF16),
             pltpu.VMEM((n_w, n_g, REST, weight_rows), BF16),
-            pltpu.SemaphoreType.DMA((n_w, n_g)),
+            pltpu.SemaphoreType.DMA((n_w, n_g, 2)),
         ],
         input_output_aliases={} if out is None else {n + 1: 0},
         compiler_params=params(12),

time: 64.1 us -> 63.9 us (level)
  transfers between devices with their start and end apart: 21 -> 21, of which waited for: 11 -> 11; matrix products, arithmetic and copies ran while one was open for 2% -> 2% of each run, Pallas kernels for 17% -> 16%
where the time goes in v4:
time: 63.9 us; the launch traced here: 63.1 us
  starting transfers between devices  34.2 us (54%)
  Pallas kernels  15.4 us (24%)
  waiting for transfers between devices  11 us (17%)
  local copies, waits for them, and re-layouts  1.32 us (2%)
  between operations  0.8 us (1%)
    ppermute x21, starting transfers between devices, swap(): return lax.ppermute(v, axis, [(i, i ^ bits) for i in range(size)])  34.2 us
    ppermute x21, waiting for transfers between devices, swap(): return lax.ppermute(v, axis, [(i, i ^ bits) for i in range(size)])  11 us
    pallas_call x3, Pallas kernels, update(): pl.pallas_call(lambda *refs: update_kernel(windows, n, *refs), in_specs=[...  4.69 us
    pallas_call x2, Pallas kernels, stage(): pl.pallas_call(lambda *refs: stage_kernel(g, *refs), in_specs=[HBM], out_...  4.41 us
    pallas_call x1, Pallas kernels, project(): pl.pallas_call(project_kernel, in_specs=[HBM] * 2, out_specs=[VMEM] * 2,...  2.04 us
    pallas_call x2, Pallas kernels, rank_far(): pl.pallas_call(lambda *refs: far_kernel(g, *refs), in_specs=[VMEM] * 3, o...  1.71 us
    pallas_call x1, Pallas kernels, rank_near(): pl.pallas_call(near_kernel, in_specs=[VMEM] * (1 + n_g), out_specs=VMEM,...  1.33 us
  transfers between devices with their start and end apart: 21, of which 11 were waited for; matrix products, arithmetic and copies ran while one was open for 2% of the time, Pallas kernels for 16%

profile of v4, /device:TPU:0, one launch (start us, length us, event | category | flops | bytes accessed | tf_op | source)
XLA Modules:
  0.0 63.1 jit_solution(5598629084974582918)
XLA Ops:
  0.7 2.0 %project.1 = (bf16[768,256]{1,0:T(8,128)(2,1)S(1)}, f32[768,256]{1,0:T(8,128)S(1)}) custom-call(bf16[1536,512]{1,0:T(8,128)(2,1)} %inputs_ref.1, bf16[2,8192,128]{2,1,0:T(8,128)(2,1)} %basis_ref.1), custom_call_target="tpu_custom_call" | custom-call | flops 402653184 | bytes 1572864 | tf_op jit(solution)/shard_map/project/pallas_call | solution.py:96
  2.8 1.1 %constant_dynamic-slice_fusion = bf16[2,1024,128]{2,1,0:T(8,128)(2,1)S(1)} fusion(bf16[2,8192,128]{2,1,0:T(8,128)(2,1)} %basis_ref.1, s32[]{:T(128)S(6)} %select_n.3), kind=kLoop, calls=%fused_computation.10 | loop fusion | bytes 1048580 | tf_op jit(solution)/shard_map/dynamic_slice | solution.py:327
  4.6 3.2 %collective-permute-start.1 = (bf16[192,256]{1,0:T(8,128)(2,1)S(1)}, bf16[192,256]{1,0:T(8,128)(2,1)S(1)}, u32[]{:S(2)}, u32[]{:S(2)}) collective-permute-start(bf16[192,256]{1,0:T(8,128)(2,1)S(1)} %get-tuple-element.63), channel_id=1, source_target_pairs={{0,4},{1,5},{2,6},{3,7},{4,0},{5,1},{6,2},{7,3},{8,12},{9,13},{10,... | collective-permute-start | bytes 294920 | tf_op jit(solution)/shard_map/ppermute | solution.py:28
  7.8 1.1 %collective-permute-start.3 = (bf16[192,256]{1,0:T(8,128)(2,1)S(1)}, bf16[192,256]{1,0:T(8,128)(2,1)S(1)}, u32[]{:S(2)}, u32[]{:S(2)}) collective-permute-start(bf16[192,256]{1,0:T(8,128)(2,1)S(1)} %get-tuple-element.64), channel_id=1, source_target_pairs={{0,6},{1,7},{2,4},{3,5},{4,2},{5,3},{6,0},{7,1},{8,14},{9,15},{10,... | collective-permute-start | bytes 294920 | tf_op jit(solution)/shard_map/ppermute | solution.py:28
  9.0 2.2 %stage.2.refs_0_.refs_2_ = bf16[1376,1536]{1,0:T(8,128)(2,1)S(1)} custom-call(bf16[2,1376,1536]{2,1,0:T(8,128)(2,1)} %bitcast.19), custom_call_target="tpu_custom_call" | custom-call | bytes 8454144 | tf_op jit(solution)/shard_map/stage/pallas_call | solution.py:123
  11.2 2.4 %collective-permute-done.3 = bf16[192,256]{1,0:T(8,128)(2,1)S(1)} collective-permute-done((bf16[192,256]{1,0:T(8,128)(2,1)S(1)}, bf16[192,256]{1,0:T(8,128)(2,1)S(1)}, u32[]{:S(2)}, u32[]{:S(2)}) %collective-permute-start.3) | collective-permute-done | bytes 98336 | tf_op jit(solution)/shard_map/ppermute | solution.py:28
  13.7 2.0 %collective-permute-start.4 = (bf16[192,256]{1,0:T(8,128)(2,1)S(1)}, bf16[192,256]{1,0:T(8,128)(2,1)S(1)}, u32[]{:S(2)}, u32[]{:S(2)}) collective-permute-start(bf16[192,256]{1,0:T(8,128)(2,1)S(1)} %convert_element_type.73), channel_id=1, source_target_pairs={{0,8},{1,9},{2,10},{3,11},{4,12},{5,13},{6,14},{7,15},{8,0},{9,1},... | collective-permute-start | bytes 294920 | tf_op jit(solution)/shard_map/ppermute | solution.py:28
  15.7 3.6 %collective-permute-start.8 = (f32[688,128]{1,0:T(8,128)S(1)}, f32[688,128]{1,0:T(8,128)S(1)}, u32[]{:S(2)}, u32[]{:S(2)}) collective-permute-start(f32[688,128]{1,0:T(8,128)S(1)} %pad_maximum_fusion.1.refs_4_), channel_id=1, source_target_pairs={{0,16},{16,0},{32,48},{48,32},{64,80},{80,64},{96,112},{112,96},{1... | collective-permute-start | bytes 1056776 | tf_op jit(solution)/shard_map/ppermute | solution.py:28
  19.3 1.8 %collective-permute-start.7 = (bf16[192,256]{1,0:T(8,128)(2,1)S(1)}, bf16[192,256]{1,0:T(8,128)(2,1)S(1)}, u32[]{:S(2)}, u32[]{:S(2)}) collective-permute-start(bf16[192,256]{1,0:T(8,128)(2,1)S(1)} %add_convert_fusion), channel_id=1, source_target_pairs={{0,4},{1,5},{2,6},{3,7},{4,0},{5,1},{6,2},{7,3},{8,12},{9,13},{10,... | collective-permute-start | bytes 294920 | tf_op jit(solution)/shard_map/ppermute | solution.py:28
  21.1 2.1 %collective-permute-start.6 = (bf16[192,256]{1,0:T(8,128)(2,1)S(1)}, bf16[192,256]{1,0:T(8,128)(2,1)S(1)}, u32[]{:S(2)}, u32[]{:S(2)}) collective-permute-start(bf16[192,256]{1,0:T(8,128)(2,1)S(1)} %add_convert_fusion), channel_id=1, source_target_pairs={{0,6},{1,7},{2,4},{3,5},{4,2},{5,3},{6,0},{7,1},{8,14},{9,15},{10,... | collective-permute-start | bytes 294920 | tf_op jit(solution)/shard_map/ppermute | solution.py:28
  23.2 2.2 %stage.3.refs_1_.refs_2_ = bf16[1376,1536]{1,0:T(8,128)(2,1)S(1)} custom-call(bf16[2,1376,1536]{2,1,0:T(8,128)(2,1)} %bitcast.20), custom_call_target="tpu_custom_call" | custom-call | bytes 8454144 | tf_op jit(solution)/shard_map/stage/pallas_call | solution.py:123
  25.4 1.1 %collective-permute-done.7 = bf16[192,256]{1,0:T(8,128)(2,1)S(1)} collective-permute-done((bf16[192,256]{1,0:T(8,128)(2,1)S(1)}, bf16[192,256]{1,0:T(8,128)(2,1)S(1)}, u32[]{:S(2)}, u32[]{:S(2)}) %collective-permute-start.7) | collective-permute-done | bytes 98336 | tf_op jit(solution)/shard_map/ppermute | solution.py:28
  26.5 0.8 %collective-permute-done.6 = bf16[192,256]{1,0:T(8,128)(2,1)S(1)} collective-permute-done((bf16[192,256]{1,0:T(8,128)(2,1)S(1)}, bf16[192,256]{1,0:T(8,128)(2,1)S(1)}, u32[]{:S(2)}, u32[]{:S(2)}) %collective-permute-start.6) | collective-permute-done | bytes 98336 | tf_op jit(solution)/shard_map/ppermute | solution.py:28
  28.2 1.3 %rank_near.1.refs_1_ = f32[2,1376,128]{2,1,0:T(8,128)S(1)} custom-call(bf16[768,256]{1,0:T(8,128)(2,1)S(1)} %pad_maximum_fusion.part_ref, bf16[1376,1536]{1,0:T(8,128)(2,1)S(1)} %stage.2.refs_0_.refs_2_, bf16[1376,1536]{1,0:T(8,128)(2,1)S(1)} %stage.3.refs_1_.refs_2_), custom_call_target="tpu_custom_call" | custom-call | flops 541065216 | bytes 4194304 | tf_op jit(solution)/shard_map/rank_near/pallas_call | solution.py:158
  29.9 0.9 %rank_far.3 = (f32[344,128]{1,0:T(8,128)S(1)}, bf16[344,128]{1,0:T(8,128)(2,1)S(1)}, bf16[344,128]{1,0:T(8,128)(2,1)S(1)}, bf16[344,128]{1,0:T(8,128)(2,1)S(1)}) custom-call(bf16[768,256]{1,0:T(8,128)(2,1)S(1)} %collective-permute-done.9.refs_0_, f32[2,1376,128]{2,1,0:T(8,128)S(1)} %rank_near.1.refs_1_, bf16[1376,1536]{1,0:T(8,128)(2,1)S(1)} %stage.3.refs_1_.refs_2_), custom_call_target="tpu_custom_call" | custom-call | flops 270532608 | bytes 2097152 | tf_op jit(solution)/shard_map/rank_far/pallas_call | solution.py:187
  30.8 3.3 %collective-permute-start.13 = (bf16[344,128]{1,0:T(8,128)(2,1)S(1)}, bf16[344,128]{1,0:T(8,128)(2,1)S(1)}, u32[]{:S(2)}, u32[]{:S(2)}) collective-permute-start(bf16[344,128]{1,0:T(8,128)(2,1)S(1)} %get-tuple-element.52), channel_id=1, source_target_pairs={{0,64},{16,80},{32,96},{48,112},{64,0},{80,16},{96,32},{112,48},{1... | collective-permute-start | bytes 264200 | tf_op jit(solution)/shard_map/ppermute | solution.py:28
  35.1 0.9 %rank_far.2 = (f32[344,128]{1,0:T(8,128)S(1)}, bf16[344,128]{1,0:T(8,128)(2,1)S(1)}, bf16[344,128]{1,0:T(8,128)(2,1)S(1)}, bf16[344,128]{1,0:T(8,128)(2,1)S(1)}) custom-call(bf16[768,256]{1,0:T(8,128)(2,1)S(1)} %collective-permute-done.9.refs_0_, f32[2,1376,128]{2,1,0:T(8,128)S(1)} %rank_near.1.refs_1_, bf16[1376,1536]{1,0:T(8,128)(2,1)S(1)} %stage.2.refs_0_.refs_2_), custom_call_target="tpu_custom_call" | custom-call | flops 270532608 | bytes 2097152 | tf_op jit(solution)/shard_map/rank_far/pallas_call | solution.py:187
  36.0 3.1 %collective-permute-start.10 = (bf16[344,128]{1,0:T(8,128)(2,1)S(1)}, bf16[344,128]{1,0:T(8,128)(2,1)S(1)}, u32[]{:S(2)}, u32[]{:S(2)}) collective-permute-start(bf16[344,128]{1,0:T(8,128)(2,1)S(1)} %get-tuple-element.48), channel_id=1, source_target_pairs={{0,64},{16,80},{32,96},{48,112},{64,0},{80,16},{96,32},{112,48},{1... | collective-permute-start | bytes 264200 | tf_op jit(solution)/shard_map/ppermute | solution.py:28
  39.1 0.7 %collective-permute-start.11 = (bf16[344,128]{1,0:T(8,128)(2,1)S(1)}, bf16[344,128]{1,0:T(8,128)(2,1)S(1)}, u32[]{:S(2)}, u32[]{:S(2)}) collective-permute-start(bf16[344,128]{1,0:T(8,128)(2,1)S(1)} %get-tuple-element.49), channel_id=1, source_target_pairs={{0,32},{16,48},{32,0},{48,16},{64,96},{80,112},{96,64},{112,80},{1... | collective-permute-start | bytes 264200 | tf_op jit(solution)/shard_map/ppermute | solution.py:28
  39.8 1.0 %collective-permute-start.12 = (bf16[344,128]{1,0:T(8,128)(2,1)S(1)}, bf16[344,128]{1,0:T(8,128)(2,1)S(1)}, u32[]{:S(2)}, u32[]{:S(2)}) collective-permute-start(bf16[344,128]{1,0:T(8,128)(2,1)S(1)} %get-tuple-element.50), channel_id=1, source_target_pairs={{0,96},{16,112},{32,64},{48,80},{64,32},{80,48},{96,0},{112,16},{1... | collective-permute-start | bytes 264200 | tf_op jit(solution)/shard_map/ppermute | solution.py:28
  40.8 0.9 %collective-permute-done.15 = bf16[344,128]{1,0:T(8,128)(2,1)S(1)} collective-permute-done((bf16[344,128]{1,0:T(8,128)(2,1)S(1)}, bf16[344,128]{1,0:T(8,128)(2,1)S(1)}, u32[]{:S(2)}, u32[]{:S(2)}) %collective-permute-start.15) | collective-permute-done | bytes 88096 | tf_op jit(solution)/shard_map/ppermute | solution.py:28
  41.8 3.9 %collective-permute-start.17 = (bf16[344,128]{1,0:T(8,128)(2,1)S(1)}, bf16[344,128]{1,0:T(8,128)(2,1)S(1)}, u32[]{:S(2)}, u32[]{:S(2)}) collective-permute-start(bf16[344,128]{1,0:T(8,128)(2,1)S(1)} %get-tuple-element.59), channel_id=1, source_target_pairs={{0,16},{16,0},{32,48},{48,32},{64,80},{80,64},{96,112},{112,96},{1... | collective-permute-start | bytes 264200 | tf_op jit(solution)/shard_map/ppermute | solution.py:28
  45.7 3.7 %collective-permute-start.16 = (bf16[344,128]{1,0:T(8,128)(2,1)S(1)}, bf16[344,128]{1,0:T(8,128)(2,1)S(1)}, u32[]{:S(2)}, u32[]{:S(2)}) collective-permute-start(bf16[344,128]{1,0:T(8,128)(2,1)S(1)} %get-tuple-element.61), channel_id=1, source_target_pairs={{0,16},{16,0},{32,48},{48,32},{64,80},{80,64},{96,112},{112,96},{1... | collective-permute-start | bytes 264200 | tf_op jit(solution)/shard_map/ppermute | solution.py:28
  49.4 2.5 %collective-permute-done.16.refs_2_ = bf16[344,128]{1,0:T(8,128)(2,1)S(1)} collective-permute-done((bf16[344,128]{1,0:T(8,128)(2,1)S(1)}, bf16[344,128]{1,0:T(8,128)(2,1)S(1)}, u32[]{:S(2)}, u32[]{:S(2)}) %collective-permute-start.16) | collective-permute-done | bytes 88096 | tf_op jit(solution)/shard_map/ppermute | solution.py:28
  52.3 1.4 %collective-permute-start.19 = (bf16[2,344,128]{2,1,0:T(8,128)(2,1)S(1)}, bf16[2,344,128]{2,1,0:T(8,128)(2,1)S(1)}, u32[]{:S(2)}, u32[]{:S(2)}) collective-permute-start(bf16[2,344,128]{2,1,0:T(8,128)(2,1)S(1)} %adam.1.refs_0_), channel_id=1, source_target_pairs={{0,64},{16,80},{32,96},{48,112},{64,0},{80,16},{96,32},{112,48},{1... | collective-permute-start | bytes 528392 | tf_op jit(solution)/shard_map/ppermute | solution.py:28
  53.7 1.4 %collective-permute-start.20 = (bf16[2,344,128]{2,1,0:T(8,128)(2,1)S(1)}, bf16[2,344,128]{2,1,0:T(8,128)(2,1)S(1)}, u32[]{:S(2)}, u32[]{:S(2)}) collective-permute-start(bf16[2,344,128]{2,1,0:T(8,128)(2,1)S(1)} %adam.1.refs_0_), channel_id=1, source_target_pairs={{0,96},{16,112},{32,64},{48,80},{64,32},{80,48},{96,0},{112,16},{1... | collective-permute-start | bytes 528392 | tf_op jit(solution)/shard_map/ppermute | solution.py:28
  55.1 0.7 %collective-permute-start.18 = (bf16[2,344,128]{2,1,0:T(8,128)(2,1)S(1)}, bf16[2,344,128]{2,1,0:T(8,128)(2,1)S(1)}, u32[]{:S(2)}, u32[]{:S(2)}) collective-permute-start(bf16[2,344,128]{2,1,0:T(8,128)(2,1)S(1)} %adam.1.refs_0_), channel_id=1, source_target_pairs={{0,32},{16,48},{32,0},{48,16},{64,96},{80,112},{96,64},{112,80},{1... | collective-permute-start | bytes 528392 | tf_op jit(solution)/shard_map/ppermute | solution.py:28
  55.8 0.9 %new_moments.1 = (f32[344,1,128]{2,1,0:T(1,128)}, f32[344,1,128]{2,1,0:T(1,128)}) custom-call(f32[344,128]{1,0:T(8,128)S(1)} %get-tuple-element.62.refs_0_, f32[344,128]{1,0:T(8,128)S(1)} %get-tuple-element.60.refs_1_, bf16[344,128]{1,0:T(8,128)(2,1)S(1)} %collective-permute-done.16.refs_2_, bf16[344,128]{1,0:T(8,128)(2,1)S(1)} %collective-permute-done.17.refs_3_, ...), custom_call_target="tpu_custom_call" | custom-call | tf_op jit(solution)/shard_map/new_moments/pallas_call | solution.py:253
  56.8 1.4 %update.3.refs_2_ = bf16[2,1376,1024]{2,1,0:T(8,128)(2,1)} custom-call(bf16[2,344,128]{2,1,0:T(8,128)(2,1)S(1)} %adam.1.refs_0_, bf16[2,128,1024]{2,1,0:T(8,128)(2,1)S(1)} %bitcast.15), custom_call_target="tpu_custom_call" | custom-call | flops 184549376 | bytes 1441792 | tf_op jit(solution)/shard_map/update/pallas_call | solution.py:305
  58.2 1.2 %collective-permute-done.19.refs_0_.refs_2_ = bf16[2,344,128]{2,1,0:T(8,128)(2,1)S(1)} collective-permute-done((bf16[2,344,128]{2,1,0:T(8,128)(2,1)S(1)}, bf16[2,344,128]{2,1,0:T(8,128)(2,1)S(1)}, u32[]{:S(2)}, u32[]{:S(2)}) %collective-permute-start.19) | collective-permute-done | bytes 176160 | tf_op jit(solution)/shard_map/ppermute | solution.py:28
  59.4 1.4 %update.4.refs_5_ = bf16[2,1376,1024]{2,1,0:T(8,128)(2,1)} custom-call(bf16[2,344,128]{2,1,0:T(8,128)(2,1)S(1)} %collective-permute-done.19.refs_0_.refs_2_, bf16[2,128,1024]{2,1,0:T(8,128)(2,1)S(1)} %bitcast.16, bf16[2,1376,1024]{2,1,0:T(8,128)(2,1)} %update.3.refs_2_), custom_call_target="tpu_custom_call", output_to_operand_aliasing={{}: (2, {})} | custom-call | flops 184549376 | bytes 1441792 | tf_op jit(solution)/shard_map/update/pallas_call | solution.py:305
  61.2 1.9 %update.5 = bf16[2,1376,1024]{2,1,0:T(8,128)(2,1)} custom-call(bf16[2,344,128]{2,1,0:T(8,128)(2,1)S(1)} %adam.1.refs_0_, bf16[2,344,128]{2,1,0:T(8,128)(2,1)S(1)} %collective-permute-done.18.refs_1_, bf16[2,344,128]{2,1,0:T(8,128)(2,1)S(1)} %collective-permute-done.19.refs_0_.refs_2_, ...), custom_call_target="tpu_custom_call", output_to_operand_aliasing={{}: (5, {})} | custom-call | flops 369098752 | bytes 2883584 | tf_op jit(solution)/shard_map/update/pallas_call | solution.py:305
  (35 shorter events, 4.1 us)
Async XLA Ops:
  0.6 8.3 %copy-start = (f32[2,128,1,172]{1,2,3,0:T(1,128)S(1)}, f32[2,128,1,172]{1,2,3,0:T(1,128)}, u32[]{:S(2)}) copy-start(f32[2,128,1,172]{1,2,3,0:T(1,128)} %param.9) | copy-start | bytes 528388
  0.6 8.3 %copy-start.1 = (f32[2,128,1,172]{1,2,3,0:T(1,128)S(1)}, f32[2,128,1,172]{1,2,3,0:T(1,128)}, u32[]{:S(2)}) copy-start(f32[2,128,1,172]{1,2,3,0:T(1,128)} %param.8) | copy-start | bytes 528388
  2.7 1.8 %collective-permute-start = (bf16[768,256]{1,0:T(8,128)(2,1)S(1)}, bf16[768,256]{1,0:T(8,128)(2,1)S(1)}, u32[]{:S(2)}, u32[]{:S(2)}) collective-permute-start(bf16[768,256]{1,0:T(8,128)(2,1)S(1)} %get-tuple-element.33), channel_id=1, source_target_pairs={{0,1},{1,0},{2,3},{3,2},{4,5},{5,4},{6,7},{7,6},{8,9},{9,8},{10,11... | collective-permute-start | bytes 1179656 | tf_op jit(solution)/shard_map/ppermute | solution.py:28
  4.6 6.6 %collective-permute-start.1 = (bf16[192,256]{1,0:T(8,128)(2,1)S(1)}, bf16[192,256]{1,0:T(8,128)(2,1)S(1)}, u32[]{:S(2)}, u32[]{:S(2)}) collective-permute-start(bf16[192,256]{1,0:T(8,128)(2,1)S(1)} %get-tuple-element.63), channel_id=1, source_target_pairs={{0,4},{1,5},{2,6},{3,7},{4,0},{5,1},{6,2},{7,3},{8,12},{9,13},{10,... | collective-permute-start | bytes 294920 | tf_op jit(solution)/shard_map/ppermute | solution.py:28
  7.8 5.8 %collective-permute-start.3 = (bf16[192,256]{1,0:T(8,128)(2,1)S(1)}, bf16[192,256]{1,0:T(8,128)(2,1)S(1)}, u32[]{:S(2)}, u32[]{:S(2)}) collective-permute-start(bf16[192,256]{1,0:T(8,128)(2,1)S(1)} %get-tuple-element.64), channel_id=1, source_target_pairs={{0,6},{1,7},{2,4},{3,5},{4,2},{5,3},{6,0},{7,1},{8,14},{9,15},{10,... | collective-permute-start | bytes 294920 | tf_op jit(solution)/shard_map/ppermute | solution.py:28
  8.9 4.7 %collective-permute-start.2 = (bf16[192,256]{1,0:T(8,128)(2,1)S(1)}, bf16[192,256]{1,0:T(8,128)(2,1)S(1)}, u32[]{:S(2)}, u32[]{:S(2)}) collective-permute-start(bf16[192,256]{1,0:T(8,128)(2,1)S(1)} %get-tuple-element.65), channel_id=1, source_target_pairs={{0,2},{1,3},{2,0},{3,1},{4,6},{5,7},{6,4},{7,5},{8,10},{9,11},{10,... | collective-permute-start | bytes 294920 | tf_op jit(solution)/shard_map/ppermute | solution.py:28
  13.7 5.6 %collective-permute-start.4 = (bf16[192,256]{1,0:T(8,128)(2,1)S(1)}, bf16[192,256]{1,0:T(8,128)(2,1)S(1)}, u32[]{:S(2)}, u32[]{:S(2)}) collective-permute-start(bf16[192,256]{1,0:T(8,128)(2,1)S(1)} %convert_element_type.73), channel_id=1, source_target_pairs={{0,8},{1,9},{2,10},{3,11},{4,12},{5,13},{6,14},{7,15},{8,0},{9,1},... | collective-permute-start | bytes 294920 | tf_op jit(solution)/shard_map/ppermute | solution.py:28
  15.7 12.5 %collective-permute-start.8 = (f32[688,128]{1,0:T(8,128)S(1)}, f32[688,128]{1,0:T(8,128)S(1)}, u32[]{:S(2)}, u32[]{:S(2)}) collective-permute-start(f32[688,128]{1,0:T(8,128)S(1)} %pad_maximum_fusion.1.refs_4_), channel_id=1, source_target_pairs={{0,16},{16,0},{32,48},{48,32},{64,80},{80,64},{96,112},{112,96},{1... | collective-permute-start | bytes 1056776 | tf_op jit(solution)/shard_map/ppermute | solution.py:28
  19.3 7.2 %collective-permute-start.7 = (bf16[192,256]{1,0:T(8,128)(2,1)S(1)}, bf16[192,256]{1,0:T(8,128)(2,1)S(1)}, u32[]{:S(2)}, u32[]{:S(2)}) collective-permute-start(bf16[192,256]{1,0:T(8,128)(2,1)S(1)} %add_convert_fusion), channel_id=1, source_target_pairs={{0,4},{1,5},{2,6},{3,7},{4,0},{5,1},{6,2},{7,3},{8,12},{9,13},{10,... | collective-permute-start | bytes 294920 | tf_op jit(solution)/shard_map/ppermute | solution.py:28
  21.1 6.1 %collective-permute-start.6 = (bf16[192,256]{1,0:T(8,128)(2,1)S(1)}, bf16[192,256]{1,0:T(8,128)(2,1)S(1)}, u32[]{:S(2)}, u32[]{:S(2)}) collective-permute-start(bf16[192,256]{1,0:T(8,128)(2,1)S(1)} %add_convert_fusion), channel_id=1, source_target_pairs={{0,6},{1,7},{2,4},{3,5},{4,2},{5,3},{6,0},{7,1},{8,14},{9,15},{10,... | collective-permute-start | bytes 294920 | tf_op jit(solution)/shard_map/ppermute | solution.py:28
  23.2 4.6 %collective-permute-start.5 = (bf16[192,256]{1,0:T(8,128)(2,1)S(1)}, bf16[192,256]{1,0:T(8,128)(2,1)S(1)}, u32[]{:S(2)}, u32[]{:S(2)}) collective-permute-start(bf16[192,256]{1,0:T(8,128)(2,1)S(1)} %add_convert_fusion), channel_id=1, source_target_pairs={{0,2},{1,3},{2,0},{3,1},{4,6},{5,7},{6,4},{7,5},{8,10},{9,11},{10,... | collective-permute-start | bytes 294920 | tf_op jit(solution)/shard_map/ppermute | solution.py:28
  28.2 1.7 %collective-permute-start.9 = (bf16[768,256]{1,0:T(8,128)(2,1)S(1)}, bf16[768,256]{1,0:T(8,128)(2,1)S(1)}, u32[]{:S(2)}, u32[]{:S(2)}) collective-permute-start(bf16[768,256]{1,0:T(8,128)(2,1)S(1)} %pad_maximum_fusion.part_ref), channel_id=1, source_target_pairs={{0,1},{1,0},{2,3},{3,2},{4,5},{5,4},{6,7},{7,6},{8,9},{9,8},{10,11... | collective-permute-start | bytes 1179656 | tf_op jit(solution)/shard_map/ppermute | solution.py:28
  30.8 9.0 %collective-permute-start.13 = (bf16[344,128]{1,0:T(8,128)(2,1)S(1)}, bf16[344,128]{1,0:T(8,128)(2,1)S(1)}, u32[]{:S(2)}, u32[]{:S(2)}) collective-permute-start(bf16[344,128]{1,0:T(8,128)(2,1)S(1)} %get-tuple-element.52), channel_id=1, source_target_pairs={{0,64},{16,80},{32,96},{48,112},{64,0},{80,16},{96,32},{112,48},{1... | collective-permute-start | bytes 264200 | tf_op jit(solution)/shard_map/ppermute | solution.py:28
  34.0 6.8 %collective-permute-start.14 = (bf16[344,128]{1,0:T(8,128)(2,1)S(1)}, bf16[344,128]{1,0:T(8,128)(2,1)S(1)}, u32[]{:S(2)}, u32[]{:S(2)}) collective-permute-start(bf16[344,128]{1,0:T(8,128)(2,1)S(1)} %get-tuple-element.53), channel_id=1, source_target_pairs={{0,32},{16,48},{32,0},{48,16},{64,96},{80,112},{96,64},{112,80},{1... | collective-permute-start | bytes 264200 | tf_op jit(solution)/shard_map/ppermute | solution.py:28
  34.7 7.0 %collective-permute-start.15 = (bf16[344,128]{1,0:T(8,128)(2,1)S(1)}, bf16[344,128]{1,0:T(8,128)(2,1)S(1)}, u32[]{:S(2)}, u32[]{:S(2)}) collective-permute-start(bf16[344,128]{1,0:T(8,128)(2,1)S(1)} %get-tuple-element.54), channel_id=1, source_target_pairs={{0,96},{16,112},{32,64},{48,80},{64,32},{80,48},{96,0},{112,16},{1... | collective-permute-start | bytes 264200 | tf_op jit(solution)/shard_map/ppermute | solution.py:28
  36.0 9.7 %collective-permute-start.10 = (bf16[344,128]{1,0:T(8,128)(2,1)S(1)}, bf16[344,128]{1,0:T(8,128)(2,1)S(1)}, u32[]{:S(2)}, u32[]{:S(2)}) collective-permute-start(bf16[344,128]{1,0:T(8,128)(2,1)S(1)} %get-tuple-element.48), channel_id=1, source_target_pairs={{0,64},{16,80},{32,96},{48,112},{64,0},{80,16},{96,32},{112,48},{1... | collective-permute-start | bytes 264200 | tf_op jit(solution)/shard_map/ppermute | solution.py:28
  39.1 6.6 %collective-permute-start.11 = (bf16[344,128]{1,0:T(8,128)(2,1)S(1)}, bf16[344,128]{1,0:T(8,128)(2,1)S(1)}, u32[]{:S(2)}, u32[]{:S(2)}) collective-permute-start(bf16[344,128]{1,0:T(8,128)(2,1)S(1)} %get-tuple-element.49), channel_id=1, source_target_pairs={{0,32},{16,48},{32,0},{48,16},{64,96},{80,112},{96,64},{112,80},{1... | collective-permute-start | bytes 264200 | tf_op jit(solution)/shard_map/ppermute | solution.py:28
  39.8 5.9 %collective-permute-start.12 = (bf16[344,128]{1,0:T(8,128)(2,1)S(1)}, bf16[344,128]{1,0:T(8,128)(2,1)S(1)}, u32[]{:S(2)}, u32[]{:S(2)}) collective-permute-start(bf16[344,128]{1,0:T(8,128)(2,1)S(1)} %get-tuple-element.50), channel_id=1, source_target_pairs={{0,96},{16,112},{32,64},{48,80},{64,32},{80,48},{96,0},{112,16},{1... | collective-permute-start | bytes 264200 | tf_op jit(solution)/shard_map/ppermute | solution.py:28
  41.8 7.6 %collective-permute-start.17 = (bf16[344,128]{1,0:T(8,128)(2,1)S(1)}, bf16[344,128]{1,0:T(8,128)(2,1)S(1)}, u32[]{:S(2)}, u32[]{:S(2)}) collective-permute-start(bf16[344,128]{1,0:T(8,128)(2,1)S(1)} %get-tuple-element.59), channel_id=1, source_target_pairs={{0,16},{16,0},{32,48},{48,32},{64,80},{80,64},{96,112},{112,96},{1... | collective-permute-start | bytes 264200 | tf_op jit(solution)/shard_map/ppermute | solution.py:28
  45.7 6.2 %collective-permute-start.16 = (bf16[344,128]{1,0:T(8,128)(2,1)S(1)}, bf16[344,128]{1,0:T(8,128)(2,1)S(1)}, u32[]{:S(2)}, u32[]{:S(2)}) collective-permute-start(bf16[344,128]{1,0:T(8,128)(2,1)S(1)} %get-tuple-element.61), channel_id=1, source_target_pairs={{0,16},{16,0},{32,48},{48,32},{64,80},{80,64},{96,112},{112,96},{1... | collective-permute-start | bytes 264200 | tf_op jit(solution)/shard_map/ppermute | solution.py:28
  52.3 7.1 %collective-permute-start.19 = (bf16[2,344,128]{2,1,0:T(8,128)(2,1)S(1)}, bf16[2,344,128]{2,1,0:T(8,128)(2,1)S(1)}, u32[]{:S(2)}, u32[]{:S(2)}) collective-permute-start(bf16[2,344,128]{2,1,0:T(8,128)(2,1)S(1)} %adam.1.refs_0_), channel_id=1, source_target_pairs={{0,64},{16,80},{32,96},{48,112},{64,0},{80,16},{96,32},{112,48},{1... | collective-permute-start | bytes 528392 | tf_op jit(solution)/shard_map/ppermute | solution.py:28
  53.7 7.5 %collective-permute-start.20 = (bf16[2,344,128]{2,1,0:T(8,128)(2,1)S(1)}, bf16[2,344,128]{2,1,0:T(8,128)(2,1)S(1)}, u32[]{:S(2)}, u32[]{:S(2)}) collective-permute-start(bf16[2,344,128]{2,1,0:T(8,128)(2,1)S(1)} %adam.1.refs_0_), channel_id=1, source_target_pairs={{0,96},{16,112},{32,64},{48,80},{64,32},{80,48},{96,0},{112,16},{1... | collective-permute-start | bytes 528392 | tf_op jit(solution)/shard_map/ppermute | solution.py:28
  55.1 6.1 %collective-permute-start.18 = (bf16[2,344,128]{2,1,0:T(8,128)(2,1)S(1)}, bf16[2,344,128]{2,1,0:T(8,128)(2,1)S(1)}, u32[]{:S(2)}, u32[]{:S(2)}) collective-permute-start(bf16[2,344,128]{2,1,0:T(8,128)(2,1)S(1)} %adam.1.refs_0_), channel_id=1, source_target_pairs={{0,32},{16,48},{32,0},{48,16},{64,96},{80,112},{96,64},{112,80},{1... | collective-permute-start | bytes 528392 | tf_op jit(solution)/shard_map/ppermute | solution.py:28

commit v5 on v4

--- a/solution.py
+++ b/solution.py
@@ -14,7 +14,7 @@
 corr_two = 1.0 - beta_two**STEP
 
 NX, NY = 4, 4
-ORDER = (2, 1, 3)
+ORDER_X, ORDER_Y = (1, 2, 3), (2, 1, 3)
 STAGE_MIB = 48
 AG_X, AG_Y = (2, 1, 3), (2, 1, 3)
 PIECES = (0, 1, 3, 2)
@@ -342,7 +342,7 @@
     sums = [part(own, k) + part(got, k) for k in range(NX)]
     sums[0], grad_a = lax.optimization_barrier((sums[0], grad_t))
     total = sums[0]
-    for k in ORDER:
+    for k in ORDER_X:
         total = total + to_x(sums[k].astype(BF16), k).astype(F32)
     grads = [stage(grad_a, 0)]
     total, moments, row_basis_t, grads[0] = lax.optimization_barrier(
@@ -367,7 +367,7 @@
     owns, gots = [], []
     for g in range(n_g):
         own, *others = rank_far(far_part, near, grads[g], g)
-        for k in ORDER:
+        for k in ORDER_Y:
             own = own + to_y(others[k - 1], k).astype(F32)
         owns.append(own)
         gots.append(to_zhi(own.astype(BF16)))

time: 63.9 us -> 63.7 us (level)
  waiting for transfers between devices: 11 us -> 12 us
    ppermute x21, waiting for transfers between devices: 11 us -> 12 us  [swap(): return lax.ppermute(v, axis, [(i, i ^ bits) for i in range(size)])]
    ppermute x21, starting transfers between devices: 34.2 us -> 33.6 us  [swap(): return lax.ppermute(v, axis, [(i, i ^ bits) for i in range(size)])]
  transfers between devices with their start and end apart: 21 -> 21, of which waited for: 11 -> 13; matrix products, arithmetic and copies ran while one was open for 2% -> 2% of each run, Pallas kernels for 16% -> 16%
where the time goes in v5:
time: 63.7 us; the launch traced here: 63.5 us
  starting transfers between devices  33.6 us (53%)
  Pallas kernels  15.5 us (24%)
  waiting for transfers between devices  12 us (19%)
  local copies, waits for them, and re-layouts  1.32 us (2%)
  between operations  0.79 us (1%)
    ppermute x21, starting transfers between devices, swap(): return lax.ppermute(v, axis, [(i, i ^ bits) for i in range(size)])  33.6 us
    ppermute x21, waiting for transfers between devices, swap(): return lax.ppermute(v, axis, [(i, i ^ bits) for i in range(size)])  12 us
    pallas_call x3, Pallas kernels, update(): pl.pallas_call(lambda *refs: update_kernel(windows, n, *refs), in_specs=[...  4.69 us
    pallas_call x2, Pallas kernels, stage(): pl.pallas_call(lambda *refs: stage_kernel(g, *refs), in_specs=[HBM], out_...  4.41 us
    pallas_call x1, Pallas kernels, project(): pl.pallas_call(project_kernel, in_specs=[HBM] * 2, out_specs=[VMEM] * 2,...  2.04 us
    pallas_call x2, Pallas kernels, rank_far(): pl.pallas_call(lambda *refs: far_kernel(g, *refs), in_specs=[VMEM] * 3, o...  1.71 us
    pallas_call x1, Pallas kernels, rank_near(): pl.pallas_call(near_kernel, in_specs=[VMEM] * (1 + n_g), out_specs=VMEM,...  1.33 us
  transfers between devices with their start and end apart: 21, of which 13 were waited for; matrix products, arithmetic and copies ran while one was open for 2% of the time, Pallas kernels for 16%

profile of v5, /device:TPU:0, one launch (start us, length us, event | category | flops | bytes accessed | tf_op | source)
XLA Modules:
  0.0 63.5 jit_solution(412581884675127360)
XLA Ops:
  0.7 2.0 %project.1 = (bf16[768,256]{1,0:T(8,128)(2,1)S(1)}, f32[768,256]{1,0:T(8,128)S(1)}) custom-call(bf16[1536,512]{1,0:T(8,128)(2,1)} %inputs_ref.1, bf16[2,8192,128]{2,1,0:T(8,128)(2,1)} %basis_ref.1), custom_call_target="tpu_custom_call" | custom-call | flops 402653184 | bytes 1572864 | tf_op jit(solution)/shard_map/project/pallas_call | solution.py:96
  2.8 1.1 %constant_dynamic-slice_fusion = bf16[2,1024,128]{2,1,0:T(8,128)(2,1)S(1)} fusion(bf16[2,8192,128]{2,1,0:T(8,128)(2,1)} %basis_ref.1, s32[]{:T(128)S(6)} %select_n.3), kind=kLoop, calls=%fused_computation.10 | loop fusion | bytes 1048580 | tf_op jit(solution)/shard_map/dynamic_slice | solution.py:327
  4.6 1.6 %collective-permute-start.1 = (bf16[192,256]{1,0:T(8,128)(2,1)S(1)}, bf16[192,256]{1,0:T(8,128)(2,1)S(1)}, u32[]{:S(2)}, u32[]{:S(2)}) collective-permute-start(bf16[192,256]{1,0:T(8,128)(2,1)S(1)} %get-tuple-element.63), channel_id=1, source_target_pairs={{0,2},{1,3},{2,0},{3,1},{4,6},{5,7},{6,4},{7,5},{8,10},{9,11},{10,... | collective-permute-start | bytes 294920 | tf_op jit(solution)/shard_map/ppermute | solution.py:28
  6.2 2.1 %collective-permute-start.3 = (bf16[192,256]{1,0:T(8,128)(2,1)S(1)}, bf16[192,256]{1,0:T(8,128)(2,1)S(1)}, u32[]{:S(2)}, u32[]{:S(2)}) collective-permute-start(bf16[192,256]{1,0:T(8,128)(2,1)S(1)} %get-tuple-element.64), channel_id=1, source_target_pairs={{0,6},{1,7},{2,4},{3,5},{4,2},{5,3},{6,0},{7,1},{8,14},{9,15},{10,... | collective-permute-start | bytes 294920 | tf_op jit(solution)/shard_map/ppermute | solution.py:28
  9.0 2.2 %stage.2.refs_0_.refs_2_ = bf16[1376,1536]{1,0:T(8,128)(2,1)S(1)} custom-call(bf16[2,1376,1536]{2,1,0:T(8,128)(2,1)} %bitcast.19), custom_call_target="tpu_custom_call" | custom-call | bytes 8454144 | tf_op jit(solution)/shard_map/stage/pallas_call | solution.py:123
  11.2 1.4 %collective-permute-done.3 = bf16[192,256]{1,0:T(8,128)(2,1)S(1)} collective-permute-done((bf16[192,256]{1,0:T(8,128)(2,1)S(1)}, bf16[192,256]{1,0:T(8,128)(2,1)S(1)}, u32[]{:S(2)}, u32[]{:S(2)}) %collective-permute-start.3) | collective-permute-done | bytes 98336 | tf_op jit(solution)/shard_map/ppermute | solution.py:28
  12.6 1.8 %collective-permute-done.2 = bf16[192,256]{1,0:T(8,128)(2,1)S(1)} collective-permute-done((bf16[192,256]{1,0:T(8,128)(2,1)S(1)}, bf16[192,256]{1,0:T(8,128)(2,1)S(1)}, u32[]{:S(2)}, u32[]{:S(2)}) %collective-permute-start.2) | collective-permute-done | bytes 98336 | tf_op jit(solution)/shard_map/ppermute | solution.py:28
  14.5 2.0 %collective-permute-start.4 = (bf16[192,256]{1,0:T(8,128)(2,1)S(1)}, bf16[192,256]{1,0:T(8,128)(2,1)S(1)}, u32[]{:S(2)}, u32[]{:S(2)}) collective-permute-start(bf16[192,256]{1,0:T(8,128)(2,1)S(1)} %convert_element_type.73), channel_id=1, source_target_pairs={{0,8},{1,9},{2,10},{3,11},{4,12},{5,13},{6,14},{7,15},{8,0},{9,1},... | collective-permute-start | bytes 294920 | tf_op jit(solution)/shard_map/ppermute | solution.py:28
  16.5 3.6 %collective-permute-start.8 = (f32[688,128]{1,0:T(8,128)S(1)}, f32[688,128]{1,0:T(8,128)S(1)}, u32[]{:S(2)}, u32[]{:S(2)}) collective-permute-start(f32[688,128]{1,0:T(8,128)S(1)} %pad_maximum_fusion.1.refs_4_), channel_id=1, source_target_pairs={{0,16},{16,0},{32,48},{48,32},{64,80},{80,64},{96,112},{112,96},{1... | collective-permute-start | bytes 1056776 | tf_op jit(solution)/shard_map/ppermute | solution.py:28
  20.1 1.3 %collective-permute-start.7 = (bf16[192,256]{1,0:T(8,128)(2,1)S(1)}, bf16[192,256]{1,0:T(8,128)(2,1)S(1)}, u32[]{:S(2)}, u32[]{:S(2)}) collective-permute-start(bf16[192,256]{1,0:T(8,128)(2,1)S(1)} %add_convert_fusion), channel_id=1, source_target_pairs={{0,4},{1,5},{2,6},{3,7},{4,0},{5,1},{6,2},{7,3},{8,12},{9,13},{10,... | collective-permute-start | bytes 294920 | tf_op jit(solution)/shard_map/ppermute | solution.py:28
  21.5 2.0 %collective-permute-start.6 = (bf16[192,256]{1,0:T(8,128)(2,1)S(1)}, bf16[192,256]{1,0:T(8,128)(2,1)S(1)}, u32[]{:S(2)}, u32[]{:S(2)}) collective-permute-start(bf16[192,256]{1,0:T(8,128)(2,1)S(1)} %add_convert_fusion), channel_id=1, source_target_pairs={{0,6},{1,7},{2,4},{3,5},{4,2},{5,3},{6,0},{7,1},{8,14},{9,15},{10,... | collective-permute-start | bytes 294920 | tf_op jit(solution)/shard_map/ppermute | solution.py:28
  23.7 2.2 %stage.3.refs_1_.refs_2_ = bf16[1376,1536]{1,0:T(8,128)(2,1)S(1)} custom-call(bf16[2,1376,1536]{2,1,0:T(8,128)(2,1)} %bitcast.20), custom_call_target="tpu_custom_call" | custom-call | bytes 8454144 | tf_op jit(solution)/shard_map/stage/pallas_call | solution.py:123
  26.3 1.0 %collective-permute-done.6 = bf16[192,256]{1,0:T(8,128)(2,1)S(1)} collective-permute-done((bf16[192,256]{1,0:T(8,128)(2,1)S(1)}, bf16[192,256]{1,0:T(8,128)(2,1)S(1)}, u32[]{:S(2)}, u32[]{:S(2)}) %collective-permute-start.6) | collective-permute-done | bytes 98336 | tf_op jit(solution)/shard_map/ppermute | solution.py:28
  28.8 1.3 %rank_near.1.refs_1_ = f32[2,1376,128]{2,1,0:T(8,128)S(1)} custom-call(bf16[768,256]{1,0:T(8,128)(2,1)S(1)} %pad_maximum_fusion.part_ref, bf16[1376,1536]{1,0:T(8,128)(2,1)S(1)} %stage.2.refs_0_.refs_2_, bf16[1376,1536]{1,0:T(8,128)(2,1)S(1)} %stage.3.refs_1_.refs_2_), custom_call_target="tpu_custom_call" | custom-call | flops 541065216 | bytes 4194304 | tf_op jit(solution)/shard_map/rank_near/pallas_call | solution.py:158
  30.5 0.9 %rank_far.3 = (f32[344,128]{1,0:T(8,128)S(1)}, bf16[344,128]{1,0:T(8,128)(2,1)S(1)}, bf16[344,128]{1,0:T(8,128)(2,1)S(1)}, bf16[344,128]{1,0:T(8,128)(2,1)S(1)}) custom-call(bf16[768,256]{1,0:T(8,128)(2,1)S(1)} %collective-permute-done.9.refs_0_, f32[2,1376,128]{2,1,0:T(8,128)S(1)} %rank_near.1.refs_1_, bf16[1376,1536]{1,0:T(8,128)(2,1)S(1)} %stage.3.refs_1_.refs_2_), custom_call_target="tpu_custom_call" | custom-call | flops 270532608 | bytes 2097152 | tf_op jit(solution)/shard_map/rank_far/pallas_call | solution.py:187
  31.4 3.3 %collective-permute-start.13 = (bf16[344,128]{1,0:T(8,128)(2,1)S(1)}, bf16[344,128]{1,0:T(8,128)(2,1)S(1)}, u32[]{:S(2)}, u32[]{:S(2)}) collective-permute-start(bf16[344,128]{1,0:T(8,128)(2,1)S(1)} %get-tuple-element.52), channel_id=1, source_target_pairs={{0,64},{16,80},{32,96},{48,112},{64,0},{80,16},{96,32},{112,48},{1... | collective-permute-start | bytes 264200 | tf_op jit(solution)/shard_map/ppermute | solution.py:28
  35.7 0.9 %rank_far.2 = (f32[344,128]{1,0:T(8,128)S(1)}, bf16[344,128]{1,0:T(8,128)(2,1)S(1)}, bf16[344,128]{1,0:T(8,128)(2,1)S(1)}, bf16[344,128]{1,0:T(8,128)(2,1)S(1)}) custom-call(bf16[768,256]{1,0:T(8,128)(2,1)S(1)} %collective-permute-done.9.refs_0_, f32[2,1376,128]{2,1,0:T(8,128)S(1)} %rank_near.1.refs_1_, bf16[1376,1536]{1,0:T(8,128)(2,1)S(1)} %stage.2.refs_0_.refs_2_), custom_call_target="tpu_custom_call" | custom-call | flops 270532608 | bytes 2097152 | tf_op jit(solution)/shard_map/rank_far/pallas_call | solution.py:187
  36.6 3.1 %collective-permute-start.10 = (bf16[344,128]{1,0:T(8,128)(2,1)S(1)}, bf16[344,128]{1,0:T(8,128)(2,1)S(1)}, u32[]{:S(2)}, u32[]{:S(2)}) collective-permute-start(bf16[344,128]{1,0:T(8,128)(2,1)S(1)} %get-tuple-element.48), channel_id=1, source_target_pairs={{0,64},{16,80},{32,96},{48,112},{64,0},{80,16},{96,32},{112,48},{1... | collective-permute-start | bytes 264200 | tf_op jit(solution)/shard_map/ppermute | solution.py:28
  39.7 0.7 %collective-permute-start.11 = (bf16[344,128]{1,0:T(8,128)(2,1)S(1)}, bf16[344,128]{1,0:T(8,128)(2,1)S(1)}, u32[]{:S(2)}, u32[]{:S(2)}) collective-permute-start(bf16[344,128]{1,0:T(8,128)(2,1)S(1)} %get-tuple-element.49), channel_id=1, source_target_pairs={{0,32},{16,48},{32,0},{48,16},{64,96},{80,112},{96,64},{112,80},{1... | collective-permute-start | bytes 264200 | tf_op jit(solution)/shard_map/ppermute | solution.py:28
  40.4 1.0 %collective-permute-start.12 = (bf16[344,128]{1,0:T(8,128)(2,1)S(1)}, bf16[344,128]{1,0:T(8,128)(2,1)S(1)}, u32[]{:S(2)}, u32[]{:S(2)}) collective-permute-start(bf16[344,128]{1,0:T(8,128)(2,1)S(1)} %get-tuple-element.50), channel_id=1, source_target_pairs={{0,96},{16,112},{32,64},{48,80},{64,32},{80,48},{96,0},{112,16},{1... | collective-permute-start | bytes 264200 | tf_op jit(solution)/shard_map/ppermute | solution.py:28
  41.4 0.9 %collective-permute-done.15 = bf16[344,128]{1,0:T(8,128)(2,1)S(1)} collective-permute-done((bf16[344,128]{1,0:T(8,128)(2,1)S(1)}, bf16[344,128]{1,0:T(8,128)(2,1)S(1)}, u32[]{:S(2)}, u32[]{:S(2)}) %collective-permute-start.15) | collective-permute-done | bytes 88096 | tf_op jit(solution)/shard_map/ppermute | solution.py:28
  42.4 3.6 %collective-permute-start.17 = (bf16[344,128]{1,0:T(8,128)(2,1)S(1)}, bf16[344,128]{1,0:T(8,128)(2,1)S(1)}, u32[]{:S(2)}, u32[]{:S(2)}) collective-permute-start(bf16[344,128]{1,0:T(8,128)(2,1)S(1)} %get-tuple-element.59), channel_id=1, source_target_pairs={{0,16},{16,0},{32,48},{48,32},{64,80},{80,64},{96,112},{112,96},{1... | collective-permute-start | bytes 264200 | tf_op jit(solution)/shard_map/ppermute | solution.py:28
  46.2 3.6 %collective-permute-start.16 = (bf16[344,128]{1,0:T(8,128)(2,1)S(1)}, bf16[344,128]{1,0:T(8,128)(2,1)S(1)}, u32[]{:S(2)}, u32[]{:S(2)}) collective-permute-start(bf16[344,128]{1,0:T(8,128)(2,1)S(1)} %get-tuple-element.61), channel_id=1, source_target_pairs={{0,16},{16,0},{32,48},{48,32},{64,80},{80,64},{96,112},{112,96},{1... | collective-permute-start | bytes 264200 | tf_op jit(solution)/shard_map/ppermute | solution.py:28
  49.8 2.5 %collective-permute-done.16.refs_2_ = bf16[344,128]{1,0:T(8,128)(2,1)S(1)} collective-permute-done((bf16[344,128]{1,0:T(8,128)(2,1)S(1)}, bf16[344,128]{1,0:T(8,128)(2,1)S(1)}, u32[]{:S(2)}, u32[]{:S(2)}) %collective-permute-start.16) | collective-permute-done | bytes 88096 | tf_op jit(solution)/shard_map/ppermute | solution.py:28
  52.6 1.4 %collective-permute-start.19 = (bf16[2,344,128]{2,1,0:T(8,128)(2,1)S(1)}, bf16[2,344,128]{2,1,0:T(8,128)(2,1)S(1)}, u32[]{:S(2)}, u32[]{:S(2)}) collective-permute-start(bf16[2,344,128]{2,1,0:T(8,128)(2,1)S(1)} %adam.1.refs_0_), channel_id=1, source_target_pairs={{0,64},{16,80},{32,96},{48,112},{64,0},{80,16},{96,32},{112,48},{1... | collective-permute-start | bytes 528392 | tf_op jit(solution)/shard_map/ppermute | solution.py:28
  54.0 1.4 %collective-permute-start.20 = (bf16[2,344,128]{2,1,0:T(8,128)(2,1)S(1)}, bf16[2,344,128]{2,1,0:T(8,128)(2,1)S(1)}, u32[]{:S(2)}, u32[]{:S(2)}) collective-permute-start(bf16[2,344,128]{2,1,0:T(8,128)(2,1)S(1)} %adam.1.refs_0_), channel_id=1, source_target_pairs={{0,96},{16,112},{32,64},{48,80},{64,32},{80,48},{96,0},{112,16},{1... | collective-permute-start | bytes 528392 | tf_op jit(solution)/shard_map/ppermute | solution.py:28
  55.5 0.7 %collective-permute-start.18 = (bf16[2,344,128]{2,1,0:T(8,128)(2,1)S(1)}, bf16[2,344,128]{2,1,0:T(8,128)(2,1)S(1)}, u32[]{:S(2)}, u32[]{:S(2)}) collective-permute-start(bf16[2,344,128]{2,1,0:T(8,128)(2,1)S(1)} %adam.1.refs_0_), channel_id=1, source_target_pairs={{0,32},{16,48},{32,0},{48,16},{64,96},{80,112},{96,64},{112,80},{1... | collective-permute-start | bytes 528392 | tf_op jit(solution)/shard_map/ppermute | solution.py:28
  56.2 0.9 %new_moments.1 = (f32[344,1,128]{2,1,0:T(1,128)}, f32[344,1,128]{2,1,0:T(1,128)}) custom-call(f32[344,128]{1,0:T(8,128)S(1)} %get-tuple-element.62.refs_0_, f32[344,128]{1,0:T(8,128)S(1)} %get-tuple-element.60.refs_1_, bf16[344,128]{1,0:T(8,128)(2,1)S(1)} %collective-permute-done.16.refs_2_, bf16[344,128]{1,0:T(8,128)(2,1)S(1)} %collective-permute-done.17.refs_3_, ...), custom_call_target="tpu_custom_call" | custom-call | tf_op jit(solution)/shard_map/new_moments/pallas_call | solution.py:253
  57.1 1.4 %update.3.refs_2_ = bf16[2,1376,1024]{2,1,0:T(8,128)(2,1)} custom-call(bf16[2,344,128]{2,1,0:T(8,128)(2,1)S(1)} %adam.1.refs_0_, bf16[2,128,1024]{2,1,0:T(8,128)(2,1)S(1)} %bitcast.15), custom_call_target="tpu_custom_call" | custom-call | flops 184549376 | bytes 1441792 | tf_op jit(solution)/shard_map/update/pallas_call | solution.py:305
  58.5 1.2 %collective-permute-done.19.refs_0_.refs_2_ = bf16[2,344,128]{2,1,0:T(8,128)(2,1)S(1)} collective-permute-done((bf16[2,344,128]{2,1,0:T(8,128)(2,1)S(1)}, bf16[2,344,128]{2,1,0:T(8,128)(2,1)S(1)}, u32[]{:S(2)}, u32[]{:S(2)}) %collective-permute-start.19) | collective-permute-done | bytes 176160 | tf_op jit(solution)/shard_map/ppermute | solution.py:28
  59.7 1.4 %update.4.refs_5_ = bf16[2,1376,1024]{2,1,0:T(8,128)(2,1)} custom-call(bf16[2,344,128]{2,1,0:T(8,128)(2,1)S(1)} %collective-permute-done.19.refs_0_.refs_2_, bf16[2,128,1024]{2,1,0:T(8,128)(2,1)S(1)} %bitcast.16, bf16[2,1376,1024]{2,1,0:T(8,128)(2,1)} %update.3.refs_2_), custom_call_target="tpu_custom_call", output_to_operand_aliasing={{}: (2, {})} | custom-call | flops 184549376 | bytes 1441792 | tf_op jit(solution)/shard_map/update/pallas_call | solution.py:305
  61.5 1.9 %update.5 = bf16[2,1376,1024]{2,1,0:T(8,128)(2,1)} custom-call(bf16[2,344,128]{2,1,0:T(8,128)(2,1)S(1)} %adam.1.refs_0_, bf16[2,344,128]{2,1,0:T(8,128)(2,1)S(1)} %collective-permute-done.18.refs_1_, bf16[2,344,128]{2,1,0:T(8,128)(2,1)S(1)} %collective-permute-done.19.refs_0_.refs_2_, ...), custom_call_target="tpu_custom_call", output_to_operand_aliasing={{}: (5, {})} | custom-call | flops 369098752 | bytes 2883584 | tf_op jit(solution)/shard_map/update/pallas_call | solution.py:305
  (35 shorter events, 6.0 us)
Async XLA Ops:
  0.6 8.3 %copy-start = (f32[2,128,1,172]{1,2,3,0:T(1,128)S(1)}, f32[2,128,1,172]{1,2,3,0:T(1,128)}, u32[]{:S(2)}) copy-start(f32[2,128,1,172]{1,2,3,0:T(1,128)} %param.9) | copy-start | bytes 528388
  0.6 8.3 %copy-start.1 = (f32[2,128,1,172]{1,2,3,0:T(1,128)S(1)}, f32[2,128,1,172]{1,2,3,0:T(1,128)}, u32[]{:S(2)}) copy-start(f32[2,128,1,172]{1,2,3,0:T(1,128)} %param.8) | copy-start | bytes 528388
  2.7 1.8 %collective-permute-start = (bf16[768,256]{1,0:T(8,128)(2,1)S(1)}, bf16[768,256]{1,0:T(8,128)(2,1)S(1)}, u32[]{:S(2)}, u32[]{:S(2)}) collective-permute-start(bf16[768,256]{1,0:T(8,128)(2,1)S(1)} %get-tuple-element.33), channel_id=1, source_target_pairs={{0,1},{1,0},{2,3},{3,2},{4,5},{5,4},{6,7},{7,6},{8,9},{9,8},{10,11... | collective-permute-start | bytes 1179656 | tf_op jit(solution)/shard_map/ppermute | solution.py:28
  4.6 6.6 %collective-permute-start.1 = (bf16[192,256]{1,0:T(8,128)(2,1)S(1)}, bf16[192,256]{1,0:T(8,128)(2,1)S(1)}, u32[]{:S(2)}, u32[]{:S(2)}) collective-permute-start(bf16[192,256]{1,0:T(8,128)(2,1)S(1)} %get-tuple-element.63), channel_id=1, source_target_pairs={{0,2},{1,3},{2,0},{3,1},{4,6},{5,7},{6,4},{7,5},{8,10},{9,11},{10,... | collective-permute-start | bytes 294920 | tf_op jit(solution)/shard_map/ppermute | solution.py:28
  6.2 6.4 %collective-permute-start.3 = (bf16[192,256]{1,0:T(8,128)(2,1)S(1)}, bf16[192,256]{1,0:T(8,128)(2,1)S(1)}, u32[]{:S(2)}, u32[]{:S(2)}) collective-permute-start(bf16[192,256]{1,0:T(8,128)(2,1)S(1)} %get-tuple-element.64), channel_id=1, source_target_pairs={{0,6},{1,7},{2,4},{3,5},{4,2},{5,3},{6,0},{7,1},{8,14},{9,15},{10,... | collective-permute-start | bytes 294920 | tf_op jit(solution)/shard_map/ppermute | solution.py:28
  8.3 6.1 %collective-permute-start.2 = (bf16[192,256]{1,0:T(8,128)(2,1)S(1)}, bf16[192,256]{1,0:T(8,128)(2,1)S(1)}, u32[]{:S(2)}, u32[]{:S(2)}) collective-permute-start(bf16[192,256]{1,0:T(8,128)(2,1)S(1)} %get-tuple-element.65), channel_id=1, source_target_pairs={{0,4},{1,5},{2,6},{3,7},{4,0},{5,1},{6,2},{7,3},{8,12},{9,13},{10,... | collective-permute-start | bytes 294920 | tf_op jit(solution)/shard_map/ppermute | solution.py:28
  14.5 5.6 %collective-permute-start.4 = (bf16[192,256]{1,0:T(8,128)(2,1)S(1)}, bf16[192,256]{1,0:T(8,128)(2,1)S(1)}, u32[]{:S(2)}, u32[]{:S(2)}) collective-permute-start(bf16[192,256]{1,0:T(8,128)(2,1)S(1)} %convert_element_type.73), channel_id=1, source_target_pairs={{0,8},{1,9},{2,10},{3,11},{4,12},{5,13},{6,14},{7,15},{8,0},{9,1},... | collective-permute-start | bytes 294920 | tf_op jit(solution)/shard_map/ppermute | solution.py:28
  16.5 12.3 %collective-permute-start.8 = (f32[688,128]{1,0:T(8,128)S(1)}, f32[688,128]{1,0:T(8,128)S(1)}, u32[]{:S(2)}, u32[]{:S(2)}) collective-permute-start(f32[688,128]{1,0:T(8,128)S(1)} %pad_maximum_fusion.1.refs_4_), channel_id=1, source_target_pairs={{0,16},{16,0},{32,48},{48,32},{64,80},{80,64},{96,112},{112,96},{1... | collective-permute-start | bytes 1056776 | tf_op jit(solution)/shard_map/ppermute | solution.py:28
  20.1 6.2 %collective-permute-start.7 = (bf16[192,256]{1,0:T(8,128)(2,1)S(1)}, bf16[192,256]{1,0:T(8,128)(2,1)S(1)}, u32[]{:S(2)}, u32[]{:S(2)}) collective-permute-start(bf16[192,256]{1,0:T(8,128)(2,1)S(1)} %add_convert_fusion), channel_id=1, source_target_pairs={{0,4},{1,5},{2,6},{3,7},{4,0},{5,1},{6,2},{7,3},{8,12},{9,13},{10,... | collective-permute-start | bytes 294920 | tf_op jit(solution)/shard_map/ppermute | solution.py:28
  21.5 5.9 %collective-permute-start.6 = (bf16[192,256]{1,0:T(8,128)(2,1)S(1)}, bf16[192,256]{1,0:T(8,128)(2,1)S(1)}, u32[]{:S(2)}, u32[]{:S(2)}) collective-permute-start(bf16[192,256]{1,0:T(8,128)(2,1)S(1)} %add_convert_fusion), channel_id=1, source_target_pairs={{0,6},{1,7},{2,4},{3,5},{4,2},{5,3},{6,0},{7,1},{8,14},{9,15},{10,... | collective-permute-start | bytes 294920 | tf_op jit(solution)/shard_map/ppermute | solution.py:28
  23.5 4.6 %collective-permute-start.5 = (bf16[192,256]{1,0:T(8,128)(2,1)S(1)}, bf16[192,256]{1,0:T(8,128)(2,1)S(1)}, u32[]{:S(2)}, u32[]{:S(2)}) collective-permute-start(bf16[192,256]{1,0:T(8,128)(2,1)S(1)} %add_convert_fusion), channel_id=1, source_target_pairs={{0,2},{1,3},{2,0},{3,1},{4,6},{5,7},{6,4},{7,5},{8,10},{9,11},{10,... | collective-permute-start | bytes 294920 | tf_op jit(solution)/shard_map/ppermute | solution.py:28
  28.8 1.7 %collective-permute-start.9 = (bf16[768,256]{1,0:T(8,128)(2,1)S(1)}, bf16[768,256]{1,0:T(8,128)(2,1)S(1)}, u32[]{:S(2)}, u32[]{:S(2)}) collective-permute-start(bf16[768,256]{1,0:T(8,128)(2,1)S(1)} %pad_maximum_fusion.part_ref), channel_id=1, source_target_pairs={{0,1},{1,0},{2,3},{3,2},{4,5},{5,4},{6,7},{7,6},{8,9},{9,8},{10,11... | collective-permute-start | bytes 1179656 | tf_op jit(solution)/shard_map/ppermute | solution.py:28
  31.4 9.0 %collective-permute-start.13 = (bf16[344,128]{1,0:T(8,128)(2,1)S(1)}, bf16[344,128]{1,0:T(8,128)(2,1)S(1)}, u32[]{:S(2)}, u32[]{:S(2)}) collective-permute-start(bf16[344,128]{1,0:T(8,128)(2,1)S(1)} %get-tuple-element.52), channel_id=1, source_target_pairs={{0,64},{16,80},{32,96},{48,112},{64,0},{80,16},{96,32},{112,48},{1... | collective-permute-start | bytes 264200 | tf_op jit(solution)/shard_map/ppermute | solution.py:28
  34.7 6.8 %collective-permute-start.14 = (bf16[344,128]{1,0:T(8,128)(2,1)S(1)}, bf16[344,128]{1,0:T(8,128)(2,1)S(1)}, u32[]{:S(2)}, u32[]{:S(2)}) collective-permute-start(bf16[344,128]{1,0:T(8,128)(2,1)S(1)} %get-tuple-element.53), channel_id=1, source_target_pairs={{0,32},{16,48},{32,0},{48,16},{64,96},{80,112},{96,64},{112,80},{1... | collective-permute-start | bytes 264200 | tf_op jit(solution)/shard_map/ppermute | solution.py:28
  35.4 7.0 %collective-permute-start.15 = (bf16[344,128]{1,0:T(8,128)(2,1)S(1)}, bf16[344,128]{1,0:T(8,128)(2,1)S(1)}, u32[]{:S(2)}, u32[]{:S(2)}) collective-permute-start(bf16[344,128]{1,0:T(8,128)(2,1)S(1)} %get-tuple-element.54), channel_id=1, source_target_pairs={{0,96},{16,112},{32,64},{48,80},{64,32},{80,48},{96,0},{112,16},{1... | collective-permute-start | bytes 264200 | tf_op jit(solution)/shard_map/ppermute | solution.py:28
  36.6 9.4 %collective-permute-start.10 = (bf16[344,128]{1,0:T(8,128)(2,1)S(1)}, bf16[344,128]{1,0:T(8,128)(2,1)S(1)}, u32[]{:S(2)}, u32[]{:S(2)}) collective-permute-start(bf16[344,128]{1,0:T(8,128)(2,1)S(1)} %get-tuple-element.48), channel_id=1, source_target_pairs={{0,64},{16,80},{32,96},{48,112},{64,0},{80,16},{96,32},{112,48},{1... | collective-permute-start | bytes 264200 | tf_op jit(solution)/shard_map/ppermute | solution.py:28
  39.7 6.3 %collective-permute-start.11 = (bf16[344,128]{1,0:T(8,128)(2,1)S(1)}, bf16[344,128]{1,0:T(8,128)(2,1)S(1)}, u32[]{:S(2)}, u32[]{:S(2)}) collective-permute-start(bf16[344,128]{1,0:T(8,128)(2,1)S(1)} %get-tuple-element.49), channel_id=1, source_target_pairs={{0,32},{16,48},{32,0},{48,16},{64,96},{80,112},{96,64},{112,80},{1... | collective-permute-start | bytes 264200 | tf_op jit(solution)/shard_map/ppermute | solution.py:28
  40.4 5.7 %collective-permute-start.12 = (bf16[344,128]{1,0:T(8,128)(2,1)S(1)}, bf16[344,128]{1,0:T(8,128)(2,1)S(1)}, u32[]{:S(2)}, u32[]{:S(2)}) collective-permute-start(bf16[344,128]{1,0:T(8,128)(2,1)S(1)} %get-tuple-element.50), channel_id=1, source_target_pairs={{0,96},{16,112},{32,64},{48,80},{64,32},{80,48},{96,0},{112,16},{1... | collective-permute-start | bytes 264200 | tf_op jit(solution)/shard_map/ppermute | solution.py:28
  42.4 7.4 %collective-permute-start.17 = (bf16[344,128]{1,0:T(8,128)(2,1)S(1)}, bf16[344,128]{1,0:T(8,128)(2,1)S(1)}, u32[]{:S(2)}, u32[]{:S(2)}) collective-permute-start(bf16[344,128]{1,0:T(8,128)(2,1)S(1)} %get-tuple-element.59), channel_id=1, source_target_pairs={{0,16},{16,0},{32,48},{48,32},{64,80},{80,64},{96,112},{112,96},{1... | collective-permute-start | bytes 264200 | tf_op jit(solution)/shard_map/ppermute | solution.py:28
  46.2 6.1 %collective-permute-start.16 = (bf16[344,128]{1,0:T(8,128)(2,1)S(1)}, bf16[344,128]{1,0:T(8,128)(2,1)S(1)}, u32[]{:S(2)}, u32[]{:S(2)}) collective-permute-start(bf16[344,128]{1,0:T(8,128)(2,1)S(1)} %get-tuple-element.61), channel_id=1, source_target_pairs={{0,16},{16,0},{32,48},{48,32},{64,80},{80,64},{96,112},{112,96},{1... | collective-permute-start | bytes 264200 | tf_op jit(solution)/shard_map/ppermute | solution.py:28
  52.6 7.1 %collective-permute-start.19 = (bf16[2,344,128]{2,1,0:T(8,128)(2,1)S(1)}, bf16[2,344,128]{2,1,0:T(8,128)(2,1)S(1)}, u32[]{:S(2)}, u32[]{:S(2)}) collective-permute-start(bf16[2,344,128]{2,1,0:T(8,128)(2,1)S(1)} %adam.1.refs_0_), channel_id=1, source_target_pairs={{0,64},{16,80},{32,96},{48,112},{64,0},{80,16},{96,32},{112,48},{1... | collective-permute-start | bytes 528392 | tf_op jit(solution)/shard_map/ppermute | solution.py:28
  54.0 7.5 %collective-permute-start.20 = (bf16[2,344,128]{2,1,0:T(8,128)(2,1)S(1)}, bf16[2,344,128]{2,1,0:T(8,128)(2,1)S(1)}, u32[]{:S(2)}, u32[]{:S(2)}) collective-permute-start(bf16[2,344,128]{2,1,0:T(8,128)(2,1)S(1)} %adam.1.refs_0_), channel_id=1, source_target_pairs={{0,96},{16,112},{32,64},{48,80},{64,32},{80,48},{96,0},{112,16},{1... | collective-permute-start | bytes 528392 | tf_op jit(solution)/shard_map/ppermute | solution.py:28
  55.5 6.1 %collective-permute-start.18 = (bf16[2,344,128]{2,1,0:T(8,128)(2,1)S(1)}, bf16[2,344,128]{2,1,0:T(8,128)(2,1)S(1)}, u32[]{:S(2)}, u32[]{:S(2)}) collective-permute-start(bf16[2,344,128]{2,1,0:T(8,128)(2,1)S(1)} %adam.1.refs_0_), channel_id=1, source_target_pairs={{0,32},{16,48},{32,0},{48,16},{64,96},{80,112},{96,64},{112,80},{1... | collective-permute-start | bytes 528392 | tf_op jit(solution)/shard_map/ppermute | solution.py:28
